TPU v7x, 32 devices: a whole 2x2x4 slice. The times are simulated.
32 devices in a mesh: groups: 2 (over y), row: 4 (over z), col: 4 (over x, core).
Axes of the slice: x: 2, y: 2, z: 4, core: 2. Of those that a mesh axis runs over, the one named last changes fastest.
Arguments:
- pair_map: bfloat16 [320, 160, 128], P(('groups', 'row'), 'col'), parts along dimension 0, may hold values from -6 to 6
- token_mask: int32 [320], P('groups'), parts along dimension 0, may hold values 0 or 1
- in_gain: float32 [2, 128], replicated, may hold values from 0.5 to 1.5
- proj_weights: bfloat16 [2, 4, 128, 128], replicated, may hold values from -0.5 to 0.5
- gate_weight: bfloat16 [2, 128, 128], replicated, may hold values from -0.5 to 0.5
- out_gain: float32 [2, 128], replicated, may hold values from 0.5 to 1.5
- out_weight: bfloat16 [2, 128, 128], replicated, may hold values from -0.5 to 0.5
Outputs:
- updated_pair: bfloat16 [320, 160, 128], P(('groups', 'row'), 'col'), parts along dimension 0
There are 2 independent parts, one for each index of `groups`. A program takes and returns all parts, laid end to end along the dimension named above; an argument that names none is the same for every part. Nothing has to cross between parts.
All inputs are finite; a program needn't handle non-finite values.
Results may differ from a plain program's by a relative error of at most 0.015.
Values may be sent and summed in bfloat16 or wider, within the bound.
No kernel may reach another device: no remote copies, remote signals or barrier semaphores. Data moves between devices by JAX's collectives and lax.ppermute only.
A program may use at most 128 MiB of HBM per device.

v0:
```python
import jax
import jax.numpy as jnp
from jax import lax
from jax.sharding import PartitionSpec as P

EPSILON = 1e-05


def layer_norm(values, gain_vec):
    mean_val = jnp.mean(values, axis=-1, keepdims=True)
    centered = values - mean_val
    variance = jnp.mean(centered * centered, axis=-1, keepdims=True)
    return centered * jax.lax.rsqrt(variance + EPSILON) * gain_vec


def project_side(pair_tile, pair_valid, layer_index, in_gain, proj_weights, gate_weight):
    normed = layer_norm(pair_tile.astype(jnp.float32), in_gain[layer_index]).astype(jnp.bfloat16)
    outputs = [
        jnp.dot(normed, proj_weights[layer_index, slot], preferred_element_type=jnp.float32)
        for slot in range(4)
    ]
    weight_mask = pair_valid[..., None]
    left_side = (jax.nn.sigmoid(outputs[1]) * outputs[0] * weight_mask).astype(jnp.bfloat16)
    right_side = (jax.nn.sigmoid(outputs[3]) * outputs[2] * weight_mask).astype(jnp.bfloat16)
    gating = jax.nn.sigmoid(
        jnp.dot(normed, gate_weight[layer_index], preferred_element_type=jnp.float32)
    )
    return (left_side, right_side, gating)


def finish(pair_tile, mixed_sum, gating, layer_index, out_gain, out_weight):
    normed = layer_norm(mixed_sum, out_gain[layer_index]).astype(jnp.bfloat16)
    update = jnp.dot(normed, out_weight[layer_index], preferred_element_type=jnp.float32)
    return (pair_tile.astype(jnp.float32) + gating * update).astype(jnp.bfloat16)


def body(pair_map, token_mask, in_gain, proj_weights, gate_weight, out_gain, out_weight):
    tile_rows = pair_map.shape[0]
    tile_cols = pair_map.shape[1]
    row_begin = lax.axis_index("row") * tile_rows
    col_begin = lax.axis_index("col") * tile_cols
    valid = token_mask.astype(jnp.float32)
    row_valid = lax.dynamic_slice_in_dim(valid, row_begin, tile_rows, 0)
    col_valid = lax.dynamic_slice_in_dim(valid, col_begin, tile_cols, 0)
    pair_valid = row_valid[:, None] * col_valid[None, :]
    left_side, right_side, gating = project_side(
        pair_map, pair_valid, 0, in_gain, proj_weights, gate_weight
    )
    right_panel = lax.all_gather(right_side, "row", axis=0, tiled=True)
    block = right_panel
    summed = lax.psum_scatter(
        jnp.einsum("jkc,ikc->jic", block, left_side, preferred_element_type=jnp.float32).astype(
            jnp.bfloat16
        ),
        "col",
        scatter_dimension=0,
        tiled=True,
    ).astype(jnp.float32)
    mixed = jnp.transpose(summed, (1, 0, 2))
    after_out = finish(pair_map, mixed, gating, 0, out_gain, out_weight)
    left_side, right_side, gating = project_side(
        after_out, pair_valid, 1, in_gain, proj_weights, gate_weight
    )
    left_panel = lax.all_gather(left_side, "col", axis=1, tiled=True)
    block = left_panel
    mixed = lax.psum_scatter(
        jnp.einsum("kic,kjc->ijc", block, right_side, preferred_element_type=jnp.float32).astype(
            jnp.bfloat16
        ),
        "row",
        scatter_dimension=0,
        tiled=True,
    ).astype(jnp.float32)
    return finish(after_out, mixed, gating, 1, out_gain, out_weight)


def solution(mesh):
    in_specs = (P(("groups", "row"), "col", None), P("groups"), P(), P(), P(), P(), P())
    out_specs = P(("groups", "row"), "col", None)
    return jax.shard_map(body, mesh=mesh, in_specs=in_specs, out_specs=out_specs, check_vma=False)
```

profile of v0, /device:TPU:0, one launch (start us, length us, event | category | flops | bytes accessed | tf_op | source)
XLA Modules:
  0.0 190.3 jit_solution(11176549990703254154)
XLA Ops:
  6.5 0.7 convert_element_type.59
  7.2 1.4 convert_reduce_fusion
  8.6 1.5 fusion.35
  10.1 0.8 slice_bitcast_fusion.1
  11.0 1.7 fusion.16
  12.7 1.6 fusion.25
  14.4 0.7 fusion.20
  15.0 0.9 fusion.24
  15.9 2.0 %copy.44 = bf16[40,40,128]{1,0,2:T(8,128)(2,1)} copy(bf16[40,40,128]{2,1,0:T(8,128)(2,1)S(1)} %fusion.24) | data formatting | bytes 819200 | tf_op jit(solution)/shard_map/convert_element_type | solution.py:23
  18.0 37.4 %all-gather.3.cloned.1.call-done = bf16[160,40,128]{2,1,0:T(8,128)(2,1)} async-done(((bf16[40,40,128]{2,1,0:T(8,128)(2,1)}), bf16[160,40,128]{2,1,0:T(8,128)(2,1)}) %all-gather.3.cloned.1.call-update) | async-done | bytes 1638416 | tf_op jit(solution)/shard_map/all_gather | solution.py:49
  55.3 8.7 %copy.45 = bf16[160,40,128]{1,0,2:T(8,128)(2,1)} copy(bf16[160,40,128]{2,1,0:T(8,128)(2,1)} %all-gather.3.cloned.1.call-done) | data formatting | bytes 3276800 | tf_op jit(solution)/shard_map/all_gather | solution.py:49
  64.0 6.1 %convert_bitcast_fusion.1 = bf16[160,40,128]{0,1,2:T(8,128)(2,1)S(1)} fusion(bf16[40,40,128]{1,0,2:T(8,128)(2,1)} %copy.44, bf16[160,40,128]{1,0,2:T(8,128)(2,1)} %copy.45), kind=kOutput, calls=%fused_computation.1 | convolution fusion | flops 66355200 | bytes 3686400 | tf_op jit(solution)/shard_map/jkc,ikc->jic/dot_general | solution.py:52
  70.2 3.8 %copy.46 = bf16[160,40,128]{2,1,0:T(8,128)(2,1)} copy(bf16[160,40,128]{0,1,2:T(8,128)(2,1)S(1)} %convert_bitcast_fusion.1) | data formatting | bytes 3276800 | tf_op jit(solution)/shard_map/convert_element_type | solution.py:52
  74.1 0.7 fusion.23
  74.7 26.8 %reduce-scatter.3.cloned.1.call-done = bf16[40,40,128]{2,1,0:T(8,128)(2,1)} async-done(((bf16[160,40,128]{2,1,0:T(8,128)(2,1)}), bf16[40,40,128]{2,1,0:T(8,128)(2,1)}) %reduce-scatter.3.cloned.1.call-update) | async-done | bytes 409616 | tf_op jit(solution)/shard_map/reduce_scatter | solution.py:51
  101.6 1.3 bitcast_reduce_fusion
  103.0 1.5 fusion.43
  104.7 1.5 fusion.45
  106.2 0.4 fusion.81
  106.7 0.5 multiply_reduce_fusion
  107.2 0.5 multiply_convert_fusion
  108.1 1.1 fusion.29
  109.9 0.4 fusion.28
  110.3 1.8 copy.52
  112.1 17.4 %all-gather.5.cloned.1.call-done = bf16[40,160,128]{2,1,0:T(8,128)(2,1)} async-done(((bf16[40,40,128]{2,1,0:T(8,128)(2,1)}), bf16[40,160,128]{2,1,0:T(8,128)(2,1)}) %all-gather.5.cloned.1.call-update) | async-done | bytes 1638416 | tf_op jit(solution)/shard_map/all_gather | solution.py:64
  129.4 3.7 %copy.53 = bf16[40,160,128]{1,0,2:T(8,128)(2,1)S(1)} copy(bf16[40,160,128]{2,1,0:T(8,128)(2,1)} %all-gather.5.cloned.1.call-done) | data formatting | bytes 3276800 | tf_op jit(solution)/shard_map/all_gather | solution.py:64
  133.1 3.7 %convert_bitcast_fusion = bf16[160,40,128]{0,1,2:T(8,128)(2,1)} fusion(bf16[40,40,128]{0,1,2:T(8,128)(2,1)} %copy.52, bf16[40,160,128]{1,0,2:T(8,128)(2,1)S(1)} %copy.53), kind=kOutput, calls=%fused_computation | convolution fusion | flops 66355200 | bytes 3686400 | tf_op jit(solution)/shard_map/kic,kjc->ijc/dot_general | solution.py:67
  136.8 5.2 %copy.54 = bf16[160,40,128]{2,1,0:T(8,128)(2,1)} copy(bf16[160,40,128]{0,1,2:T(8,128)(2,1)} %convert_bitcast_fusion) | data formatting | bytes 3276800 | tf_op jit(solution)/shard_map/convert_element_type | solution.py:67
  142.4 36.1 %reduce-scatter.5.cloned.1.call-done = bf16[40,40,128]{2,1,0:T(8,128)(2,1)} async-done(((bf16[160,40,128]{2,1,0:T(8,128)(2,1)}), bf16[40,40,128]{2,1,0:T(8,128)(2,1)}) %reduce-scatter.5.cloned.1.call-update) | async-done | bytes 409616 | tf_op jit(solution)/shard_map/reduce_scatter | solution.py:66
  178.5 1.3 convert_reduce_fusion.1
  179.8 1.5 fusion.38
  181.3 2.4 %fusion.30 = bf16[40,40,128]{2,1,0:T(8,128)(2,1)} fusion(f32[40,40,128]{2,1,0:T(8,128)S(1)} %get-tuple-element.12, f32[40,40,128]{2,1,0:T(8,128)S(1)} %fusion.11, bf16[40,40,128]{2,1,0:T(8,128)(2,1)} %reduce-scatter.5.cloned.1.call-done, f32[128]{0:T(128)S(1)} %get-tuple-element.5, f32[40,40]{1,0:T(8,128)S(1)} %add_rsqrt_fusion, ...), kind=kOutput, calls=%fused_computation.44 | convolution fusion | flops 54067200 | bytes 2531840 | tf_op jit(solution)/shard_map/dot_general | solution.py:33
  (41 shorter events, 2.0 us)
Async XLA Ops:
  6.5 48.8 %all-gather.3.cloned.1.call-start = ((), (), s32[]{:S(2)}) async-start(), calls=%async_computation.2 | async-start | bytes 2048000 | tf_op jit(solution)/shard_map/all_gather | solution.py:49
  7.2 5.5 %copy-start = (bf16[40,40,128]{2,1,0:T(8,128)(2,1)S(1)}, bf16[40,40,128]{2,1,0:T(8,128)(2,1)}, u32[]{:S(2)}) copy-start(bf16[40,40,128]{2,1,0:T(8,128)(2,1)} %param.7) | copy-start | bytes 1228804
  7.2 5.5 %copy-start.4 = (bf16[2,4,128,128]{3,2,1,0:T(8,128)(2,1)S(1)}, bf16[2,4,128,128]{3,2,1,0:T(8,128)(2,1)}, u32[]{:S(2)}) copy-start(bf16[2,4,128,128]{3,2,1,0:T(8,128)(2,1)} %param.10) | copy-start | bytes 786436
  14.3 87.2 %reduce-scatter.3.cloned.1.call-start = ((), (), s32[]{:S(2)}) async-start(), calls=%async_computation.3 | async-start | bytes 2048000 | tf_op jit(solution)/shard_map/reduce_scatter | solution.py:51
  70.1 3.9 %copy-start.5 = (f32[2,128]{1,0:T(2,128)S(1)}, f32[2,128]{1,0:T(2,128)}, u32[]{:S(2)}) copy-start(f32[2,128]{1,0:T(2,128)} %param.12) | copy-start | bytes 3076
  70.2 3.9 %copy-start.6 = (bf16[2,128,128]{2,1,0:T(8,128)(2,1)S(1)}, bf16[2,128,128]{2,1,0:T(8,128)(2,1)}, u32[]{:S(2)}) copy-start(bf16[2,128,128]{2,1,0:T(8,128)(2,1)} %param.11) | copy-start | bytes 196612
  74.0 55.5 %all-gather.5.cloned.1.call-start = ((), (), s32[]{:S(2)}) async-start(), calls=%async_computation.4 | async-start | bytes 2048000 | tf_op jit(solution)/shard_map/all_gather | solution.py:64
  74.1 32.2 %copy-start.3 = (bf16[2,128,128]{2,1,0:T(8,128)(2,1)S(1)}, bf16[2,128,128]{2,1,0:T(8,128)(2,1)}, u32[]{:S(2)}) copy-start(bf16[2,128,128]{2,1,0:T(8,128)(2,1)} %param.13) | copy-start | bytes 196612
  107.7 2.2 %copy-start.1 = (bf16[40,40,128]{2,1,0:T(8,128)(2,1)}, bf16[40,40,128]{2,1,0:T(8,128)(2,1)S(1)}, u32[]{:S(2)}) copy-start(bf16[40,40,128]{2,1,0:T(8,128)(2,1)S(1)} %multiply_convert_fusion) | copy-start | bytes 1228804
  109.3 69.2 %reduce-scatter.5.cloned.1.call-start = ((), (), s32[]{:S(2)}) async-start(), calls=%async_computation.5 | async-start | bytes 2048000 | tf_op jit(solution)/shard_map/reduce_scatter | solution.py:66
  136.8 5.2 %copy-start.2 = (bf16[40,40,128]{2,1,0:T(8,128)(2,1)S(1)}, bf16[40,40,128]{2,1,0:T(8,128)(2,1)}, u32[]{:S(2)}) copy-start(bf16[40,40,128]{2,1,0:T(8,128)(2,1)} %copy-done.1) | copy-start | bytes 1228804
  136.8 5.2 %copy-start.7 = (bf16[2,128,128]{2,1,0:T(8,128)(2,1)S(1)}, bf16[2,128,128]{2,1,0:T(8,128)(2,1)}, u32[]{:S(2)}) copy-start(bf16[2,128,128]{2,1,0:T(8,128)(2,1)} %param.11) | copy-start | bytes 196612
Sparse Core Ops, SparseCore 0:
  14.4 40.8 all-gather.2
  74.1 27.4 reduce-scatter.2
  109.4 20.0 all-gather.4
  142.1 36.3 reduce-scatter.4
where the time goes:
time: 191 us; the launch traced here: 190 us
  waiting for transfers between devices  118 us (62%)
  local copies, waits for them, and re-layouts  26.3 us (14%)
  matrix products  20.7 us (11%)
  between operations  13.4 us (7%)
  other arithmetic  11.8 us (6%)
    all_gather x1, waiting for transfers between devices, body(): right_panel = lax.all_gather(right_side, 'row', axis=0, tiled=True)  37.4 us
    reduce_scatter x1, waiting for transfers between devices, body(): lax.psum_scatter(jnp.einsum('kic,kjc->ijc', block, right_side, preferred_...  36.1 us
    reduce_scatter x1, waiting for transfers between devices, body(): lax.psum_scatter(jnp.einsum('jkc,ikc->jic', block, left_side, preferred_e...  26.8 us
    all_gather x1, waiting for transfers between devices, body(): left_panel = lax.all_gather(left_side, 'col', axis=1, tiled=True)  17.4 us
    all_gather x1, local copies, waits for them, and re-layouts, body(): right_panel = lax.all_gather(right_side, 'row', axis=0, tiled=True)  8.66 us
    dot_general x8, matrix products, project_side(): jnp.dot(normed, proj_weights[layer_index, slot], preferred_element_type=j...  7.05 us
    dot_general x1, matrix products, body(): jnp.einsum('jkc,ikc->jic', block, left_side, preferred_element_type=jnp.f...  6.12 us
    convert_element_type x1, local copies, waits for them, and re-layouts, body(): jnp.einsum('kic,kjc->ijc', block, right_side, preferred_element_type=jnp....  5.18 us
  transfers between devices with their start and end apart: 4, of which 4 were waited for; matrix products, arithmetic and copies ran while one was open for 4% of the time, Pallas kernels for 0%

commit v1 on v0

v1 whole, which is shorter than its diff:
```python
import functools

import jax
import jax.numpy as jnp
from jax import lax
from jax.experimental import pallas as pl
from jax.experimental.pallas import tpu as pltpu
from jax.sharding import PartitionSpec as P

EPSILON = 1e-05
LANES = 128
F32 = jnp.float32
BF16 = jnp.bfloat16


def layer_norm(values, gain_vec):
    mean_val = jnp.mean(values, axis=-1, keepdims=True)
    centered = values - mean_val
    variance = jnp.mean(centered * centered, axis=-1, keepdims=True)
    return centered * jax.lax.rsqrt(variance + EPSILON) * gain_vec


def project_side(pair_tile, pair_valid, layer_index, in_gain, proj_weights, gate_weight):
    normed = layer_norm(pair_tile.astype(F32), in_gain[layer_index]).astype(BF16)
    outputs = [
        jnp.dot(normed, proj_weights[layer_index, slot], preferred_element_type=F32)
        for slot in range(4)
    ]
    weight_mask = pair_valid[..., None]
    left_side = (jax.nn.sigmoid(outputs[1]) * outputs[0] * weight_mask).astype(BF16)
    right_side = (jax.nn.sigmoid(outputs[3]) * outputs[2] * weight_mask).astype(BF16)
    gating = jax.nn.sigmoid(jnp.dot(normed, gate_weight[layer_index], preferred_element_type=F32))
    return (left_side, right_side, gating)


def finish(pair_tile, mixed_sum, gating, layer_index, out_gain, out_weight):
    normed = layer_norm(mixed_sum, out_gain[layer_index]).astype(BF16)
    update = jnp.dot(normed, out_weight[layer_index], preferred_element_type=F32)
    return (pair_tile.astype(F32) + gating * update).astype(BF16)


def pair_mask(token_mask, tile_rows, row_begin, tile_cols, col_begin):
    valid = token_mask.astype(F32)
    row_valid = lax.dynamic_slice_in_dim(valid, row_begin, tile_rows, 0)
    col_valid = lax.dynamic_slice_in_dim(valid, col_begin, tile_cols, 0)
    return row_valid[:, None] * col_valid[None, :]


def gather_body(pair_map, token_mask, in_gain, proj_weights, gate_weight, out_gain, out_weight):
    tile_rows, tile_cols = pair_map.shape[:2]
    pair_valid = pair_mask(
        token_mask,
        tile_rows,
        lax.axis_index("row") * tile_rows,
        tile_cols,
        lax.axis_index("col") * tile_cols,
    )
    left_side, right_side, gating = project_side(
        pair_map, pair_valid, 0, in_gain, proj_weights, gate_weight
    )
    block = lax.all_gather(right_side, "row", axis=0, tiled=True)
    summed = lax.psum_scatter(
        jnp.einsum("jkc,ikc->jic", block, left_side, preferred_element_type=F32).astype(BF16),
        "col",
        scatter_dimension=0,
        tiled=True,
    ).astype(F32)
    mixed = jnp.transpose(summed, (1, 0, 2))
    after_out = finish(pair_map, mixed, gating, 0, out_gain, out_weight)
    left_side, right_side, gating = project_side(
        after_out, pair_valid, 1, in_gain, proj_weights, gate_weight
    )
    block = lax.all_gather(left_side, "col", axis=1, tiled=True)
    mixed = lax.psum_scatter(
        jnp.einsum("kic,kjc->ijc", block, right_side, preferred_element_type=F32).astype(BF16),
        "row",
        scatter_dimension=0,
        tiled=True,
    ).astype(F32)
    return finish(after_out, mixed, gating, 1, out_gain, out_weight)


NEAR = 4


class Place:
    def __init__(self):
        z = lax.axis_index("row")
        col = lax.axis_index("col")
        self.z = z
        self.x = lax.div(col, 2)
        self.core = lax.rem(col, 2)
        self.half = lax.div(z, 2)
        self.group = lax.rem(z, 2) * 2 + self.x

    def channels(self, d, ch, other=False):
        core = 1 - self.core if other else self.core
        begin = jnp.bitwise_xor(self.group, d) * (2 * ch) + core * ch
        return pl.ds(pl.multiple_of(begin, ch), ch)


def lane_of(rows):
    return lax.broadcasted_iota(jnp.int32, (rows, LANES), 1)


def take_piece(value, index, width, lane):
    tile, offset = divmod(index * width, LANES)
    part = value[:, tile * LANES : (tile + 1) * LANES]
    if offset:
        part = pltpu.roll(part, LANES - offset, 1)
    if offset + width > LANES:
        after = value[:, (tile + 1) * LANES : (tile + 2) * LANES]
        part = jnp.where(lane < LANES - offset, part, pltpu.roll(after, LANES - offset, 1))
    return jnp.where(lane < width, part, 0.0)


def join_pieces(piece, count, width, tile, lane):
    low = tile * LANES
    out = None
    for index in range(low // width, min(count, -(-(low + LANES) // width))):
        shift = index * width - low
        part = piece(index)
        if shift % LANES:
            part = pltpu.roll(part, shift % LANES, 1)
        out = part if out is None else jnp.where(lane >= shift, part, out)
    return out


def column_of(ref, layer_index, lanes):
    tall = jnp.broadcast_to(ref[layer_index : layer_index + 1, :], (LANES, LANES)).T
    return jnp.concatenate([tall] * (lanes // LANES), axis=1)


def norm_rows(values, gain_col):
    mean_val = jnp.mean(values, axis=0, keepdims=True)
    centered = values - mean_val
    variance = jnp.mean(centered * centered, axis=0, keepdims=True)
    return (centered * lax.rsqrt(variance + EPSILON) * gain_col).astype(BF16)


def turned(weight):
    return weight.astype(F32).T.astype(BF16)


def select_weights(proj_ref, layer_index, turned_ref, chosen_ref, place, ch):
    for slot in range(4):
        turned_ref[slot] = turned(proj_ref[layer_index, slot])
    for slot in range(4):
        for d in range(NEAR):
            begin = (slot * NEAR + d) * ch
            chosen_ref[begin : begin + ch, :] = turned_ref[slot, place.channels(d, ch), :]


def project_chunk(normed, valid, chosen_ref, near_refs, far_refs, lanes, ch):
    out = jnp.dot(chosen_ref[...], normed, preferred_element_type=F32)
    half = NEAR * ch
    left = (jax.nn.sigmoid(out[half : 2 * half]) * out[:half] * valid).astype(BF16)
    right = (jax.nn.sigmoid(out[3 * half :]) * out[2 * half : 3 * half] * valid).astype(BF16)
    for d in range(NEAR):
        rows = slice(d * ch, (d + 1) * ch)
        near_refs[d][:ch, lanes] = left[rows]
        near_refs[d][ch:, lanes] = right[rows]
        if far_refs:
            far_refs[d][:, lanes] = right[rows]


def chunks_of(total, size):
    return [slice(begin, min(begin + size, total)) for begin in range(0, total, size)]


def first_kernel(
    chunk, own_ref, sibling_ref, valid_ref, gain_ref, proj_ref, *rest
):
    near_refs, far_refs = rest[:NEAR], rest[NEAR : 2 * NEAR]
    turned_pair_ref, normed_ref, pair_ref, turned_ref, chosen_ref = rest[2 * NEAR :]
    place = Place()
    rows, cols = own_ref.shape[:2]
    ch = far_refs[0].shape[0]
    total = valid_ref.shape[1]
    own_at = pl.multiple_of(place.core * cols, 8)
    sibling_at = pl.multiple_of((1 - place.core) * cols, 8)
    pair_ref[:, pl.ds(own_at, cols), :] = own_ref[...].astype(F32)
    pair_ref[:, pl.ds(sibling_at, cols), :] = sibling_ref[...].astype(F32)
    select_weights(proj_ref, 0, turned_ref, chosen_ref, place, ch)
    gain_col = column_of(gain_ref, 0, chunk)
    flat = pair_ref[...].reshape(total, LANES)
    for lanes in chunks_of(total, chunk):
        pair = flat[lanes].T
        turned_pair_ref[:, lanes] = pair.astype(BF16)
        normed = norm_rows(pair, gain_col)
        normed_ref[:, lanes] = normed
        project_chunk(normed, valid_ref[:, lanes], chosen_ref, near_refs, far_refs, lanes, ch)


def finish_chunk(mixed, pair, normed, gain_col, gate, weight):
    normed_out = norm_rows(mixed, gain_col)
    update = jnp.dot(weight, normed_out, preferred_element_type=F32)
    gating = jax.nn.sigmoid(jnp.dot(gate, normed, preferred_element_type=F32))
    return pair.astype(F32) + gating * update


def middle_kernel(chunk, *refs):
    mine, other = refs[:NEAR], refs[NEAR : 2 * NEAR]
    pair_ref, normed_in_ref, valid_ref, gain_ref, out_gain_ref = refs[2 * NEAR : 2 * NEAR + 5]
    proj_ref, gate_ref, weight_ref = refs[2 * NEAR + 5 : 2 * NEAR + 8]
    near_refs = refs[2 * NEAR + 8 : 3 * NEAR + 8]
    after_ref, normed_ref, mixed_ref, turned_ref, chosen_ref = refs[3 * NEAR + 8 :]
    place = Place()
    ch = mine[0].shape[0]
    total = valid_ref.shape[1]
    for d in range(NEAR):
        mixed_ref[place.channels(d, ch), :] = mine[d][...]
        mixed_ref[place.channels(d, ch, True), :] = other[d][...]
    select_weights(proj_ref, 1, turned_ref, chosen_ref, place, ch)
    gate, weight = turned(gate_ref[0]), turned(weight_ref[0])
    out_gain_col = column_of(out_gain_ref, 0, chunk)
    gain_col = column_of(gain_ref, 1, chunk)
    for lanes in chunks_of(total, chunk):
        after = finish_chunk(
            mixed_ref[:, lanes].astype(F32),
            pair_ref[:, lanes],
            normed_in_ref[:, lanes],
            out_gain_col,
            gate,
            weight,
        ).astype(BF16)
        after_ref[:, lanes] = after
        normed = norm_rows(after.astype(F32), gain_col)
        normed_ref[:, lanes] = normed
        project_chunk(normed, valid_ref[:, lanes], chosen_ref, near_refs, (), lanes, ch)


def last_kernel(chunk, *refs):
    mine, other = refs[: 2 * NEAR], refs[2 * NEAR : 4 * NEAR]
    pair_ref, normed_in_ref, out_gain_ref, gate_ref, weight_ref = refs[4 * NEAR : 4 * NEAR + 5]
    out_ref, mixed_ref, after_ref = refs[4 * NEAR + 5 :]
    place = Place()
    ch = mine[0].shape[0]
    total = pair_ref.shape[1]
    rows, cols = out_ref.shape[:2]
    for d in range(NEAR):
        for parts, flag in ((mine, False), (other, True)):
            summed = parts[d][...].astype(F32) + parts[NEAR + d][...].astype(F32)
            mixed_ref[place.channels(d, ch, flag), :] = summed
    gate, weight = turned(gate_ref[1]), turned(weight_ref[1])
    out_gain_col = column_of(out_gain_ref, 1, chunk)
    for lanes in chunks_of(total, chunk):
        after = finish_chunk(
            mixed_ref[:, lanes],
            pair_ref[:, lanes],
            normed_in_ref[:, lanes],
            out_gain_col,
            gate,
            weight,
        )
        after_ref[lanes, :] = after.T
    own_at = pl.multiple_of(place.core * cols, 8)
    for row in range(rows):
        out_ref[row] = after_ref[pl.ds(row * 2 * cols + own_at, cols), :].astype(BF16)


def outgoing_kernel(rows, width, *refs):
    near, far = refs[:NEAR], refs[NEAR : 2 * NEAR]
    outs = refs[2 * NEAR : 3 * NEAR]
    left_ref, right_ref, mixed_ref = refs[3 * NEAR :]
    place = Place()
    ch = far[0].shape[0]
    lane = lane_of(ch)

    def spread(value, ref, side, begin):
        for row in range(rows):
            ref[side, pl.ds(begin + row * ch, ch), :] = take_piece(value, row, width, lane)

    for d in range(NEAR):
        dl, dx = divmod(d, 2)
        for dh, ref in ((0, near[d]), (1, far[d])):
            z = jnp.bitwise_xor(place.z, 2 * dh + dl)
            block = jnp.bitwise_xor(lax.div(z, 2), place.x) * 2 + lax.rem(z, 2)
            begin = pl.multiple_of(block * (rows * ch), 16)
            value = ref[...].astype(F32)
            if dh == 0:
                spread(value[:ch], left_ref, dx, dl * rows * ch)
                value = value[ch:]
            spread(value, right_ref, dx, begin)
    tall = 2 * rows
    for c in range(ch):
        left = jnp.concatenate(
            [left_ref[side, pl.ds(c, tall, stride=ch), :] for side in range(2)], axis=1
        ).astype(BF16)
        for block in range(2):
            begin = block * tall * ch + c
            right = jnp.concatenate(
                [right_ref[side, pl.ds(begin, tall, stride=ch), :] for side in range(2)], axis=1
            ).astype(BF16)
            part = lax.dot_general(
                left, right, (((1,), (1,)), ((), ())), preferred_element_type=F32
            )
            mixed_ref[block, pl.ds(c, tall, stride=ch), :] = jnp.pad(
                part, ((0, 0), (0, LANES - tall))
            )
    for d in range(NEAR):
        dl, dx = divmod(d, 2)
        for tile in range(rows * width // LANES):
            outs[d][:, tile * LANES : (tile + 1) * LANES] = join_pieces(
                lambda row: mixed_ref[dx, pl.ds((dl * rows + row) * ch, ch), :],
                rows,
                width,
                tile,
                lane,
            ).astype(BF16)


def incoming_kernel(rows, width, *refs):
    near = refs[:NEAR]
    outs = refs[NEAR : 3 * NEAR]
    left_ref, right_ref, mixed_ref = refs[3 * NEAR :]
    place = Place()
    ch = outs[0].shape[0]
    lane = lane_of(ch)
    for d in range(NEAR):
        dl, dx = divmod(d, 2)
        value = near[d][...].astype(F32)
        for side, ref in ((value[:ch], left_ref), (value[ch:], right_ref)):
            for row in range(rows):
                ref[dx, pl.ds((dl * rows + row) * ch, ch), :] = take_piece(side, row, width, lane)
    tall = 2 * rows
    for c in range(ch):
        right = jnp.concatenate(
            [right_ref[side, pl.ds(c, tall, stride=ch), :] for side in range(2)], axis=1
        ).astype(BF16)
        for block in range(2):
            left = left_ref[block, pl.ds(c, tall, stride=ch), :].astype(BF16)
            part = lax.dot_general(
                left, right, (((0,), (0,)), ((), ())), preferred_element_type=F32
            )
            for side in range(2):
                mixed_ref[side, pl.ds(block * width * ch + c, width, stride=ch), :] = part[
                    :width, side * LANES : (side + 1) * LANES
                ]
    for d in range(2 * NEAR):
        dz, dx = divmod(d, 2)
        z = jnp.bitwise_xor(place.z, dz)
        block = jnp.bitwise_xor(lax.div(z, 2), place.x) * 2 + lax.rem(z, 2)
        begin = pl.multiple_of(block * (rows * ch), 16)
        for tile in range(rows * width // LANES):
            outs[d][:, tile * LANES : (tile + 1) * LANES] = join_pieces(
                lambda row: mixed_ref[dx, pl.ds(begin + row * ch, ch), :],
                rows,
                width,
                tile,
                lane,
            ).astype(BF16)


def call(kernel, outs, scratch, *args):
    return pl.pallas_call(
        kernel,
        out_shape=[jax.ShapeDtypeStruct(shape, BF16) for shape in outs],
        in_specs=[pl.BlockSpec(memory_space=pltpu.VMEM) for _ in args],
        out_specs=[pl.BlockSpec(memory_space=pltpu.VMEM) for _ in outs],
        scratch_shapes=[pltpu.VMEM(shape, dtype) for shape, dtype in scratch],
        compiler_params=pltpu.CompilerParams(vmem_limit_bytes=24 * 2**20),
    )(*args)


def direct_body(pair_map, token_mask, in_gain, proj_weights, gate_weight, out_gain, out_weight):
    n_row, n_col = lax.axis_size("row"), lax.axis_size("col")
    rows, cols, channels = pair_map.shape
    width = 2 * cols
    total = rows * width
    ch = channels // (2 * NEAR)
    chunk = 5 * LANES

    def swap(value, dz, dx, core=0):
        flip = dz * n_col + dx * 2 + core
        pairs = [(i, i ^ flip) for i in range(n_row * n_col)]
        return lax.ppermute(value, ("row", "col"), pairs)

    def swap_all(values, offset):
        got = [None] * len(values)
        for d in reversed(range(len(values))):
            dz, dx = divmod(d + offset, 2)
            got[d] = swap(values[d], dz, dx) if d + offset else values[d]
        return got

    sibling = swap(pair_map, 0, 0, 1)
    chip_x = lax.div(lax.axis_index("col"), 2)
    valid = pair_mask(
        token_mask, rows, lax.axis_index("row") * rows, width, chip_x * width
    ).reshape(1, total)
    wide = (channels, total)
    weights_scratch = [((4, channels, channels), BF16), ((4 * NEAR * ch, channels), BF16)]

    out = call(
        functools.partial(first_kernel, chunk),
        [(2 * ch, total)] * NEAR + [(ch, total)] * NEAR + [wide, wide],
        [((rows, width, channels), F32)] + weights_scratch,
        pair_map,
        sibling,
        valid,
        in_gain,
        proj_weights,
    )
    far = swap_all(out[NEAR : 2 * NEAR], NEAR)
    near = swap_all(out[:NEAR], 0)
    pair, normed = out[2 * NEAR :]
    tall = 2 * rows
    mixed = call(
        functools.partial(outgoing_kernel, rows, width),
        [(ch, total)] * NEAR,
        [((2, tall * ch, LANES), F32), ((2, 2 * tall * ch, LANES), F32), ((2, tall * ch, LANES), F32)],
        *near,
        *far,
    )
    mixed = swap_all(mixed, 0)
    other = [swap(part, 0, 0, 1) for part in mixed]

    out = call(
        functools.partial(middle_kernel, chunk),
        [(2 * ch, total)] * NEAR + [wide, wide],
        [(wide, BF16)] + weights_scratch,
        *mixed,
        *other,
        pair,
        normed,
        valid,
        in_gain,
        out_gain,
        proj_weights,
        gate_weight,
        out_weight,
    )
    near = swap_all(out[:NEAR], 0)
    pair, normed = out[NEAR:]
    mixed = call(
        functools.partial(incoming_kernel, rows, width),
        [(ch, total)] * (2 * NEAR),
        [((2, tall * ch, LANES), F32), ((2, tall * ch, LANES), F32), ((2, 2 * width * ch, LANES), F32)],
        *near,
    )
    mixed = swap_all(mixed, 0)
    other = [swap(part, 0, 0, 1) for part in mixed]
    return call(
        functools.partial(last_kernel, chunk),
        [(rows, cols, channels)],
        [(wide, F32), ((total, channels), F32)],
        *mixed,
        *other,
        pair,
        normed,
        out_gain,
        gate_weight,
        out_weight,
    )[0]


def solution(mesh):
    in_specs = (P(("groups", "row"), "col", None), P("groups"), P(), P(), P(), P(), P())
    out_specs = P(("groups", "row"), "col", None)
    direct = mesh.shape["row"] == 4 and mesh.shape["col"] == 4
    body = direct_body if direct else gather_body
    return jax.shard_map(body, mesh=mesh, in_specs=in_specs, out_specs=out_specs, check_vma=False)
```

time: 191 us -> 89.1 us (0.47)
  waiting for transfers between devices: 118 us -> 35.3 us
  starting transfers between devices: 0.31 us -> 37.2 us
  local copies, waits for them, and re-layouts: 26.3 us -> 3.56 us
  matrix products: 20.7 us -> 0 us
  between operations: 13.4 us -> 0.09 us
  Pallas kernels: 0 us -> 12 us
  other arithmetic: 11.8 us -> 0.08 us
    reduce_scatter x2 -> x0, waiting for transfers between devices: 62.9 us -> none  [the longest x1 36.1 us: body(): lax.psum_scatter(jnp.einsum('kic,kjc->ijc', block, right_side, preferred_...]
    all_gather x2 -> x0, waiting for transfers between devices: 54.7 us -> none  [the longest x1 37.4 us: body(): right_panel = lax.all_gather(right_side, 'row', axis=0, tiled=True)]
    ppermute x0 -> x33, starting transfers between devices: none -> 37.2 us  [swap(): return lax.ppermute(value, ('row', 'col'), pairs)]
    ppermute x0 -> x33, waiting for transfers between devices: none -> 35.3 us  [swap(): return lax.ppermute(value, ('row', 'col'), pairs)]
    dot_general x14 -> x0, matrix products: 20.7 us -> none  [the longest x8 7.05 us: project_side(): jnp.dot(normed, proj_weights[layer_index, slot], preferred_element_type=j...]
    convert_element_type x4 -> x0, local copies, waits for them, and re-layouts: 12.8 us -> none  [the longest x1 5.18 us: body(): jnp.einsum('kic,kjc->ijc', block, right_side, preferred_element_type=jnp....]
    all_gather x2 -> x0, local copies, waits for them, and re-layouts: 12.3 us -> none  [the longest x1 8.66 us: body(): right_panel = lax.all_gather(right_side, 'row', axis=0, tiled=True)]
    pallas_call x0 -> x5, Pallas kernels: none -> 12 us  [call(): pl.pallas_call(kernel, out_shape=[jax.ShapeDtypeStruct(shape, BF16) for s...]
  transfers between devices with their start and end apart: 4 -> 33, of which waited for: 4 -> 19; matrix products, arithmetic and copies ran while one was open for 4% -> 0% of each run, Pallas kernels for 0% -> 0%
where the time goes in v1:
time: 89.1 us; the launch traced here: 88.2 us
  starting transfers between devices  37.2 us (42%)
  waiting for transfers between devices  35.3 us (40%)
  Pallas kernels  12 us (13%)
  local copies, waits for them, and re-layouts  3.56 us (4%)
    ppermute x33, starting transfers between devices, swap(): return lax.ppermute(value, ('row', 'col'), pairs)  37.2 us
    ppermute x33, waiting for transfers between devices, swap(): return lax.ppermute(value, ('row', 'col'), pairs)  35.3 us
    pallas_call x5, Pallas kernels, call(): pl.pallas_call(kernel, out_shape=[jax.ShapeDtypeStruct(shape, BF16) for s...  12 us
    unnamed x16, local copies, waits for them, and re-layouts  3.32 us
  transfers between devices with their start and end apart: 33, of which 19 were waited for; matrix products, arithmetic and copies ran while one was open for 0% of the time, Pallas kernels for 0%

profile of v1, /device:TPU:0, one launch (start us, length us, event | category | flops | bytes accessed | tf_op | source)
XLA Modules:
  0.0 88.2 jit_solution(5835880742793243820)
XLA Ops:
  3.0 1.0 %copy-done.2 = bf16[40,40,128]{2,1,0:T(8,128)(2,1)S(1)} copy-done((bf16[40,40,128]{2,1,0:T(8,128)(2,1)S(1)}, bf16[40,40,128]{2,1,0:T(8,128)(2,1)}, u32[]{:S(2)}) %copy-start.2) | copy-done | bytes 409624
  4.0 1.3 %shard_map.73 = (bf16[32,3200]{1,0:T(8,128)(2,1)S(1)}, bf16[32,3200]{1,0:T(8,128)(2,1)S(1)}, bf16[32,3200]{1,0:T(8,128)(2,1)S(1)}, bf16[32,3200]{1,0:T(8,128)(2,...) custom-call(bf16[40,40,128]{2,1,0:T(8,128)(2,1)S(1)} %copy-done.2, ...), custom_call_target="tpu_custom_call" | custom-call | tf_op jit(solution)/shard_map/pallas_call | solution.py:356
  5.3 4.0 %collective-permute-start.4 = (bf16[16,3200]{1,0:T(8,128)(2,1)S(1)}, bf16[16,3200]{1,0:T(8,128)(2,1)S(1)}, u32[]{:S(2)}, u32[]{:S(2)}) collective-permute-start(bf16[16,3200]{1,0:T(8,128)(2,1)S(1)} %get-tuple-element.37), channel_id=1, source_target_pairs={{0,8},{1,9},{2,10},{3,11},{4,12},{5,13},{6,14},{7,15},{8,0},{9,1},... | collective-permute-start | bytes 307208 | tf_op jit(solution)/shard_map/ppermute | solution.py:377
  9.4 1.3 %collective-permute-start.5 = (bf16[16,3200]{1,0:T(8,128)(2,1)S(1)}, bf16[16,3200]{1,0:T(8,128)(2,1)S(1)}, u32[]{:S(2)}, u32[]{:S(2)}) collective-permute-start(bf16[16,3200]{1,0:T(8,128)(2,1)S(1)} %get-tuple-element.38), channel_id=1, source_target_pairs={{0,10},{1,11},{2,8},{3,9},{4,14},{5,15},{6,12},{7,13},{8,2},{9,3},... | collective-permute-start | bytes 307208 | tf_op jit(solution)/shard_map/ppermute | solution.py:377
  10.9 1.8 %collective-permute-start.2 = (bf16[32,3200]{1,0:T(8,128)(2,1)S(1)}, bf16[32,3200]{1,0:T(8,128)(2,1)S(1)}, u32[]{:S(2)}, u32[]{:S(2)}) collective-permute-start(bf16[32,3200]{1,0:T(8,128)(2,1)S(1)} %get-tuple-element.35), channel_id=1, source_target_pairs={{0,4},{1,5},{2,6},{3,7},{4,0},{5,1},{6,2},{7,3},{8,12},{9,13},{10,... | collective-permute-start | bytes 614408 | tf_op jit(solution)/shard_map/ppermute | solution.py:377
  12.7 1.4 %collective-permute-start.3 = (bf16[32,3200]{1,0:T(8,128)(2,1)S(1)}, bf16[32,3200]{1,0:T(8,128)(2,1)S(1)}, u32[]{:S(2)}, u32[]{:S(2)}) collective-permute-start(bf16[32,3200]{1,0:T(8,128)(2,1)S(1)} %get-tuple-element.36), channel_id=1, source_target_pairs={{0,6},{1,7},{2,4},{3,5},{4,2},{5,3},{6,0},{7,1},{8,14},{9,15},{10,... | collective-permute-start | bytes 614408 | tf_op jit(solution)/shard_map/ppermute | solution.py:377
  14.1 2.8 %collective-permute-done.4.refs_4_ = bf16[16,3200]{1,0:T(8,128)(2,1)S(1)} collective-permute-done((bf16[16,3200]{1,0:T(8,128)(2,1)S(1)}, bf16[16,3200]{1,0:T(8,128)(2,1)S(1)}, u32[]{:S(2)}, u32[]{:S(2)}) %collective-permute-start.4) | collective-permute-done | bytes 102432 | tf_op jit(solution)/shard_map/ppermute | solution.py:377
  16.9 3.8 %collective-permute-start.6 = (bf16[16,3200]{1,0:T(8,128)(2,1)S(1)}, bf16[16,3200]{1,0:T(8,128)(2,1)S(1)}, u32[]{:S(2)}, u32[]{:S(2)}) collective-permute-start(bf16[16,3200]{1,0:T(8,128)(2,1)S(1)} %get-tuple-element.39), channel_id=1, source_target_pairs={{0,12},{1,13},{2,14},{3,15},{4,8},{5,9},{6,10},{7,11},{8,4},{9,5},... | collective-permute-start | bytes 307208 | tf_op jit(solution)/shard_map/ppermute | solution.py:377
  20.7 3.0 %collective-permute-start.7 = (bf16[16,3200]{1,0:T(8,128)(2,1)S(1)}, bf16[16,3200]{1,0:T(8,128)(2,1)S(1)}, u32[]{:S(2)}, u32[]{:S(2)}) collective-permute-start(bf16[16,3200]{1,0:T(8,128)(2,1)S(1)} %get-tuple-element.40), channel_id=1, source_target_pairs={{0,14},{1,15},{2,12},{3,13},{4,10},{5,11},{6,8},{7,9},{8,6},{9,7},... | collective-permute-start | bytes 307208 | tf_op jit(solution)/shard_map/ppermute | solution.py:377
  23.7 5.4 %collective-permute-done.6.refs_6_ = bf16[16,3200]{1,0:T(8,128)(2,1)S(1)} collective-permute-done((bf16[16,3200]{1,0:T(8,128)(2,1)S(1)}, bf16[16,3200]{1,0:T(8,128)(2,1)S(1)}, u32[]{:S(2)}, u32[]{:S(2)}) %collective-permute-start.6) | collective-permute-done | bytes 102432 | tf_op jit(solution)/shard_map/ppermute | solution.py:377
  29.1 1.1 %collective-permute-done.7.refs_7_ = bf16[16,3200]{1,0:T(8,128)(2,1)S(1)} collective-permute-done((bf16[16,3200]{1,0:T(8,128)(2,1)S(1)}, bf16[16,3200]{1,0:T(8,128)(2,1)S(1)}, u32[]{:S(2)}, u32[]{:S(2)}) %collective-permute-start.7) | collective-permute-done | bytes 102432 | tf_op jit(solution)/shard_map/ppermute | solution.py:377
  30.4 2.8 %shard_map.74 = (bf16[16,3200]{1,0:T(8,128)(2,1)S(1)}, bf16[16,3200]{1,0:T(8,128)(2,1)S(1)}, bf16[16,3200]{1,0:T(8,128)(2,1)S(1)}, bf16[16,3200]{1,0:T(8,128)(2,1)S(1)}) custom-call(bf16[32,3200]{1,0:T(8,128)(2,1)S(1)} %get-tuple-element.33.refs_0_, bf16[32,3200]{1,0:T(8,128)(2,1)S(1)} %collective-permute-done.1.refs_1_, ...), custom_call_target="tpu_custom_call" | custom-call | tf_op jit(solution)/shard_map/pallas_call | solution.py:356
  33.2 1.3 %collective-permute-start.8 = (bf16[16,3200]{1,0:T(8,128)(2,1)S(1)}, bf16[16,3200]{1,0:T(8,128)(2,1)S(1)}, u32[]{:S(2)}, u32[]{:S(2)}) collective-permute-start(bf16[16,3200]{1,0:T(8,128)(2,1)S(1)} %get-tuple-element.42), channel_id=1, source_target_pairs={{0,2},{1,3},{2,0},{3,1},{4,6},{5,7},{6,4},{7,5},{8,10},{9,11},{10,... | collective-permute-start | bytes 307208 | tf_op jit(solution)/shard_map/ppermute | solution.py:377
  34.6 2.2 %collective-permute-start.10 = (bf16[16,3200]{1,0:T(8,128)(2,1)S(1)}, bf16[16,3200]{1,0:T(8,128)(2,1)S(1)}, u32[]{:S(2)}, u32[]{:S(2)}) collective-permute-start(bf16[16,3200]{1,0:T(8,128)(2,1)S(1)} %get-tuple-element.44), channel_id=1, source_target_pairs={{0,6},{1,7},{2,4},{3,5},{4,2},{5,3},{6,0},{7,1},{8,14},{9,15},{10,... | collective-permute-start | bytes 307208 | tf_op jit(solution)/shard_map/ppermute | solution.py:377
  36.8 2.3 %collective-permute-done.8.refs_1_ = bf16[16,3200]{1,0:T(8,128)(2,1)S(1)} collective-permute-done((bf16[16,3200]{1,0:T(8,128)(2,1)S(1)}, bf16[16,3200]{1,0:T(8,128)(2,1)S(1)}, u32[]{:S(2)}, u32[]{:S(2)}) %collective-permute-start.8) | collective-permute-done | bytes 102432 | tf_op jit(solution)/shard_map/ppermute | solution.py:377
  40.6 1.3 %collective-permute-done.14.refs_7_ = bf16[16,3200]{1,0:T(8,128)(2,1)S(1)} collective-permute-done((bf16[16,3200]{1,0:T(8,128)(2,1)S(1)}, bf16[16,3200]{1,0:T(8,128)(2,1)S(1)}, u32[]{:S(2)}, u32[]{:S(2)}) %collective-permute-start.14) | collective-permute-done | bytes 102432 | tf_op jit(solution)/shard_map/ppermute | solution.py:377
  42.5 2.5 %shard_map.75 = (bf16[32,3200]{1,0:T(8,128)(2,1)S(1)}, bf16[32,3200]{1,0:T(8,128)(2,1)S(1)}, bf16[32,3200]{1,0:T(8,128)(2,1)S(1)}, bf16[32,3200]{1,0:T(8,128)(2,...) custom-call(bf16[16,3200]{1,0:T(8,128)(2,1)S(1)} %get-tuple-element.41.refs_0_, ...), custom_call_target="tpu_custom_call" | custom-call | tf_op jit(solution)/shard_map/pallas_call | solution.py:356
  45.0 1.4 %collective-permute-start.15 = (bf16[32,3200]{1,0:T(8,128)(2,1)S(1)}, bf16[32,3200]{1,0:T(8,128)(2,1)S(1)}, u32[]{:S(2)}, u32[]{:S(2)}) collective-permute-start(bf16[32,3200]{1,0:T(8,128)(2,1)S(1)} %get-tuple-element.48), channel_id=1, source_target_pairs={{0,2},{1,3},{2,0},{3,1},{4,6},{5,7},{6,4},{7,5},{8,10},{9,11},{10,... | collective-permute-start | bytes 614408 | tf_op jit(solution)/shard_map/ppermute | solution.py:377
  46.4 1.1 %collective-permute-start.16 = (bf16[32,3200]{1,0:T(8,128)(2,1)S(1)}, bf16[32,3200]{1,0:T(8,128)(2,1)S(1)}, u32[]{:S(2)}, u32[]{:S(2)}) collective-permute-start(bf16[32,3200]{1,0:T(8,128)(2,1)S(1)} %get-tuple-element.49), channel_id=1, source_target_pairs={{0,4},{1,5},{2,6},{3,7},{4,0},{5,1},{6,2},{7,3},{8,12},{9,13},{10,... | collective-permute-start | bytes 614408 | tf_op jit(solution)/shard_map/ppermute | solution.py:377
  47.5 1.1 %collective-permute-start.17 = (bf16[32,3200]{1,0:T(8,128)(2,1)S(1)}, bf16[32,3200]{1,0:T(8,128)(2,1)S(1)}, u32[]{:S(2)}, u32[]{:S(2)}) collective-permute-start(bf16[32,3200]{1,0:T(8,128)(2,1)S(1)} %get-tuple-element.50), channel_id=1, source_target_pairs={{0,6},{1,7},{2,4},{3,5},{4,2},{5,3},{6,0},{7,1},{8,14},{9,15},{10,... | collective-permute-start | bytes 614408 | tf_op jit(solution)/shard_map/ppermute | solution.py:377
  48.6 3.6 %collective-permute-done.15.refs_1_ = bf16[32,3200]{1,0:T(8,128)(2,1)S(1)} collective-permute-done((bf16[32,3200]{1,0:T(8,128)(2,1)S(1)}, bf16[32,3200]{1,0:T(8,128)(2,1)S(1)}, u32[]{:S(2)}, u32[]{:S(2)}) %collective-permute-start.15) | collective-permute-done | bytes 204832 | tf_op jit(solution)/shard_map/ppermute | solution.py:377
  52.2 2.1 %collective-permute-done.16.refs_2_ = bf16[32,3200]{1,0:T(8,128)(2,1)S(1)} collective-permute-done((bf16[32,3200]{1,0:T(8,128)(2,1)S(1)}, bf16[32,3200]{1,0:T(8,128)(2,1)S(1)}, u32[]{:S(2)}, u32[]{:S(2)}) %collective-permute-start.16) | collective-permute-done | bytes 204832 | tf_op jit(solution)/shard_map/ppermute | solution.py:377
  54.4 3.4 %collective-permute-done.17.refs_3_ = bf16[32,3200]{1,0:T(8,128)(2,1)S(1)} collective-permute-done((bf16[32,3200]{1,0:T(8,128)(2,1)S(1)}, bf16[32,3200]{1,0:T(8,128)(2,1)S(1)}, u32[]{:S(2)}, u32[]{:S(2)}) %collective-permute-start.17) | collective-permute-done | bytes 204832 | tf_op jit(solution)/shard_map/ppermute | solution.py:377
  57.8 3.2 %shard_map.76 = (bf16[16,3200]{1,0:T(8,128)(2,1)S(1)}, bf16[16,3200]{1,0:T(8,128)(2,1)S(1)}, bf16[16,3200]{1,0:T(8,128)(2,1)S(1)}, bf16[16,3200]{1,0:T(8,128)(2,...) custom-call(bf16[32,3200]{1,0:T(8,128)(2,1)S(1)} %get-tuple-element., ...), custom_call_target="tpu_custom_call" | custom-call | tf_op jit(solution)/shard_map/pallas_call | solution.py:356
  61.0 1.4 %collective-permute-start.18 = (bf16[16,3200]{1,0:T(8,128)(2,1)S(1)}, bf16[16,3200]{1,0:T(8,128)(2,1)S(1)}, u32[]{:S(2)}, u32[]{:S(2)}) collective-permute-start(bf16[16,3200]{1,0:T(8,128)(2,1)S(1)} %get-tuple-element.52), channel_id=1, source_target_pairs={{0,2},{1,3},{2,0},{3,1},{4,6},{5,7},{6,4},{7,5},{8,10},{9,11},{10,... | collective-permute-start | bytes 307208 | tf_op jit(solution)/shard_map/ppermute | solution.py:377
  62.4 1.1 %collective-permute-start.19 = (bf16[16,3200]{1,0:T(8,128)(2,1)S(1)}, bf16[16,3200]{1,0:T(8,128)(2,1)S(1)}, u32[]{:S(2)}, u32[]{:S(2)}) collective-permute-start(bf16[16,3200]{1,0:T(8,128)(2,1)S(1)} %get-tuple-element.53), channel_id=1, source_target_pairs={{0,4},{1,5},{2,6},{3,7},{4,0},{5,1},{6,2},{7,3},{8,12},{9,13},{10,... | collective-permute-start | bytes 307208 | tf_op jit(solution)/shard_map/ppermute | solution.py:377
  63.5 1.1 %collective-permute-start.20 = (bf16[16,3200]{1,0:T(8,128)(2,1)S(1)}, bf16[16,3200]{1,0:T(8,128)(2,1)S(1)}, u32[]{:S(2)}, u32[]{:S(2)}) collective-permute-start(bf16[16,3200]{1,0:T(8,128)(2,1)S(1)} %get-tuple-element.54), channel_id=1, source_target_pairs={{0,6},{1,7},{2,4},{3,5},{4,2},{5,3},{6,0},{7,1},{8,14},{9,15},{10,... | collective-permute-start | bytes 307208 | tf_op jit(solution)/shard_map/ppermute | solution.py:377
  64.6 4.0 %collective-permute-start.21 = (bf16[16,3200]{1,0:T(8,128)(2,1)S(1)}, bf16[16,3200]{1,0:T(8,128)(2,1)S(1)}, u32[]{:S(2)}, u32[]{:S(2)}) collective-permute-start(bf16[16,3200]{1,0:T(8,128)(2,1)S(1)} %get-tuple-element.55), channel_id=1, source_target_pairs={{0,8},{1,9},{2,10},{3,11},{4,12},{5,13},{6,14},{7,15},{8,0},{9,1},... | collective-permute-start | bytes 307208 | tf_op jit(solution)/shard_map/ppermute | solution.py:377
  69.6 2.6 %collective-permute-start.23 = (bf16[16,3200]{1,0:T(8,128)(2,1)S(1)}, bf16[16,3200]{1,0:T(8,128)(2,1)S(1)}, u32[]{:S(2)}, u32[]{:S(2)}) collective-permute-start(bf16[16,3200]{1,0:T(8,128)(2,1)S(1)} %get-tuple-element.57), channel_id=1, source_target_pairs={{0,12},{1,13},{2,14},{3,15},{4,8},{5,9},{6,10},{7,11},{8,4},{9,5},... | collective-permute-start | bytes 307208 | tf_op jit(solution)/shard_map/ppermute | solution.py:377
  72.2 1.2 %collective-permute-start.24 = (bf16[16,3200]{1,0:T(8,128)(2,1)S(1)}, bf16[16,3200]{1,0:T(8,128)(2,1)S(1)}, u32[]{:S(2)}, u32[]{:S(2)}) collective-permute-start(bf16[16,3200]{1,0:T(8,128)(2,1)S(1)} %get-tuple-element.58), channel_id=1, source_target_pairs={{0,14},{1,15},{2,12},{3,13},{4,10},{5,11},{6,8},{7,9},{8,6},{9,7},... | collective-permute-start | bytes 307208 | tf_op jit(solution)/shard_map/ppermute | solution.py:377
  73.9 9.6 %collective-permute-done.22.refs_5_ = bf16[16,3200]{1,0:T(8,128)(2,1)S(1)} collective-permute-done((bf16[16,3200]{1,0:T(8,128)(2,1)S(1)}, bf16[16,3200]{1,0:T(8,128)(2,1)S(1)}, u32[]{:S(2)}, u32[]{:S(2)}) %collective-permute-start.22) | collective-permute-done | bytes 102432 | tf_op jit(solution)/shard_map/ppermute | solution.py:377
  86.1 2.1 %shard_map.77 = bf16[40,40,128]{2,1,0:T(8,128)(2,1)} custom-call(bf16[16,3200]{1,0:T(8,128)(2,1)S(1)} %get-tuple-element.51.refs_0_, bf16[16,3200]{1,0:T(8,128)(2,1)S(1)} %collective-permute-done.18.refs_1_, bf16[16,3200]{1,0:T(8,128)(2,1)S(1)} %collective-permute-done.19.refs_2_, bf16[16,3200]{1,0:T(8,128)(2,1)S(1)} %collective-permute-done.20.refs_3_, ...), custom_call_target="tpu_custom_call" | custom-call | tf_op jit(solution)/shard_map/pallas_call | solution.py:356
  (60 shorter events, 9.8 us)
Async XLA Ops:
  0.0 2.0 %collective-permute-start = (bf16[40,40,128]{2,1,0:T(8,128)(2,1)}, bf16[40,40,128]{2,1,0:T(8,128)(2,1)S(1)}, u32[]{:S(2)}, u32[]{:S(2)}) collective-permute-start(bf16[40,40,128]{2,1,0:T(8,128)(2,1)} %own_ref.1), channel_id=1, source_target_pairs={{0,1},{1,0},{2,3},{3,2},{4,5},{5,4},{6,7},{7,6},{8,9},{9,8},{10,11... | collective-permute-start | bytes 1228808 | tf_op jit(solution)/shard_map/ppermute | solution.py:377
  5.3 11.5 %collective-permute-start.4 = (bf16[16,3200]{1,0:T(8,128)(2,1)S(1)}, bf16[16,3200]{1,0:T(8,128)(2,1)S(1)}, u32[]{:S(2)}, u32[]{:S(2)}) collective-permute-start(bf16[16,3200]{1,0:T(8,128)(2,1)S(1)} %get-tuple-element.37), channel_id=1, source_target_pairs={{0,8},{1,9},{2,10},{3,11},{4,12},{5,13},{6,14},{7,15},{8,0},{9,1},... | collective-permute-start | bytes 307208 | tf_op jit(solution)/shard_map/ppermute | solution.py:377
  9.4 11.3 %collective-permute-start.5 = (bf16[16,3200]{1,0:T(8,128)(2,1)S(1)}, bf16[16,3200]{1,0:T(8,128)(2,1)S(1)}, u32[]{:S(2)}, u32[]{:S(2)}) collective-permute-start(bf16[16,3200]{1,0:T(8,128)(2,1)S(1)} %get-tuple-element.38), channel_id=1, source_target_pairs={{0,10},{1,11},{2,8},{3,9},{4,14},{5,15},{6,12},{7,13},{8,2},{9,3},... | collective-permute-start | bytes 307208 | tf_op jit(solution)/shard_map/ppermute | solution.py:377
  10.6 19.5 %collective-permute-start.1 = (bf16[32,3200]{1,0:T(8,128)(2,1)S(1)}, bf16[32,3200]{1,0:T(8,128)(2,1)S(1)}, u32[]{:S(2)}, u32[]{:S(2)}) collective-permute-start(bf16[32,3200]{1,0:T(8,128)(2,1)S(1)} %get-tuple-element.34), channel_id=1, source_target_pairs={{0,2},{1,3},{2,0},{3,1},{4,6},{5,7},{6,4},{7,5},{8,10},{9,11},{10,... | collective-permute-start | bytes 614408 | tf_op jit(solution)/shard_map/ppermute | solution.py:377
  10.9 19.3 %collective-permute-start.2 = (bf16[32,3200]{1,0:T(8,128)(2,1)S(1)}, bf16[32,3200]{1,0:T(8,128)(2,1)S(1)}, u32[]{:S(2)}, u32[]{:S(2)}) collective-permute-start(bf16[32,3200]{1,0:T(8,128)(2,1)S(1)} %get-tuple-element.35), channel_id=1, source_target_pairs={{0,4},{1,5},{2,6},{3,7},{4,0},{5,1},{6,2},{7,3},{8,12},{9,13},{10,... | collective-permute-start | bytes 614408 | tf_op jit(solution)/shard_map/ppermute | solution.py:377
  12.7 17.7 %collective-permute-start.3 = (bf16[32,3200]{1,0:T(8,128)(2,1)S(1)}, bf16[32,3200]{1,0:T(8,128)(2,1)S(1)}, u32[]{:S(2)}, u32[]{:S(2)}) collective-permute-start(bf16[32,3200]{1,0:T(8,128)(2,1)S(1)} %get-tuple-element.36), channel_id=1, source_target_pairs={{0,6},{1,7},{2,4},{3,5},{4,2},{5,3},{6,0},{7,1},{8,14},{9,15},{10,... | collective-permute-start | bytes 614408 | tf_op jit(solution)/shard_map/ppermute | solution.py:377
  16.9 12.2 %collective-permute-start.6 = (bf16[16,3200]{1,0:T(8,128)(2,1)S(1)}, bf16[16,3200]{1,0:T(8,128)(2,1)S(1)}, u32[]{:S(2)}, u32[]{:S(2)}) collective-permute-start(bf16[16,3200]{1,0:T(8,128)(2,1)S(1)} %get-tuple-element.39), channel_id=1, source_target_pairs={{0,12},{1,13},{2,14},{3,15},{4,8},{5,9},{6,10},{7,11},{8,4},{9,5},... | collective-permute-start | bytes 307208 | tf_op jit(solution)/shard_map/ppermute | solution.py:377
  20.7 9.5 %collective-permute-start.7 = (bf16[16,3200]{1,0:T(8,128)(2,1)S(1)}, bf16[16,3200]{1,0:T(8,128)(2,1)S(1)}, u32[]{:S(2)}, u32[]{:S(2)}) collective-permute-start(bf16[16,3200]{1,0:T(8,128)(2,1)S(1)} %get-tuple-element.40), channel_id=1, source_target_pairs={{0,14},{1,15},{2,12},{3,13},{4,10},{5,11},{6,8},{7,9},{8,6},{9,7},... | collective-permute-start | bytes 307208 | tf_op jit(solution)/shard_map/ppermute | solution.py:377
  33.2 5.8 %collective-permute-start.8 = (bf16[16,3200]{1,0:T(8,128)(2,1)S(1)}, bf16[16,3200]{1,0:T(8,128)(2,1)S(1)}, u32[]{:S(2)}, u32[]{:S(2)}) collective-permute-start(bf16[16,3200]{1,0:T(8,128)(2,1)S(1)} %get-tuple-element.42), channel_id=1, source_target_pairs={{0,2},{1,3},{2,0},{3,1},{4,6},{5,7},{6,4},{7,5},{8,10},{9,11},{10,... | collective-permute-start | bytes 307208 | tf_op jit(solution)/shard_map/ppermute | solution.py:377
  34.6 4.7 %collective-permute-start.9 = (bf16[16,3200]{1,0:T(8,128)(2,1)S(1)}, bf16[16,3200]{1,0:T(8,128)(2,1)S(1)}, u32[]{:S(2)}, u32[]{:S(2)}) collective-permute-start(bf16[16,3200]{1,0:T(8,128)(2,1)S(1)} %get-tuple-element.43), channel_id=1, source_target_pairs={{0,4},{1,5},{2,6},{3,7},{4,0},{5,1},{6,2},{7,3},{8,12},{9,13},{10,... | collective-permute-start | bytes 307208 | tf_op jit(solution)/shard_map/ppermute | solution.py:377
  34.6 5.9 %collective-permute-start.10 = (bf16[16,3200]{1,0:T(8,128)(2,1)S(1)}, bf16[16,3200]{1,0:T(8,128)(2,1)S(1)}, u32[]{:S(2)}, u32[]{:S(2)}) collective-permute-start(bf16[16,3200]{1,0:T(8,128)(2,1)S(1)} %get-tuple-element.44), channel_id=1, source_target_pairs={{0,6},{1,7},{2,4},{3,5},{4,2},{5,3},{6,0},{7,1},{8,14},{9,15},{10,... | collective-permute-start | bytes 307208 | tf_op jit(solution)/shard_map/ppermute | solution.py:377
  36.8 3.7 %collective-permute-start.11 = (bf16[16,3200]{1,0:T(8,128)(2,1)S(1)}, bf16[16,3200]{1,0:T(8,128)(2,1)S(1)}, u32[]{:S(2)}, u32[]{:S(2)}) collective-permute-start(bf16[16,3200]{1,0:T(8,128)(2,1)S(1)} %get-tuple-element.41.refs_0_), channel_id=1, source_target_pairs={{0,1},{1,0},{2,3},{3,2},{4,5},{5,4},{6,7},{7,6},{8,9},{9,8},{10,11... | collective-permute-start | bytes 307208 | tf_op jit(solution)/shard_map/ppermute | solution.py:377
  39.1 1.5 %collective-permute-start.12 = (bf16[16,3200]{1,0:T(8,128)(2,1)S(1)}, bf16[16,3200]{1,0:T(8,128)(2,1)S(1)}, u32[]{:S(2)}, u32[]{:S(2)}) collective-permute-start(bf16[16,3200]{1,0:T(8,128)(2,1)S(1)} %collective-permute-done.8.refs_1_), channel_id=1, source_target_pairs={{0,1},{1,0},{2,3},{3,2},{4,5},{5,4},{6,7},{7,6},{8,9},{9,8},{10,11... | collective-permute-start | bytes 307208 | tf_op jit(solution)/shard_map/ppermute | solution.py:377
  39.3 1.3 %collective-permute-start.13 = (bf16[16,3200]{1,0:T(8,128)(2,1)S(1)}, bf16[16,3200]{1,0:T(8,128)(2,1)S(1)}, u32[]{:S(2)}, u32[]{:S(2)}) collective-permute-start(bf16[16,3200]{1,0:T(8,128)(2,1)S(1)} %collective-permute-done.9.refs_2_), channel_id=1, source_target_pairs={{0,1},{1,0},{2,3},{3,2},{4,5},{5,4},{6,7},{7,6},{8,9},{9,8},{10,11... | collective-permute-start | bytes 307208 | tf_op jit(solution)/shard_map/ppermute | solution.py:377
  40.5 1.3 %collective-permute-start.14 = (bf16[16,3200]{1,0:T(8,128)(2,1)S(1)}, bf16[16,3200]{1,0:T(8,128)(2,1)S(1)}, u32[]{:S(2)}, u32[]{:S(2)}) collective-permute-start(bf16[16,3200]{1,0:T(8,128)(2,1)S(1)} %collective-permute-done.10.refs_3_), channel_id=1, source_target_pairs={{0,1},{1,0},{2,3},{3,2},{4,5},{5,4},{6,7},{7,6},{8,9},{9,8},{10,11... | collective-permute-start | bytes 307208 | tf_op jit(solution)/shard_map/ppermute | solution.py:377
  45.0 7.2 %collective-permute-start.15 = (bf16[32,3200]{1,0:T(8,128)(2,1)S(1)}, bf16[32,3200]{1,0:T(8,128)(2,1)S(1)}, u32[]{:S(2)}, u32[]{:S(2)}) collective-permute-start(bf16[32,3200]{1,0:T(8,128)(2,1)S(1)} %get-tuple-element.48), channel_id=1, source_target_pairs={{0,2},{1,3},{2,0},{3,1},{4,6},{5,7},{6,4},{7,5},{8,10},{9,11},{10,... | collective-permute-start | bytes 614408 | tf_op jit(solution)/shard_map/ppermute | solution.py:377
  46.4 8.0 %collective-permute-start.16 = (bf16[32,3200]{1,0:T(8,128)(2,1)S(1)}, bf16[32,3200]{1,0:T(8,128)(2,1)S(1)}, u32[]{:S(2)}, u32[]{:S(2)}) collective-permute-start(bf16[32,3200]{1,0:T(8,128)(2,1)S(1)} %get-tuple-element.49), channel_id=1, source_target_pairs={{0,4},{1,5},{2,6},{3,7},{4,0},{5,1},{6,2},{7,3},{8,12},{9,13},{10,... | collective-permute-start | bytes 614408 | tf_op jit(solution)/shard_map/ppermute | solution.py:377
  47.5 10.3 %collective-permute-start.17 = (bf16[32,3200]{1,0:T(8,128)(2,1)S(1)}, bf16[32,3200]{1,0:T(8,128)(2,1)S(1)}, u32[]{:S(2)}, u32[]{:S(2)}) collective-permute-start(bf16[32,3200]{1,0:T(8,128)(2,1)S(1)} %get-tuple-element.50), channel_id=1, source_target_pairs={{0,6},{1,7},{2,4},{3,5},{4,2},{5,3},{6,0},{7,1},{8,14},{9,15},{10,... | collective-permute-start | bytes 614408 | tf_op jit(solution)/shard_map/ppermute | solution.py:377
  61.0 8.5 %collective-permute-start.18 = (bf16[16,3200]{1,0:T(8,128)(2,1)S(1)}, bf16[16,3200]{1,0:T(8,128)(2,1)S(1)}, u32[]{:S(2)}, u32[]{:S(2)}) collective-permute-start(bf16[16,3200]{1,0:T(8,128)(2,1)S(1)} %get-tuple-element.52), channel_id=1, source_target_pairs={{0,2},{1,3},{2,0},{3,1},{4,6},{5,7},{6,4},{7,5},{8,10},{9,11},{10,... | collective-permute-start | bytes 307208 | tf_op jit(solution)/shard_map/ppermute | solution.py:377
  62.4 9.8 %collective-permute-start.19 = (bf16[16,3200]{1,0:T(8,128)(2,1)S(1)}, bf16[16,3200]{1,0:T(8,128)(2,1)S(1)}, u32[]{:S(2)}, u32[]{:S(2)}) collective-permute-start(bf16[16,3200]{1,0:T(8,128)(2,1)S(1)} %get-tuple-element.53), channel_id=1, source_target_pairs={{0,4},{1,5},{2,6},{3,7},{4,0},{5,1},{6,2},{7,3},{8,12},{9,13},{10,... | collective-permute-start | bytes 307208 | tf_op jit(solution)/shard_map/ppermute | solution.py:377
  63.5 9.9 %collective-permute-start.20 = (bf16[16,3200]{1,0:T(8,128)(2,1)S(1)}, bf16[16,3200]{1,0:T(8,128)(2,1)S(1)}, u32[]{:S(2)}, u32[]{:S(2)}) collective-permute-start(bf16[16,3200]{1,0:T(8,128)(2,1)S(1)} %get-tuple-element.54), channel_id=1, source_target_pairs={{0,6},{1,7},{2,4},{3,5},{4,2},{5,3},{6,0},{7,1},{8,14},{9,15},{10,... | collective-permute-start | bytes 307208 | tf_op jit(solution)/shard_map/ppermute | solution.py:377
  64.6 9.2 %collective-permute-start.21 = (bf16[16,3200]{1,0:T(8,128)(2,1)S(1)}, bf16[16,3200]{1,0:T(8,128)(2,1)S(1)}, u32[]{:S(2)}, u32[]{:S(2)}) collective-permute-start(bf16[16,3200]{1,0:T(8,128)(2,1)S(1)} %get-tuple-element.55), channel_id=1, source_target_pairs={{0,8},{1,9},{2,10},{3,11},{4,12},{5,13},{6,14},{7,15},{8,0},{9,1},... | collective-permute-start | bytes 307208 | tf_op jit(solution)/shard_map/ppermute | solution.py:377
  68.6 14.9 %collective-permute-start.22 = (bf16[16,3200]{1,0:T(8,128)(2,1)S(1)}, bf16[16,3200]{1,0:T(8,128)(2,1)S(1)}, u32[]{:S(2)}, u32[]{:S(2)}) collective-permute-start(bf16[16,3200]{1,0:T(8,128)(2,1)S(1)} %get-tuple-element.56), channel_id=1, source_target_pairs={{0,10},{1,11},{2,8},{3,9},{4,14},{5,15},{6,12},{7,13},{8,2},{9,3},... | collective-permute-start | bytes 307208 | tf_op jit(solution)/shard_map/ppermute | solution.py:377
  69.6 13.9 %collective-permute-start.23 = (bf16[16,3200]{1,0:T(8,128)(2,1)S(1)}, bf16[16,3200]{1,0:T(8,128)(2,1)S(1)}, u32[]{:S(2)}, u32[]{:S(2)}) collective-permute-start(bf16[16,3200]{1,0:T(8,128)(2,1)S(1)} %get-tuple-element.57), channel_id=1, source_target_pairs={{0,12},{1,13},{2,14},{3,15},{4,8},{5,9},{6,10},{7,11},{8,4},{9,5},... | collective-permute-start | bytes 307208 | tf_op jit(solution)/shard_map/ppermute | solution.py:377
  72.2 11.8 %collective-permute-start.24 = (bf16[16,3200]{1,0:T(8,128)(2,1)S(1)}, bf16[16,3200]{1,0:T(8,128)(2,1)S(1)}, u32[]{:S(2)}, u32[]{:S(2)}) collective-permute-start(bf16[16,3200]{1,0:T(8,128)(2,1)S(1)} %get-tuple-element.58), channel_id=1, source_target_pairs={{0,14},{1,15},{2,12},{3,13},{4,10},{5,11},{6,8},{7,9},{8,6},{9,7},... | collective-permute-start | bytes 307208 | tf_op jit(solution)/shard_map/ppermute | solution.py:377
  73.4 10.7 %collective-permute-start.25 = (bf16[16,3200]{1,0:T(8,128)(2,1)S(1)}, bf16[16,3200]{1,0:T(8,128)(2,1)S(1)}, u32[]{:S(2)}, u32[]{:S(2)}) collective-permute-start(bf16[16,3200]{1,0:T(8,128)(2,1)S(1)} %get-tuple-element.51.refs_0_), channel_id=1, source_target_pairs={{0,1},{1,0},{2,3},{3,2},{4,5},{5,4},{6,7},{7,6},{8,9},{9,8},{10,11... | collective-permute-start | bytes 307208 | tf_op jit(solution)/shard_map/ppermute | solution.py:377
  73.8 10.7 %collective-permute-start.26 = (bf16[16,3200]{1,0:T(8,128)(2,1)S(1)}, bf16[16,3200]{1,0:T(8,128)(2,1)S(1)}, u32[]{:S(2)}, u32[]{:S(2)}) collective-permute-start(bf16[16,3200]{1,0:T(8,128)(2,1)S(1)} %collective-permute-done.18.refs_1_), channel_id=1, source_target_pairs={{0,1},{1,0},{2,3},{3,2},{4,5},{5,4},{6,7},{7,6},{8,9},{9,8},{10,11... | collective-permute-start | bytes 307208 | tf_op jit(solution)/shard_map/ppermute | solution.py:377
  83.5 1.3 %collective-permute-start.27 = (bf16[16,3200]{1,0:T(8,128)(2,1)S(1)}, bf16[16,3200]{1,0:T(8,128)(2,1)S(1)}, u32[]{:S(2)}, u32[]{:S(2)}) collective-permute-start(bf16[16,3200]{1,0:T(8,128)(2,1)S(1)} %collective-permute-done.19.refs_2_), channel_id=1, source_target_pairs={{0,1},{1,0},{2,3},{3,2},{4,5},{5,4},{6,7},{7,6},{8,9},{9,8},{10,11... | collective-permute-start | bytes 307208 | tf_op jit(solution)/shard_map/ppermute | solution.py:377
  83.5 1.5 %collective-permute-start.28 = (bf16[16,3200]{1,0:T(8,128)(2,1)S(1)}, bf16[16,3200]{1,0:T(8,128)(2,1)S(1)}, u32[]{:S(2)}, u32[]{:S(2)}) collective-permute-start(bf16[16,3200]{1,0:T(8,128)(2,1)S(1)} %collective-permute-done.20.refs_3_), channel_id=1, source_target_pairs={{0,1},{1,0},{2,3},{3,2},{4,5},{5,4},{6,7},{7,6},{8,9},{9,8},{10,11... | collective-permute-start | bytes 307208 | tf_op jit(solution)/shard_map/ppermute | solution.py:377
  84.0 1.3 %collective-permute-start.29 = (bf16[16,3200]{1,0:T(8,128)(2,1)S(1)}, bf16[16,3200]{1,0:T(8,128)(2,1)S(1)}, u32[]{:S(2)}, u32[]{:S(2)}) collective-permute-start(bf16[16,3200]{1,0:T(8,128)(2,1)S(1)} %collective-permute-done.21.refs_4_), channel_id=1, source_target_pairs={{0,1},{1,0},{2,3},{3,2},{4,5},{5,4},{6,7},{7,6},{8,9},{9,8},{10,11... | collective-permute-start | bytes 307208 | tf_op jit(solution)/shard_map/ppermute | solution.py:377
  84.1 1.4 %collective-permute-start.30 = (bf16[16,3200]{1,0:T(8,128)(2,1)S(1)}, bf16[16,3200]{1,0:T(8,128)(2,1)S(1)}, u32[]{:S(2)}, u32[]{:S(2)}) collective-permute-start(bf16[16,3200]{1,0:T(8,128)(2,1)S(1)} %collective-permute-done.22.refs_5_), channel_id=1, source_target_pairs={{0,1},{1,0},{2,3},{3,2},{4,5},{5,4},{6,7},{7,6},{8,9},{9,8},{10,11... | collective-permute-start | bytes 307208 | tf_op jit(solution)/shard_map/ppermute | solution.py:377
  84.5 1.3 %collective-permute-start.31 = (bf16[16,3200]{1,0:T(8,128)(2,1)S(1)}, bf16[16,3200]{1,0:T(8,128)(2,1)S(1)}, u32[]{:S(2)}, u32[]{:S(2)}) collective-permute-start(bf16[16,3200]{1,0:T(8,128)(2,1)S(1)} %collective-permute-done.23.refs_6_), channel_id=1, source_target_pairs={{0,1},{1,0},{2,3},{3,2},{4,5},{5,4},{6,7},{7,6},{8,9},{9,8},{10,11... | collective-permute-start | bytes 307208 | tf_op jit(solution)/shard_map/ppermute | solution.py:377
  (9 other events, 39.5 us)

commit v2 on v0

v2 whole, which is shorter than its diff:
```python
import functools

import jax
import jax.numpy as jnp
from jax import lax
from jax.experimental import pallas as pl
from jax.experimental.pallas import tpu as pltpu
from jax.sharding import PartitionSpec as P

EPSILON = 1e-05
LANES = 128
F32 = jnp.float32
BF16 = jnp.bfloat16


def layer_norm(values, gain_vec):
    mean_val = jnp.mean(values, axis=-1, keepdims=True)
    centered = values - mean_val
    variance = jnp.mean(centered * centered, axis=-1, keepdims=True)
    return centered * jax.lax.rsqrt(variance + EPSILON) * gain_vec


def project_side(pair_tile, pair_valid, layer_index, in_gain, proj_weights, gate_weight):
    normed = layer_norm(pair_tile.astype(F32), in_gain[layer_index]).astype(BF16)
    outputs = [
        jnp.dot(normed, proj_weights[layer_index, slot], preferred_element_type=F32)
        for slot in range(4)
    ]
    weight_mask = pair_valid[..., None]
    left_side = (jax.nn.sigmoid(outputs[1]) * outputs[0] * weight_mask).astype(BF16)
    right_side = (jax.nn.sigmoid(outputs[3]) * outputs[2] * weight_mask).astype(BF16)
    gating = jax.nn.sigmoid(jnp.dot(normed, gate_weight[layer_index], preferred_element_type=F32))
    return (left_side, right_side, gating)


def finish(pair_tile, mixed_sum, gating, layer_index, out_gain, out_weight):
    normed = layer_norm(mixed_sum, out_gain[layer_index]).astype(BF16)
    update = jnp.dot(normed, out_weight[layer_index], preferred_element_type=F32)
    return (pair_tile.astype(F32) + gating * update).astype(BF16)


def pair_mask(token_mask, tile_rows, row_begin, tile_cols, col_begin):
    valid = token_mask.astype(F32)
    row_valid = lax.dynamic_slice_in_dim(valid, row_begin, tile_rows, 0)
    col_valid = lax.dynamic_slice_in_dim(valid, col_begin, tile_cols, 0)
    return row_valid[:, None] * col_valid[None, :]


def gather_body(pair_map, token_mask, in_gain, proj_weights, gate_weight, out_gain, out_weight):
    tile_rows, tile_cols = pair_map.shape[:2]
    pair_valid = pair_mask(
        token_mask,
        tile_rows,
        lax.axis_index("row") * tile_rows,
        tile_cols,
        lax.axis_index("col") * tile_cols,
    )
    left_side, right_side, gating = project_side(
        pair_map, pair_valid, 0, in_gain, proj_weights, gate_weight
    )
    block = lax.all_gather(right_side, "row", axis=0, tiled=True)
    summed = lax.psum_scatter(
        jnp.einsum("jkc,ikc->jic", block, left_side, preferred_element_type=F32).astype(BF16),
        "col",
        scatter_dimension=0,
        tiled=True,
    ).astype(F32)
    mixed = jnp.transpose(summed, (1, 0, 2))
    after_out = finish(pair_map, mixed, gating, 0, out_gain, out_weight)
    left_side, right_side, gating = project_side(
        after_out, pair_valid, 1, in_gain, proj_weights, gate_weight
    )
    block = lax.all_gather(left_side, "col", axis=1, tiled=True)
    mixed = lax.psum_scatter(
        jnp.einsum("kic,kjc->ijc", block, right_side, preferred_element_type=F32).astype(BF16),
        "row",
        scatter_dimension=0,
        tiled=True,
    ).astype(F32)
    return finish(after_out, mixed, gating, 1, out_gain, out_weight)


NEAR = 4


class Place:
    def __init__(self):
        z = lax.axis_index("row")
        col = lax.axis_index("col")
        self.z = z
        self.x = lax.div(col, 2)
        self.core = lax.rem(col, 2)
        self.half = lax.div(z, 2)
        self.group = lax.rem(z, 2) * 2 + self.x

    def channels(self, d, ch, other=False, compact=False, absolute=False):
        core = 1 - self.core if other else self.core
        group = d if absolute else jnp.bitwise_xor(self.group, d)
        begin = group * ch if compact else group * (2 * ch) + core * ch
        return pl.ds(pl.multiple_of(begin, ch), ch)


def lane_of(rows):
    return lax.broadcasted_iota(jnp.int32, (rows, LANES), 1)


def take_piece(value, index, width, lane):
    tile, offset = divmod(index * width, LANES)
    part = value[:, tile * LANES : (tile + 1) * LANES]
    if offset:
        part = pltpu.roll(part, LANES - offset, 1)
    if offset + width > LANES:
        after = value[:, (tile + 1) * LANES : (tile + 2) * LANES]
        part = jnp.where(lane < LANES - offset, part, pltpu.roll(after, LANES - offset, 1))
    return jnp.where(lane < width, part, jnp.zeros_like(part))


def join_pieces(piece, count, width, tile, lane):
    low = tile * LANES
    out = None
    for index in range(low // width, min(count, -(-(low + LANES) // width))):
        shift = index * width - low
        part, begin = piece(index)
        if (shift - begin) % LANES:
            part = pltpu.roll(part, (shift - begin) % LANES, 1)
        out = part if out is None else jnp.where(lane >= shift, part, out)
    return out


def norm_rows(values, gain_col):
    mean_val = jnp.mean(values, axis=0, keepdims=True)
    centered = values - mean_val
    variance = jnp.mean(centered * centered, axis=0, keepdims=True)
    return (centered * lax.rsqrt(variance + EPSILON) * gain_col).astype(BF16)


def turned(weight):
    return weight.astype(F32).T.astype(BF16)


def project_chunk(normed, valid, chosen, lanes):
    out = jnp.dot(chosen, normed, preferred_element_type=F32)
    half = out.shape[0] // 2
    return (jax.nn.sigmoid(out[half:]) * out[:half] * valid).astype(BF16)


def chunks_of(total, size):
    return [slice(begin, min(begin + size, total)) for begin in range(0, total, size)]


def prepare_kernel(
    pair_in,
    mask_in,
    proj_in,
    gate_in,
    weight_in,
    gain_in,
    out_gain_in,
    pair_ref,
    valid_ref,
    chosen_ref,
    gate_ref,
    weight_ref,
    gain_ref,
    out_gain_ref,
    mask_ref,
    proj_ref,
    gates_ref,
    weights_ref,
    gains_ref,
    out_gains_ref,
    turned_ref,
    sems,
):
    moves = [
        (mask_in, mask_ref),
        (proj_in, proj_ref),
        (gain_in, gains_ref),
        (out_gain_in, out_gains_ref),
        (gate_in, gates_ref),
        (weight_in, weights_ref),
        (pair_in, pair_ref),
    ]
    copies = [
        pltpu.make_async_copy(there, here, sems.at[i]) for i, (there, here) in enumerate(moves)
    ]
    for copy in copies:
        copy.start()
    place = Place()
    ch = chosen_ref.shape[1] // (4 * NEAR)
    total = valid_ref.shape[1]
    rows, cols = pair_ref.shape[:2]
    width = 2 * cols
    copies[0].wait()
    lane = lane_of(1)
    mask = mask_ref[...].astype(F32).astype(BF16)

    def lanes_from(begin):
        shape = (mask.shape[1], LANES)
        token = lax.broadcasted_iota(jnp.int32, shape, 0)
        lanes = lax.broadcasted_iota(jnp.int32, shape, 1)
        pick = jnp.where(token == lanes + begin, 1.0, 0.0).astype(BF16)
        return jnp.dot(mask, pick, preferred_element_type=F32)

    col_valid = lanes_from(place.x * width)
    row_valid = lanes_from(place.z * rows)
    for tile in range(total // LANES):
        valid_ref[:, tile * LANES : (tile + 1) * LANES] = join_pieces(
            lambda row: (col_valid * row_valid[:, row : row + 1], 0), rows, width, tile, lane
        )
    copies[1].wait()
    for layer in range(2):
        for slot in range(4):
            turned_ref[slot] = turned(proj_ref[layer, (0, 2, 1, 3)[slot]])
        for slot in range(4):
            for d in range(NEAR):
                begin = (slot * NEAR + d) * ch
                chosen_ref[layer, begin : begin + ch, :] = turned_ref[slot, place.channels(d, ch), :]
    copies[2].wait()
    copies[3].wait()
    for layer in range(2):
        for gains, ref in ((gains_ref, gain_ref), (out_gains_ref, out_gain_ref)):
            ref[layer] = jnp.broadcast_to(gains[layer : layer + 1, :], (LANES, LANES)).T
    copies[4].wait()
    copies[5].wait()
    gate_ref[0] = turned(gates_ref[0])
    weight_ref[0] = turned(weights_ref[0])
    gate_ref[1] = gates_ref[1]
    weight_ref[1] = weights_ref[1]
    copies[6].wait()


def column_of(ref, layer, lanes):
    return jnp.concatenate([ref[layer]] * (-(-lanes // LANES)), axis=1)[:, :lanes]


def chosen_rows(chosen_ref, layer, side):
    half = chosen_ref.shape[1] // 4
    values, gates = (side * half, (side + 1) * half), ((side + 2) * half, (side + 3) * half)
    return jnp.concatenate(
        [chosen_ref[layer, slice(*values), :], chosen_ref[layer, slice(*gates), :]], axis=0
    )


def first_far_kernel(
    chunk, own_ref, sibling_ref, valid_ref, gain_ref, chosen_ref, *rest
):
    far_refs = rest[:NEAR]
    turned_pair_ref, normed_ref, pair_ref = rest[NEAR:]
    place = Place()
    cols = own_ref.shape[1]
    ch = far_refs[0].shape[0]
    total = valid_ref.shape[1]
    own_at = pl.multiple_of(place.core * cols, 8)
    sibling_at = pl.multiple_of((1 - place.core) * cols, 8)
    pair_ref[:, pl.ds(own_at, cols), :] = own_ref[...].astype(F32)
    pair_ref[:, pl.ds(sibling_at, cols), :] = sibling_ref[...].astype(F32)
    gain_col = column_of(gain_ref, 0, chunk)
    flat = pair_ref[...].reshape(total, LANES)
    chosen = chosen_rows(chosen_ref, 0, 1)
    for lanes in chunks_of(total, chunk):
        pair = flat[lanes].T
        turned_pair_ref[:, lanes] = pair.astype(BF16)
        normed = norm_rows(pair, gain_col)
        normed_ref[:, lanes] = normed
        right = project_chunk(normed, valid_ref[:, lanes], chosen, lanes)
        for d in range(NEAR):
            far_refs[d][:, lanes] = right[d * ch : (d + 1) * ch]


def first_near_kernel(chunk, normed_ref, valid_ref, chosen_ref, *rest):
    far_refs, near_refs = rest[:NEAR], rest[NEAR:]
    ch = far_refs[0].shape[0]
    total = valid_ref.shape[1]
    chosen = chosen_rows(chosen_ref, 0, 0)
    for lanes in chunks_of(total, chunk):
        left = project_chunk(normed_ref[:, lanes], valid_ref[:, lanes], chosen, lanes)
        for d in range(NEAR):
            near_refs[d][:ch, lanes] = left[d * ch : (d + 1) * ch]
    for d in range(NEAR):
        near_refs[d][ch:, :] = far_refs[d][...]


def gate_rows(normed_ref, gate, gating_ref, chunk):
    for lanes in chunks_of(normed_ref.shape[1], chunk):
        gating_ref[:, lanes] = jax.nn.sigmoid(
            jnp.dot(gate, normed_ref[:, lanes], preferred_element_type=F32)
        )


def middle_kernel(chunk, *refs):
    mine, other = refs[:NEAR], refs[NEAR : 2 * NEAR]
    pair_ref, gating_ref, valid_ref, gain_ref, out_gain_ref = refs[2 * NEAR : 2 * NEAR + 5]
    chosen_ref, weight_ref = refs[2 * NEAR + 5 : 2 * NEAR + 7]
    near_refs = refs[2 * NEAR + 7 : 3 * NEAR + 7]
    after_ref, normed_ref, mixed_ref = refs[3 * NEAR + 7 :]
    place = Place()
    ch = mine[0].shape[0]
    total = valid_ref.shape[1]
    for d in range(NEAR):
        mixed_ref[place.channels(d, ch), :] = mine[d][...]
        mixed_ref[place.channels(d, ch, True), :] = other[d][...]
    weight = weight_ref[0]
    out_gain_col = column_of(out_gain_ref, 0, chunk)
    gain_col = column_of(gain_ref, 1, chunk)
    sides = [chosen_rows(chosen_ref, 1, side) for side in range(2)]
    for lanes in chunks_of(total, chunk):
        normed_out = norm_rows(mixed_ref[:, lanes].astype(F32), out_gain_col)
        update = jnp.dot(weight, normed_out, preferred_element_type=F32)
        after = (pair_ref[:, lanes].astype(F32) + gating_ref[:, lanes] * update).astype(BF16)
        after_ref[:, lanes] = after
        normed = norm_rows(after.astype(F32), gain_col)
        normed_ref[:, lanes] = normed
        for side in range(2):
            out = project_chunk(normed, valid_ref[:, lanes], sides[side], lanes)
            for d in range(NEAR):
                near_refs[d][side * ch : (side + 1) * ch, lanes] = out[d * ch : (d + 1) * ch]


def own_kernel(chunk, cols, after_ref, normed_ref, gate_ref, own_ref, gating_ref, rows_ref):
    place = Place()
    total = after_ref.shape[1]
    rows = total // (2 * cols)
    own_at = pl.multiple_of(place.core * cols, 8)
    for lanes in chunks_of(total, chunk):
        rows_ref[0, lanes, :] = after_ref[:, lanes].astype(F32).T
        rows_ref[1, lanes, :] = lax.dot_general(
            normed_ref[:, lanes],
            gate_ref[1],
            (((0,), (0,)), ((), ())),
            preferred_element_type=F32,
        )
    for row in range(rows):
        here = pl.ds(row * 2 * cols + own_at, cols)
        own_ref[row * cols : (row + 1) * cols, :] = rows_ref[0, here, :]
        gating_ref[row * cols : (row + 1) * cols, :] = jax.nn.sigmoid(rows_ref[1, here, :])


def sum_kernel(*refs):
    near, far = refs[:NEAR], refs[NEAR : 2 * NEAR]
    keep_ref, send_ref = refs[2 * NEAR :]
    place = Place()
    ch = near[0].shape[0]
    half = keep_ref.shape[1]
    begin = half // LANES * LANES
    for d in range(NEAR):
        total = near[d][...].astype(F32) + far[d][:, : 2 * half].astype(F32)
        rows = place.channels(d, ch, compact=True)
        first = total[:, :half]
        second = pltpu.roll(total[:, begin:], half, 1)[:, :half]
        keep_ref[rows, :] = jnp.where(place.core == 0, first, second).astype(BF16)
        send_ref[rows, :] = jnp.where(place.core == 0, second, first).astype(BF16)


def last_kernel(chunk, keep_ref, got_ref, own_ref, gating_ref, gain_ref, weight_ref, out_ref, mixed_ref):
    place = Place()
    ch = keep_ref.shape[0] // NEAR
    for group in range(NEAR):
        rows = slice(group * ch, (group + 1) * ch)
        mixed_ref[place.channels(group, ch, absolute=True), :] = keep_ref[rows, :]
        mixed_ref[place.channels(group, ch, True, absolute=True), :] = got_ref[rows, :]
    for lanes in chunks_of(keep_ref.shape[1], chunk):
        gain_col = column_of(gain_ref, 1, lanes.stop - lanes.start)
        normed = norm_rows(mixed_ref[:, lanes].astype(F32), gain_col)
        update = lax.dot_general(
            normed, weight_ref[1], (((0,), (0,)), ((), ())), preferred_element_type=F32
        )
        out_ref[lanes, :] = (own_ref[lanes, :] + gating_ref[lanes, :] * update).astype(BF16)


def unpack(value, ref, begin, rows, width, lane):
    ch = value.shape[0]
    for row in range(rows):
        ref[pl.ds(begin + row * ch, ch), :] = take_piece(value, row, width, lane).astype(F32)


def pack(ref, begin, out_ref, rows, width, lane):
    ch = out_ref.shape[0]
    for tile in range(rows * width // LANES):
        out_ref[:, tile * LANES : (tile + 1) * LANES] = join_pieces(
            lambda row: (ref[pl.ds(begin + row * ch, ch), :].astype(BF16), 0), rows, width, tile, lane
        )


def pack_halves(ref, begin, out_ref, rows, cols, lane):
    ch = out_ref.shape[0]
    for tile in range(out_ref.shape[1] // LANES):
        lanes = slice(tile * LANES, (tile + 1) * LANES)
        if tile * LANES >= 2 * rows * cols:
            out_ref[:, lanes] = jnp.zeros((ch, LANES), BF16)
            continue

        def piece(index):
            part = ref[pl.ds(begin + (index % rows) * ch, ch), :].astype(BF16)
            return part, index // rows * cols

        out_ref[:, lanes] = join_pieces(piece, 2 * rows, cols, tile, lane)


def channel_of(ref, c, ch, tall):
    return jnp.concatenate(
        [ref[side, pl.ds(c, tall, stride=ch), :] for side in range(2)], axis=1
    ).astype(BF16)


def widen(part):
    return jnp.pad(part, ((0, 0), (0, LANES - part.shape[1])))


def outgoing_multiply(left_ref, right_ref, mixed_ref, ch, tall):
    for c in range(ch):
        left = channel_of(left_ref, c, ch, tall)
        right = channel_of(right_ref, c, ch, tall)
        part = lax.dot_general(left, right, (((1,), (1,)), ((), ())), preferred_element_type=F32)
        mixed_ref[pl.ds(c, tall, stride=ch), :] = widen(part)


def outgoing_near_kernel(rows, width, *refs):
    near, (normed_ref, gate_ref) = refs[:NEAR], refs[NEAR : NEAR + 2]
    gating_ref, left_ref, *outs = refs[NEAR + 2 : NEAR + 6]
    right_ref, mixed_ref = refs[NEAR + 6 :]
    gate_rows(normed_ref, gate_ref[0], gating_ref, 5 * LANES)
    place = Place()
    ch = outs[0].shape[0]
    lane = lane_of(ch)
    for d in range(NEAR):
        dl, dx = divmod(d, 2)
        value = near[d][...]
        unpack(value[:ch], left_ref.at[dx], dl * rows * ch, rows, width, lane)
        low = jnp.bitwise_xor(lax.rem(place.z, 2), dl)
        begin = pl.multiple_of(low * (rows * ch), 16)
        unpack(value[ch:], right_ref.at[dx], begin, rows, width, lane)
    outgoing_multiply(left_ref, right_ref, mixed_ref, ch, 2 * rows)
    for dl in range(2):
        pack(mixed_ref, dl * rows * ch, outs[dl], rows, width, lane)


def outgoing_far_kernel(rows, width, *refs):
    far, left_ref, done = refs[:NEAR], refs[NEAR], refs[NEAR + 1 : NEAR + 3]
    outs = refs[NEAR + 3 : 2 * NEAR + 3]
    right_ref, mixed_ref = refs[2 * NEAR + 3 :]
    place = Place()
    ch = far[0].shape[0]
    lane = lane_of(ch)
    for d in range(NEAR):
        dl, dx = divmod(d, 2)
        low = jnp.bitwise_xor(lax.rem(place.z, 2), dl)
        begin = pl.multiple_of(low * (rows * ch), 16)
        unpack(far[d][...], right_ref.at[dx], begin, rows, width, lane)
    outgoing_multiply(left_ref, right_ref, mixed_ref, ch, 2 * rows)
    same = jnp.bitwise_xor(place.half, place.x)
    for dx in range(2):

        @pl.when(same == dx)
        def _(dx=dx):
            for dl in range(2):
                outs[2 * dl + dx][...] = done[dl][...]
                pack(mixed_ref, dl * rows * ch, outs[2 * dl + 1 - dx], rows, width, lane)


def incoming_kernel(rows, width, dh, *refs):
    near = refs[:NEAR]
    outs = refs[NEAR : 2 * NEAR]
    left_ref, right_ref, mixed_ref = refs[2 * NEAR :]
    place = Place()
    ch = outs[0].shape[0]
    lane = lane_of(ch)
    wanted = jnp.bitwise_xor(jnp.bitwise_xor(place.half, dh), place.x)
    for d in range(NEAR):
        dl, dx = divmod(d, 2)
        begin = dl * rows * ch
        unpack(near[d][ch:, :], right_ref.at[dx], begin, rows, width, lane)

        @pl.when(wanted == dx)
        def _(d=d, begin=begin):
            unpack(near[d][:ch, :], left_ref, begin, rows, width, lane)

    tall = 2 * rows
    for c in range(ch):
        right = channel_of(right_ref, c, ch, tall)
        left = left_ref[pl.ds(c, tall, stride=ch), :].astype(BF16)
        part = lax.dot_general(left, right, (((0,), (0,)), ((), ())), preferred_element_type=F32)
        for side in range(2):
            mixed_ref[side, pl.ds(c, width, stride=ch), :] = part[
                :width, side * LANES : (side + 1) * LANES
            ]
    for d in range(NEAR):
        dl, dx = divmod(d, 2)
        low = jnp.bitwise_xor(lax.rem(place.z, 2), dl)
        begin = pl.multiple_of(low * (rows * ch), 16)
        pack_halves(mixed_ref.at[dx], begin, outs[d], rows, width // 2, lane)


def call(kernel, micros, outs, scratch, *args, space=pltpu.VMEM):
    outs = [(out, BF16) if isinstance(out[0], int) else out for out in outs]
    if space is pltpu.HBM:
        args = [pltpu.with_memory_space_constraint(arg, space) for arg in args]
    return pl.pallas_call(
        kernel,
        out_shape=[jax.ShapeDtypeStruct(shape, dtype) for shape, dtype in outs],
        in_specs=[pl.BlockSpec(memory_space=space) for _ in args],
        out_specs=[pl.BlockSpec(memory_space=pltpu.VMEM) for _ in outs],
        scratch_shapes=[
            entry if not isinstance(entry, tuple) else pltpu.VMEM(*entry) for entry in scratch
        ],
        compiler_params=pltpu.CompilerParams(vmem_limit_bytes=24 * 2**20),
        cost_estimate=pl.CostEstimate(
            flops=int(micros * 1.1e9), bytes_accessed=0, transcendentals=0
        ),
    )(*args)


def direct_body(pair_map, token_mask, in_gain, proj_weights, gate_weight, out_gain, out_weight):
    n_row, n_col = lax.axis_size("row"), lax.axis_size("col")
    rows, cols, channels = pair_map.shape
    width = 2 * cols
    total = rows * width
    ch = channels // (2 * NEAR)
    chunk = 5 * LANES

    def swap(value, dz, dx, core=0):
        flip = dz * n_col + dx * 2 + core
        pairs = [(i, i ^ flip) for i in range(n_row * n_col)]
        return lax.ppermute(value, ("row", "col"), pairs)

    def swap_all(values, offset):
        return [
            swap(value, *divmod(d + offset, 2)) if d + offset else value
            for d, value in enumerate(values)
        ]

    sibling = swap(pair_map, 0, 0, 1)
    wide = (channels, total)
    square = (channels, channels)
    mask = token_mask.reshape(1, -1)
    own, valid, chosen, gates, weights, gains, out_gains = call(
        prepare_kernel,
        1.5,
        [
            pair_map.shape,
            ((1, total), F32),
            (2, 4 * NEAR * ch, channels),
            (2, *square),
            (2, *square),
            ((2, *square), F32),
            ((2, *square), F32),
        ],
        [
            (mask.shape, mask.dtype),
            (proj_weights.shape, BF16),
            (gate_weight.shape, BF16),
            (out_weight.shape, BF16),
            (in_gain.shape, F32),
            (out_gain.shape, F32),
            ((4, *square), BF16),
            pltpu.SemaphoreType.DMA((7,)),
        ],
        pair_map,
        mask,
        proj_weights,
        gate_weight,
        out_weight,
        in_gain,
        out_gain,
        space=pltpu.HBM,
    )
    *right, pair, normed = call(
        functools.partial(first_far_kernel, chunk),
        1.0,
        [(ch, total)] * NEAR + [wide, wide],
        [((rows, width, channels), F32)],
        own,
        sibling,
        valid,
        gains,
        chosen,
    )
    near = call(
        functools.partial(first_near_kernel, chunk),
        0.6,
        [(2 * ch, total)] * NEAR,
        [],
        normed,
        valid,
        chosen,
        *right,
    )
    far = swap_all(right, NEAR)
    near = swap_all(near, 0)
    tall = 2 * rows
    side = ((tall * ch, LANES), F32)
    sides = ((2, tall * ch, LANES), F32)
    gating, left, *mixed = call(
        functools.partial(outgoing_near_kernel, rows, width),
        2.0,
        [(wide, F32), sides] + [(ch, total)] * 2,
        [sides, side],
        *near,
        normed,
        gates,
    )
    mixed = call(
        functools.partial(outgoing_far_kernel, rows, width),
        1.2,
        [(ch, total)] * NEAR,
        [sides, side],
        *far,
        left,
        *mixed,
    )
    mixed = swap_all(mixed, 0)
    other = [swap(part, 0, 0, 1) for part in mixed]

    *near, pair, normed = call(
        functools.partial(middle_kernel, chunk),
        2.3,
        [(2 * ch, total)] * NEAR + [wide, wide],
        [(wide, BF16)],
        *mixed,
        *other,
        pair,
        gating,
        valid,
        gains,
        out_gains,
        chosen,
        weights,
    )
    near = swap_all(near, 0)
    half = rows * cols
    parts = [
        call(
            functools.partial(incoming_kernel, rows, width, dh),
            2.0,
            [(ch, total)] * NEAR,
            [side, sides, ((2, width * ch, LANES), F32)],
            *near,
        )
        for dh in range(2)
    ]
    own, gating = call(
        functools.partial(own_kernel, chunk, cols),
        2.0,
        [((half, channels), F32)] * 2,
        [((2, total, channels), F32)],
        pair,
        normed,
        gates,
    )
    mixed = swap_all(parts[0], 0) + swap_all(parts[1], NEAR)
    keep, send = call(sum_kernel, 1.0, [(NEAR * ch, half)] * 2, [], *mixed)
    got = swap(send, 0, 0, 1)
    out = call(
        functools.partial(last_kernel, chunk),
        1.0,
        [(half, channels)],
        [((channels, half), BF16)],
        keep,
        got,
        own,
        gating,
        out_gains,
        weights,
    )[0]
    return out.reshape(rows, cols, channels)


def solution(mesh):
    in_specs = (P(("groups", "row"), "col", None), P("groups"), P(), P(), P(), P(), P())
    out_specs = P(("groups", "row"), "col", None)
    direct = mesh.shape["row"] == 4 and mesh.shape["col"] == 4
    body = direct_body if direct else gather_body
    return jax.shard_map(body, mesh=mesh, in_specs=in_specs, out_specs=out_specs, check_vma=False)
```

time: 191 us -> 83.5 us (0.44)
  waiting for transfers between devices: 118 us -> 35.2 us
  starting transfers between devices: 0.31 us -> 32.2 us
  local copies, waits for them, and re-layouts: 26.3 us -> 0 us
  matrix products: 20.7 us -> 0 us
  Pallas kernels: 0 us -> 15.8 us
  between operations: 13.4 us -> 0.14 us
  other arithmetic: 11.8 us -> 0 us
    reduce_scatter x2 -> x0, waiting for transfers between devices: 62.9 us -> none  [the longest x1 36.1 us: body(): lax.psum_scatter(jnp.einsum('kic,kjc->ijc', block, right_side, preferred_...]
    all_gather x2 -> x0, waiting for transfers between devices: 54.7 us -> none  [the longest x1 37.4 us: body(): right_panel = lax.all_gather(right_side, 'row', axis=0, tiled=True)]
    ppermute x0 -> x26, waiting for transfers between devices: none -> 35.2 us  [swap(): return lax.ppermute(value, ('row', 'col'), pairs)]
    ppermute x0 -> x26, starting transfers between devices: none -> 32.2 us  [swap(): return lax.ppermute(value, ('row', 'col'), pairs)]
    dot_general x14 -> x0, matrix products: 20.7 us -> none  [the longest x8 7.05 us: project_side(): jnp.dot(normed, proj_weights[layer_index, slot], preferred_element_type=j...]
    pallas_call x0 -> x11, Pallas kernels: none -> 15.8 us  [call(): pl.pallas_call(kernel, out_shape=[jax.ShapeDtypeStruct(shape, dtype) for...]
    convert_element_type x4 -> x0, local copies, waits for them, and re-layouts: 12.8 us -> none  [the longest x1 5.18 us: body(): jnp.einsum('kic,kjc->ijc', block, right_side, preferred_element_type=jnp....]
    all_gather x2 -> x0, local copies, waits for them, and re-layouts: 12.3 us -> none  [the longest x1 8.66 us: body(): right_panel = lax.all_gather(right_side, 'row', axis=0, tiled=True)]
  transfers between devices with their start and end apart: 4 -> 26, of which waited for: 4 -> 16; matrix products, arithmetic and copies ran while one was open for 4% -> 0% of each run, Pallas kernels for 0% -> 8%
where the time goes in v2:
time: 83.5 us; the launch traced here: 83.3 us
  waiting for transfers between devices  35.2 us (42%)
  starting transfers between devices  32.2 us (39%)
  Pallas kernels  15.8 us (19%)
    ppermute x26, waiting for transfers between devices, swap(): return lax.ppermute(value, ('row', 'col'), pairs)  35.2 us
    ppermute x26, starting transfers between devices, swap(): return lax.ppermute(value, ('row', 'col'), pairs)  32.2 us
    pallas_call x11, Pallas kernels, call(): pl.pallas_call(kernel, out_shape=[jax.ShapeDtypeStruct(shape, dtype) for...  15.8 us
  transfers between devices with their start and end apart: 26, of which 16 were waited for; matrix products, arithmetic and copies ran while one was open for 0% of the time, Pallas kernels for 8%

profile of v2, /device:TPU:0, one launch (start us, length us, event | category | flops | bytes accessed | tf_op | source)
XLA Modules:
  0.0 83.3 jit_solution(12952408620646514237)
XLA Ops:
  0.5 1.5 %shard_map.73 = (bf16[40,40,128]{2,1,0:T(8,128)(2,1)S(1)}, f32[1,3200]{1,0:T(1,128)S(1)}, bf16[2,256,128]{2,1,0:T(8,128)(2,1)S(1)}, bf16[2,128,128]{2,1,0:T(8,12...) custom-call(bf16[40,40,128]{2,1,0:T(8,128)(2,1)} %pair_in.1, ...), custom_call_target="tpu_custom_call" | custom-call | flops 1650000000 | tf_op jit(solution)/shard_map/pallas_call | solution.py:498
  3.6 2.9 %collective-permute-start.5 = (bf16[32,3200]{1,0:T(8,128)(2,1)S(1)}, bf16[32,3200]{1,0:T(8,128)(2,1)S(1)}, u32[]{:S(2)}, u32[]{:S(2)}) collective-permute-start(bf16[32,3200]{1,0:T(8,128)(2,1)S(1)} %get-tuple-element.58), channel_id=1, source_target_pairs={{0,2},{1,3},{2,0},{3,1},{4,6},{5,7},{6,4},{7,5},{8,10},{9,11},{10,... | collective-permute-start | bytes 614408 | tf_op jit(solution)/shard_map/ppermute | solution.py:524
  6.5 1.6 %collective-permute-start.6 = (bf16[32,3200]{1,0:T(8,128)(2,1)S(1)}, bf16[32,3200]{1,0:T(8,128)(2,1)S(1)}, u32[]{:S(2)}, u32[]{:S(2)}) collective-permute-start(bf16[32,3200]{1,0:T(8,128)(2,1)S(1)} %get-tuple-element.59), channel_id=1, source_target_pairs={{0,4},{1,5},{2,6},{3,7},{4,0},{5,1},{6,2},{7,3},{8,12},{9,13},{10,... | collective-permute-start | bytes 614408 | tf_op jit(solution)/shard_map/ppermute | solution.py:524
  8.1 3.0 %collective-permute-start.1 = (bf16[16,3200]{1,0:T(8,128)(2,1)S(1)}, bf16[16,3200]{1,0:T(8,128)(2,1)S(1)}, u32[]{:S(2)}, u32[]{:S(2)}) collective-permute-start(bf16[16,3200]{1,0:T(8,128)(2,1)S(1)} %get-tuple-element.52.rest_0_), channel_id=1, source_target_pairs={{0,8},{1,9},{2,10},{3,11},{4,12},{5,13},{6,14},{7,15},{8,0},{9,1},... | collective-permute-start | bytes 307208 | tf_op jit(solution)/shard_map/ppermute | solution.py:524
  11.1 1.3 %collective-permute-start.2 = (bf16[16,3200]{1,0:T(8,128)(2,1)S(1)}, bf16[16,3200]{1,0:T(8,128)(2,1)S(1)}, u32[]{:S(2)}, u32[]{:S(2)}) collective-permute-start(bf16[16,3200]{1,0:T(8,128)(2,1)S(1)} %get-tuple-element.53.rest_1_), channel_id=1, source_target_pairs={{0,10},{1,11},{2,8},{3,9},{4,14},{5,15},{6,12},{7,13},{8,2},{9,3},... | collective-permute-start | bytes 307208 | tf_op jit(solution)/shard_map/ppermute | solution.py:524
  12.4 3.6 %collective-permute-start.3 = (bf16[16,3200]{1,0:T(8,128)(2,1)S(1)}, bf16[16,3200]{1,0:T(8,128)(2,1)S(1)}, u32[]{:S(2)}, u32[]{:S(2)}) collective-permute-start(bf16[16,3200]{1,0:T(8,128)(2,1)S(1)} %get-tuple-element.54.rest_2_), channel_id=1, source_target_pairs={{0,12},{1,13},{2,14},{3,15},{4,8},{5,9},{6,10},{7,11},{8,4},{9,5},... | collective-permute-start | bytes 307208 | tf_op jit(solution)/shard_map/ppermute | solution.py:524
  16.0 2.9 %collective-permute-done.6.refs_2_ = bf16[32,3200]{1,0:T(8,128)(2,1)S(1)} collective-permute-done((bf16[32,3200]{1,0:T(8,128)(2,1)S(1)}, bf16[32,3200]{1,0:T(8,128)(2,1)S(1)}, u32[]{:S(2)}, u32[]{:S(2)}) %collective-permute-start.6) | collective-permute-done | bytes 204832 | tf_op jit(solution)/shard_map/ppermute | solution.py:524
  18.9 3.1 %collective-permute-start.4 = (bf16[16,3200]{1,0:T(8,128)(2,1)S(1)}, bf16[16,3200]{1,0:T(8,128)(2,1)S(1)}, u32[]{:S(2)}, u32[]{:S(2)}) collective-permute-start(bf16[16,3200]{1,0:T(8,128)(2,1)S(1)} %get-tuple-element.55.rest_3_), channel_id=1, source_target_pairs={{0,14},{1,15},{2,12},{3,13},{4,10},{5,11},{6,8},{7,9},{8,6},{9,7},... | collective-permute-start | bytes 307208 | tf_op jit(solution)/shard_map/ppermute | solution.py:524
  21.9 1.7 %shard_map.76 = (f32[128,3200]{1,0:T(8,128)S(1)}, f32[2,1280,128]{2,1,0:T(8,128)S(1)}, bf16[16,3200]{1,0:T(8,128)(2,1)S(1)}, bf16[16,3200]{1,0:T(8,128)(2,1)S(1)}) custom-call(bf16[32,3200]{1,0:T(8,128)(2,1)S(1)} %get-tuple-element.57.refs_0_, bf16[32,3200]{1,0:T(8,128)(2,1)S(1)} %collective-permute-done.5.refs_1_, ...), custom_call_target="tpu_custom_call" | custom-call | flops 2200000000 | tf_op jit(solution)/shard_map/pallas_call | solution.py:498
  23.7 3.9 %collective-permute-done.3.refs_2_ = bf16[16,3200]{1,0:T(8,128)(2,1)S(1)} collective-permute-done((bf16[16,3200]{1,0:T(8,128)(2,1)S(1)}, bf16[16,3200]{1,0:T(8,128)(2,1)S(1)}, u32[]{:S(2)}, u32[]{:S(2)}) %collective-permute-start.3) | collective-permute-done | bytes 102432 | tf_op jit(solution)/shard_map/ppermute | solution.py:524
  28.6 1.4 %shard_map.77 = (bf16[16,3200]{1,0:T(8,128)(2,1)S(1)}, bf16[16,3200]{1,0:T(8,128)(2,1)S(1)}, bf16[16,3200]{1,0:T(8,128)(2,1)S(1)}, bf16[16,3200]{1,0:T(8,128)(2,1)S(1)}) custom-call(bf16[16,3200]{1,0:T(8,128)(2,1)S(1)} %collective-permute-done.1.refs_0_, bf16[16,3200]{1,0:T(8,128)(2,1)S(1)} %collective-permute-done.2.refs_1_, ...), custom_call_target="tpu_custom_call" | custom-call | flops 1320000000 | tf_op jit(solution)/shard_map/pallas_call | solution.py:498
  30.0 1.6 %collective-permute-start.8 = (bf16[16,3200]{1,0:T(8,128)(2,1)S(1)}, bf16[16,3200]{1,0:T(8,128)(2,1)S(1)}, u32[]{:S(2)}, u32[]{:S(2)}) collective-permute-start(bf16[16,3200]{1,0:T(8,128)(2,1)S(1)} %get-tuple-element.66), channel_id=1, source_target_pairs={{0,2},{1,3},{2,0},{3,1},{4,6},{5,7},{6,4},{7,5},{8,10},{9,11},{10,... | collective-permute-start | bytes 307208 | tf_op jit(solution)/shard_map/ppermute | solution.py:524
  31.6 1.9 %collective-permute-start.9 = (bf16[16,3200]{1,0:T(8,128)(2,1)S(1)}, bf16[16,3200]{1,0:T(8,128)(2,1)S(1)}, u32[]{:S(2)}, u32[]{:S(2)}) collective-permute-start(bf16[16,3200]{1,0:T(8,128)(2,1)S(1)} %get-tuple-element.67), channel_id=1, source_target_pairs={{0,4},{1,5},{2,6},{3,7},{4,0},{5,1},{6,2},{7,3},{8,12},{9,13},{10,... | collective-permute-start | bytes 307208 | tf_op jit(solution)/shard_map/ppermute | solution.py:524
  34.7 1.9 %collective-permute-done.9.refs_2_ = bf16[16,3200]{1,0:T(8,128)(2,1)S(1)} collective-permute-done((bf16[16,3200]{1,0:T(8,128)(2,1)S(1)}, bf16[16,3200]{1,0:T(8,128)(2,1)S(1)}, u32[]{:S(2)}, u32[]{:S(2)}) %collective-permute-start.9) | collective-permute-done | bytes 102432 | tf_op jit(solution)/shard_map/ppermute | solution.py:524
  36.6 2.4 %collective-permute-done.10.refs_3_ = bf16[16,3200]{1,0:T(8,128)(2,1)S(1)} collective-permute-done((bf16[16,3200]{1,0:T(8,128)(2,1)S(1)}, bf16[16,3200]{1,0:T(8,128)(2,1)S(1)}, u32[]{:S(2)}, u32[]{:S(2)}) %collective-permute-start.10) | collective-permute-done | bytes 102432 | tf_op jit(solution)/shard_map/ppermute | solution.py:524
  39.0 1.3 %collective-permute-done.14.refs_7_ = bf16[16,3200]{1,0:T(8,128)(2,1)S(1)} collective-permute-done((bf16[16,3200]{1,0:T(8,128)(2,1)S(1)}, bf16[16,3200]{1,0:T(8,128)(2,1)S(1)}, u32[]{:S(2)}, u32[]{:S(2)}) %collective-permute-start.14) | collective-permute-done | bytes 102432 | tf_op jit(solution)/shard_map/ppermute | solution.py:524
  40.3 2.3 %shard_map.78 = (bf16[32,3200]{1,0:T(8,128)(2,1)S(1)}, bf16[32,3200]{1,0:T(8,128)(2,1)S(1)}, bf16[32,3200]{1,0:T(8,128)(2,1)S(1)}, bf16[32,3200]{1,0:T(8,128)(2,...) custom-call(bf16[16,3200]{1,0:T(8,128)(2,1)S(1)} %get-tuple-element.65.refs_0_, ...), custom_call_target="tpu_custom_call" | custom-call | flops 2529999872 | tf_op jit(solution)/shard_map/pallas_call | solution.py:498
  44.5 1.7 %collective-permute-start.17 = (bf16[32,3200]{1,0:T(8,128)(2,1)S(1)}, bf16[32,3200]{1,0:T(8,128)(2,1)S(1)}, u32[]{:S(2)}, u32[]{:S(2)}) collective-permute-start(bf16[32,3200]{1,0:T(8,128)(2,1)S(1)} %get-tuple-element.76), channel_id=1, source_target_pairs={{0,6},{1,7},{2,4},{3,5},{4,2},{5,3},{6,0},{7,1},{8,14},{9,15},{10,... | collective-permute-start | bytes 614408 | tf_op jit(solution)/shard_map/ppermute | solution.py:524
  46.1 3.7 %collective-permute-done.15.refs_1_ = bf16[32,3200]{1,0:T(8,128)(2,1)S(1)} collective-permute-done((bf16[32,3200]{1,0:T(8,128)(2,1)S(1)}, bf16[32,3200]{1,0:T(8,128)(2,1)S(1)}, u32[]{:S(2)}, u32[]{:S(2)}) %collective-permute-start.15) | collective-permute-done | bytes 204832 | tf_op jit(solution)/shard_map/ppermute | solution.py:524
  49.8 1.8 %collective-permute-done.16.refs_2_ = bf16[32,3200]{1,0:T(8,128)(2,1)S(1)} collective-permute-done((bf16[32,3200]{1,0:T(8,128)(2,1)S(1)}, bf16[32,3200]{1,0:T(8,128)(2,1)S(1)}, u32[]{:S(2)}, u32[]{:S(2)}) %collective-permute-start.16) | collective-permute-done | bytes 204832 | tf_op jit(solution)/shard_map/ppermute | solution.py:524
  51.6 3.7 %collective-permute-done.17.refs_3_ = bf16[32,3200]{1,0:T(8,128)(2,1)S(1)} collective-permute-done((bf16[32,3200]{1,0:T(8,128)(2,1)S(1)}, bf16[32,3200]{1,0:T(8,128)(2,1)S(1)}, u32[]{:S(2)}, u32[]{:S(2)}) %collective-permute-start.17) | collective-permute-done | bytes 204832 | tf_op jit(solution)/shard_map/ppermute | solution.py:524
  55.4 2.3 %shard_map.80 = (bf16[16,3200]{1,0:T(8,128)(2,1)S(1)}, bf16[16,3200]{1,0:T(8,128)(2,1)S(1)}, bf16[16,3200]{1,0:T(8,128)(2,1)S(1)}, bf16[16,3200]{1,0:T(8,128)(2,1)S(1)}) custom-call(bf16[32,3200]{1,0:T(8,128)(2,1)S(1)} %get-tuple-element.73.refs_0_, bf16[32,3200]{1,0:T(8,128)(2,1)S(1)} %collective-permute-done.15.refs_1_, ...), custom_call_target="tpu_custom_call" | custom-call | flops 2200000000 | tf_op jit(solution)/shard_map/pallas_call | solution.py:498
  57.7 2.3 %collective-permute-start.21 = (bf16[16,3200]{1,0:T(8,128)(2,1)S(1)}, bf16[16,3200]{1,0:T(8,128)(2,1)S(1)}, u32[]{:S(2)}, u32[]{:S(2)}) collective-permute-start(bf16[16,3200]{1,0:T(8,128)(2,1)S(1)} %get-tuple-element.81), channel_id=1, source_target_pairs={{0,8},{1,9},{2,10},{3,11},{4,12},{5,13},{6,14},{7,15},{8,0},{9,1},... | collective-permute-start | bytes 307208 | tf_op jit(solution)/shard_map/ppermute | solution.py:524
  61.1 3.1 %collective-permute-start.23 = (bf16[16,3200]{1,0:T(8,128)(2,1)S(1)}, bf16[16,3200]{1,0:T(8,128)(2,1)S(1)}, u32[]{:S(2)}, u32[]{:S(2)}) collective-permute-start(bf16[16,3200]{1,0:T(8,128)(2,1)S(1)} %get-tuple-element.83), channel_id=1, source_target_pairs={{0,12},{1,13},{2,14},{3,15},{4,8},{5,9},{6,10},{7,11},{8,4},{9,5},... | collective-permute-start | bytes 307208 | tf_op jit(solution)/shard_map/ppermute | solution.py:524
  64.2 1.2 %collective-permute-start.24 = (bf16[16,3200]{1,0:T(8,128)(2,1)S(1)}, bf16[16,3200]{1,0:T(8,128)(2,1)S(1)}, u32[]{:S(2)}, u32[]{:S(2)}) collective-permute-start(bf16[16,3200]{1,0:T(8,128)(2,1)S(1)} %get-tuple-element.84), channel_id=1, source_target_pairs={{0,14},{1,15},{2,12},{3,13},{4,10},{5,11},{6,8},{7,9},{8,6},{9,7},... | collective-permute-start | bytes 307208 | tf_op jit(solution)/shard_map/ppermute | solution.py:524
  65.4 2.5 %shard_map.79 = (bf16[16,3200]{1,0:T(8,128)(2,1)S(1)}, bf16[16,3200]{1,0:T(8,128)(2,1)S(1)}, bf16[16,3200]{1,0:T(8,128)(2,1)S(1)}, bf16[16,3200]{1,0:T(8,128)(2,1)S(1)}) custom-call(bf16[32,3200]{1,0:T(8,128)(2,1)S(1)} %get-tuple-element.73.refs_0_, bf16[32,3200]{1,0:T(8,128)(2,1)S(1)} %collective-permute-done.15.refs_1_, ...), custom_call_target="tpu_custom_call" | custom-call | flops 2200000000 | tf_op jit(solution)/shard_map/pallas_call | solution.py:498
  69.0 3.2 %collective-permute-done.21.refs_4_ = bf16[16,3200]{1,0:T(8,128)(2,1)S(1)} collective-permute-done((bf16[16,3200]{1,0:T(8,128)(2,1)S(1)}, bf16[16,3200]{1,0:T(8,128)(2,1)S(1)}, u32[]{:S(2)}, u32[]{:S(2)}) %collective-permute-start.21) | collective-permute-done | bytes 102432 | tf_op jit(solution)/shard_map/ppermute | solution.py:524
  72.2 2.6 %collective-permute-done.22.refs_5_ = bf16[16,3200]{1,0:T(8,128)(2,1)S(1)} collective-permute-done((bf16[16,3200]{1,0:T(8,128)(2,1)S(1)}, bf16[16,3200]{1,0:T(8,128)(2,1)S(1)}, u32[]{:S(2)}, u32[]{:S(2)}) %collective-permute-start.22) | collective-permute-done | bytes 102432 | tf_op jit(solution)/shard_map/ppermute | solution.py:524
  74.8 2.8 %collective-permute-done.19.refs_2_ = bf16[16,3200]{1,0:T(8,128)(2,1)S(1)} collective-permute-done((bf16[16,3200]{1,0:T(8,128)(2,1)S(1)}, bf16[16,3200]{1,0:T(8,128)(2,1)S(1)}, u32[]{:S(2)}, u32[]{:S(2)}) %collective-permute-start.19) | collective-permute-done | bytes 102432 | tf_op jit(solution)/shard_map/ppermute | solution.py:524
  77.7 2.7 %collective-permute-done.20.refs_3_ = bf16[16,3200]{1,0:T(8,128)(2,1)S(1)} collective-permute-done((bf16[16,3200]{1,0:T(8,128)(2,1)S(1)}, bf16[16,3200]{1,0:T(8,128)(2,1)S(1)}, u32[]{:S(2)}, u32[]{:S(2)}) %collective-permute-start.20) | collective-permute-done | bytes 102432 | tf_op jit(solution)/shard_map/ppermute | solution.py:524
  80.6 1.2 %shard_map.82 = (f32[1600,128]{1,0:T(8,128)S(1)}, f32[1600,128]{1,0:T(8,128)S(1)}) custom-call(bf16[128,3200]{1,0:T(8,128)(2,1)S(1)} %get-tuple-element.87.after_ref, bf16[128,3200]{1,0:T(8,128)(2,1)S(1)} %get-tuple-element.88.normed_ref, bf16[2,128,128]{2,1,0:T(8,128)(2,1)S(1)} %get-tuple-element.61.refs_5_.gate_ref), custom_call_target="tpu_custom_call" | custom-call | flops 2200000000 | tf_op jit(solution)/shard_map/pallas_call | solution.py:498
  82.1 1.3 %shard_map.83 = bf16[1600,128]{1,0:T(8,128)(2,1)} custom-call(bf16[64,1600]{1,0:T(8,128)(2,1)S(1)} %get-tuple-element.85.keep_ref, bf16[64,1600]{1,0:T(8,128)(2,1)S(1)} %collective-permute-done.25.got_ref, f32[1600,128]{1,0:T(8,128)S(1)} %get-tuple-element.89.own_ref, f32[1600,128]{1,0:T(8,128)S(1)} %get-tuple-element.90.gating_ref, ...), custom_call_target="tpu_custom_call" | custom-call | flops 1100000000 | tf_op jit(solution)/shard_map/pallas_call | solution.py:498
  (31 shorter events, 9.1 us)
Async XLA Ops:
  0.0 2.0 %collective-permute-start = (bf16[40,40,128]{2,1,0:T(8,128)(2,1)}, bf16[40,40,128]{2,1,0:T(8,128)(2,1)S(1)}, u32[]{:S(2)}, u32[]{:S(2)}) collective-permute-start(bf16[40,40,128]{2,1,0:T(8,128)(2,1)} %pair_in.1), channel_id=1, source_target_pairs={{0,1},{1,0},{2,3},{3,2},{4,5},{5,4},{6,7},{7,6},{8,9},{9,8},{10,11... | collective-permute-start | bytes 1228808 | tf_op jit(solution)/shard_map/ppermute | solution.py:524
  3.6 8.8 %collective-permute-start.5 = (bf16[32,3200]{1,0:T(8,128)(2,1)S(1)}, bf16[32,3200]{1,0:T(8,128)(2,1)S(1)}, u32[]{:S(2)}, u32[]{:S(2)}) collective-permute-start(bf16[32,3200]{1,0:T(8,128)(2,1)S(1)} %get-tuple-element.58), channel_id=1, source_target_pairs={{0,2},{1,3},{2,0},{3,1},{4,6},{5,7},{6,4},{7,5},{8,10},{9,11},{10,... | collective-permute-start | bytes 614408 | tf_op jit(solution)/shard_map/ppermute | solution.py:524
  6.5 12.3 %collective-permute-start.6 = (bf16[32,3200]{1,0:T(8,128)(2,1)S(1)}, bf16[32,3200]{1,0:T(8,128)(2,1)S(1)}, u32[]{:S(2)}, u32[]{:S(2)}) collective-permute-start(bf16[32,3200]{1,0:T(8,128)(2,1)S(1)} %get-tuple-element.59), channel_id=1, source_target_pairs={{0,4},{1,5},{2,6},{3,7},{4,0},{5,1},{6,2},{7,3},{8,12},{9,13},{10,... | collective-permute-start | bytes 614408 | tf_op jit(solution)/shard_map/ppermute | solution.py:524
  8.1 13.8 %collective-permute-start.7 = (bf16[32,3200]{1,0:T(8,128)(2,1)S(1)}, bf16[32,3200]{1,0:T(8,128)(2,1)S(1)}, u32[]{:S(2)}, u32[]{:S(2)}) collective-permute-start(bf16[32,3200]{1,0:T(8,128)(2,1)S(1)} %get-tuple-element.60), channel_id=1, source_target_pairs={{0,6},{1,7},{2,4},{3,5},{4,2},{5,3},{6,0},{7,1},{8,14},{9,15},{10,... | collective-permute-start | bytes 614408 | tf_op jit(solution)/shard_map/ppermute | solution.py:524
  8.1 15.6 %collective-permute-start.1 = (bf16[16,3200]{1,0:T(8,128)(2,1)S(1)}, bf16[16,3200]{1,0:T(8,128)(2,1)S(1)}, u32[]{:S(2)}, u32[]{:S(2)}) collective-permute-start(bf16[16,3200]{1,0:T(8,128)(2,1)S(1)} %get-tuple-element.52.rest_0_), channel_id=1, source_target_pairs={{0,8},{1,9},{2,10},{3,11},{4,12},{5,13},{6,14},{7,15},{8,0},{9,1},... | collective-permute-start | bytes 307208 | tf_op jit(solution)/shard_map/ppermute | solution.py:524
  11.1 12.6 %collective-permute-start.2 = (bf16[16,3200]{1,0:T(8,128)(2,1)S(1)}, bf16[16,3200]{1,0:T(8,128)(2,1)S(1)}, u32[]{:S(2)}, u32[]{:S(2)}) collective-permute-start(bf16[16,3200]{1,0:T(8,128)(2,1)S(1)} %get-tuple-element.53.rest_1_), channel_id=1, source_target_pairs={{0,10},{1,11},{2,8},{3,9},{4,14},{5,15},{6,12},{7,13},{8,2},{9,3},... | collective-permute-start | bytes 307208 | tf_op jit(solution)/shard_map/ppermute | solution.py:524
  12.4 15.2 %collective-permute-start.3 = (bf16[16,3200]{1,0:T(8,128)(2,1)S(1)}, bf16[16,3200]{1,0:T(8,128)(2,1)S(1)}, u32[]{:S(2)}, u32[]{:S(2)}) collective-permute-start(bf16[16,3200]{1,0:T(8,128)(2,1)S(1)} %get-tuple-element.54.rest_2_), channel_id=1, source_target_pairs={{0,12},{1,13},{2,14},{3,15},{4,8},{5,9},{6,10},{7,11},{8,4},{9,5},... | collective-permute-start | bytes 307208 | tf_op jit(solution)/shard_map/ppermute | solution.py:524
  18.9 9.8 %collective-permute-start.4 = (bf16[16,3200]{1,0:T(8,128)(2,1)S(1)}, bf16[16,3200]{1,0:T(8,128)(2,1)S(1)}, u32[]{:S(2)}, u32[]{:S(2)}) collective-permute-start(bf16[16,3200]{1,0:T(8,128)(2,1)S(1)} %get-tuple-element.55.rest_3_), channel_id=1, source_target_pairs={{0,14},{1,15},{2,12},{3,13},{4,10},{5,11},{6,8},{7,9},{8,6},{9,7},... | collective-permute-start | bytes 307208 | tf_op jit(solution)/shard_map/ppermute | solution.py:524
  30.0 4.7 %collective-permute-start.8 = (bf16[16,3200]{1,0:T(8,128)(2,1)S(1)}, bf16[16,3200]{1,0:T(8,128)(2,1)S(1)}, u32[]{:S(2)}, u32[]{:S(2)}) collective-permute-start(bf16[16,3200]{1,0:T(8,128)(2,1)S(1)} %get-tuple-element.66), channel_id=1, source_target_pairs={{0,2},{1,3},{2,0},{3,1},{4,6},{5,7},{6,4},{7,5},{8,10},{9,11},{10,... | collective-permute-start | bytes 307208 | tf_op jit(solution)/shard_map/ppermute | solution.py:524
  31.6 5.1 %collective-permute-start.9 = (bf16[16,3200]{1,0:T(8,128)(2,1)S(1)}, bf16[16,3200]{1,0:T(8,128)(2,1)S(1)}, u32[]{:S(2)}, u32[]{:S(2)}) collective-permute-start(bf16[16,3200]{1,0:T(8,128)(2,1)S(1)} %get-tuple-element.67), channel_id=1, source_target_pairs={{0,4},{1,5},{2,6},{3,7},{4,0},{5,1},{6,2},{7,3},{8,12},{9,13},{10,... | collective-permute-start | bytes 307208 | tf_op jit(solution)/shard_map/ppermute | solution.py:524
  33.4 5.6 %collective-permute-start.10 = (bf16[16,3200]{1,0:T(8,128)(2,1)S(1)}, bf16[16,3200]{1,0:T(8,128)(2,1)S(1)}, u32[]{:S(2)}, u32[]{:S(2)}) collective-permute-start(bf16[16,3200]{1,0:T(8,128)(2,1)S(1)} %get-tuple-element.68), channel_id=1, source_target_pairs={{0,6},{1,7},{2,4},{3,5},{4,2},{5,3},{6,0},{7,1},{8,14},{9,15},{10,... | collective-permute-start | bytes 307208 | tf_op jit(solution)/shard_map/ppermute | solution.py:524
  33.9 5.1 %collective-permute-start.11 = (bf16[16,3200]{1,0:T(8,128)(2,1)S(1)}, bf16[16,3200]{1,0:T(8,128)(2,1)S(1)}, u32[]{:S(2)}, u32[]{:S(2)}) collective-permute-start(bf16[16,3200]{1,0:T(8,128)(2,1)S(1)} %get-tuple-element.65.refs_0_), channel_id=1, source_target_pairs={{0,1},{1,0},{2,3},{3,2},{4,5},{5,4},{6,7},{7,6},{8,9},{9,8},{10,11... | collective-permute-start | bytes 307208 | tf_op jit(solution)/shard_map/ppermute | solution.py:524
  34.7 4.3 %collective-permute-start.12 = (bf16[16,3200]{1,0:T(8,128)(2,1)S(1)}, bf16[16,3200]{1,0:T(8,128)(2,1)S(1)}, u32[]{:S(2)}, u32[]{:S(2)}) collective-permute-start(bf16[16,3200]{1,0:T(8,128)(2,1)S(1)} %collective-permute-done.8.refs_1_), channel_id=1, source_target_pairs={{0,1},{1,0},{2,3},{3,2},{4,5},{5,4},{6,7},{7,6},{8,9},{9,8},{10,11... | collective-permute-start | bytes 307208 | tf_op jit(solution)/shard_map/ppermute | solution.py:524
  36.6 2.4 %collective-permute-start.13 = (bf16[16,3200]{1,0:T(8,128)(2,1)S(1)}, bf16[16,3200]{1,0:T(8,128)(2,1)S(1)}, u32[]{:S(2)}, u32[]{:S(2)}) collective-permute-start(bf16[16,3200]{1,0:T(8,128)(2,1)S(1)} %collective-permute-done.9.refs_2_), channel_id=1, source_target_pairs={{0,1},{1,0},{2,3},{3,2},{4,5},{5,4},{6,7},{7,6},{8,9},{9,8},{10,11... | collective-permute-start | bytes 307208 | tf_op jit(solution)/shard_map/ppermute | solution.py:524
  39.0 1.3 %collective-permute-start.14 = (bf16[16,3200]{1,0:T(8,128)(2,1)S(1)}, bf16[16,3200]{1,0:T(8,128)(2,1)S(1)}, u32[]{:S(2)}, u32[]{:S(2)}) collective-permute-start(bf16[16,3200]{1,0:T(8,128)(2,1)S(1)} %collective-permute-done.10.refs_3_), channel_id=1, source_target_pairs={{0,1},{1,0},{2,3},{3,2},{4,5},{5,4},{6,7},{7,6},{8,9},{9,8},{10,11... | collective-permute-start | bytes 307208 | tf_op jit(solution)/shard_map/ppermute | solution.py:524
  42.6 7.2 %collective-permute-start.15 = (bf16[32,3200]{1,0:T(8,128)(2,1)S(1)}, bf16[32,3200]{1,0:T(8,128)(2,1)S(1)}, u32[]{:S(2)}, u32[]{:S(2)}) collective-permute-start(bf16[32,3200]{1,0:T(8,128)(2,1)S(1)} %get-tuple-element.74), channel_id=1, source_target_pairs={{0,2},{1,3},{2,0},{3,1},{4,6},{5,7},{6,4},{7,5},{8,10},{9,11},{10,... | collective-permute-start | bytes 614408 | tf_op jit(solution)/shard_map/ppermute | solution.py:524
  43.7 8.0 %collective-permute-start.16 = (bf16[32,3200]{1,0:T(8,128)(2,1)S(1)}, bf16[32,3200]{1,0:T(8,128)(2,1)S(1)}, u32[]{:S(2)}, u32[]{:S(2)}) collective-permute-start(bf16[32,3200]{1,0:T(8,128)(2,1)S(1)} %get-tuple-element.75), channel_id=1, source_target_pairs={{0,4},{1,5},{2,6},{3,7},{4,0},{5,1},{6,2},{7,3},{8,12},{9,13},{10,... | collective-permute-start | bytes 614408 | tf_op jit(solution)/shard_map/ppermute | solution.py:524
  44.5 10.9 %collective-permute-start.17 = (bf16[32,3200]{1,0:T(8,128)(2,1)S(1)}, bf16[32,3200]{1,0:T(8,128)(2,1)S(1)}, u32[]{:S(2)}, u32[]{:S(2)}) collective-permute-start(bf16[32,3200]{1,0:T(8,128)(2,1)S(1)} %get-tuple-element.76), channel_id=1, source_target_pairs={{0,6},{1,7},{2,4},{3,5},{4,2},{5,3},{6,0},{7,1},{8,14},{9,15},{10,... | collective-permute-start | bytes 614408 | tf_op jit(solution)/shard_map/ppermute | solution.py:524
  57.7 14.5 %collective-permute-start.21 = (bf16[16,3200]{1,0:T(8,128)(2,1)S(1)}, bf16[16,3200]{1,0:T(8,128)(2,1)S(1)}, u32[]{:S(2)}, u32[]{:S(2)}) collective-permute-start(bf16[16,3200]{1,0:T(8,128)(2,1)S(1)} %get-tuple-element.81), channel_id=1, source_target_pairs={{0,8},{1,9},{2,10},{3,11},{4,12},{5,13},{6,14},{7,15},{8,0},{9,1},... | collective-permute-start | bytes 307208 | tf_op jit(solution)/shard_map/ppermute | solution.py:524
  60.0 14.8 %collective-permute-start.22 = (bf16[16,3200]{1,0:T(8,128)(2,1)S(1)}, bf16[16,3200]{1,0:T(8,128)(2,1)S(1)}, u32[]{:S(2)}, u32[]{:S(2)}) collective-permute-start(bf16[16,3200]{1,0:T(8,128)(2,1)S(1)} %get-tuple-element.82), channel_id=1, source_target_pairs={{0,10},{1,11},{2,8},{3,9},{4,14},{5,15},{6,12},{7,13},{8,2},{9,3},... | collective-permute-start | bytes 307208 | tf_op jit(solution)/shard_map/ppermute | solution.py:524
  61.1 13.7 %collective-permute-start.23 = (bf16[16,3200]{1,0:T(8,128)(2,1)S(1)}, bf16[16,3200]{1,0:T(8,128)(2,1)S(1)}, u32[]{:S(2)}, u32[]{:S(2)}) collective-permute-start(bf16[16,3200]{1,0:T(8,128)(2,1)S(1)} %get-tuple-element.83), channel_id=1, source_target_pairs={{0,12},{1,13},{2,14},{3,15},{4,8},{5,9},{6,10},{7,11},{8,4},{9,5},... | collective-permute-start | bytes 307208 | tf_op jit(solution)/shard_map/ppermute | solution.py:524
  64.2 10.6 %collective-permute-start.24 = (bf16[16,3200]{1,0:T(8,128)(2,1)S(1)}, bf16[16,3200]{1,0:T(8,128)(2,1)S(1)}, u32[]{:S(2)}, u32[]{:S(2)}) collective-permute-start(bf16[16,3200]{1,0:T(8,128)(2,1)S(1)} %get-tuple-element.84), channel_id=1, source_target_pairs={{0,14},{1,15},{2,12},{3,13},{4,10},{5,11},{6,8},{7,9},{8,6},{9,7},... | collective-permute-start | bytes 307208 | tf_op jit(solution)/shard_map/ppermute | solution.py:524
  67.9 6.9 %collective-permute-start.18 = (bf16[16,3200]{1,0:T(8,128)(2,1)S(1)}, bf16[16,3200]{1,0:T(8,128)(2,1)S(1)}, u32[]{:S(2)}, u32[]{:S(2)}) collective-permute-start(bf16[16,3200]{1,0:T(8,128)(2,1)S(1)} %get-tuple-element.78), channel_id=1, source_target_pairs={{0,2},{1,3},{2,0},{3,1},{4,6},{5,7},{6,4},{7,5},{8,10},{9,11},{10,... | collective-permute-start | bytes 307208 | tf_op jit(solution)/shard_map/ppermute | solution.py:524
  72.2 5.5 %collective-permute-start.19 = (bf16[16,3200]{1,0:T(8,128)(2,1)S(1)}, bf16[16,3200]{1,0:T(8,128)(2,1)S(1)}, u32[]{:S(2)}, u32[]{:S(2)}) collective-permute-start(bf16[16,3200]{1,0:T(8,128)(2,1)S(1)} %get-tuple-element.79), channel_id=1, source_target_pairs={{0,4},{1,5},{2,6},{3,7},{4,0},{5,1},{6,2},{7,3},{8,12},{9,13},{10,... | collective-permute-start | bytes 307208 | tf_op jit(solution)/shard_map/ppermute | solution.py:524
  74.8 5.6 %collective-permute-start.20 = (bf16[16,3200]{1,0:T(8,128)(2,1)S(1)}, bf16[16,3200]{1,0:T(8,128)(2,1)S(1)}, u32[]{:S(2)}, u32[]{:S(2)}) collective-permute-start(bf16[16,3200]{1,0:T(8,128)(2,1)S(1)} %get-tuple-element.80), channel_id=1, source_target_pairs={{0,6},{1,7},{2,4},{3,5},{4,2},{5,3},{6,0},{7,1},{8,14},{9,15},{10,... | collective-permute-start | bytes 307208 | tf_op jit(solution)/shard_map/ppermute | solution.py:524
  80.5 1.5 %collective-permute-start.25 = (bf16[64,1600]{1,0:T(8,128)(2,1)S(1)}, bf16[64,1600]{1,0:T(8,128)(2,1)S(1)}, u32[]{:S(2)}, u32[]{:S(2)}) collective-permute-start(bf16[64,1600]{1,0:T(8,128)(2,1)S(1)} %get-tuple-element.86), channel_id=1, source_target_pairs={{0,1},{1,0},{2,3},{3,2},{4,5},{5,4},{6,7},{7,6},{8,9},{9,8},{10,11... | collective-permute-start | bytes 614408 | tf_op jit(solution)/shard_map/ppermute | solution.py:524

commit v3 on v2

--- a/solution.py
+++ b/solution.py
@@ -81,6 +81,20 @@
 
 
 NEAR = 4
+RIGHT_NEAR = (0, 1, 2, 3)
+RIGHT_FAR = (0, 1, 2, 3)
+OUTGOING = (0, 3, 2, 1)
+INCOMING = (0, 2, 1, 3)
+SUMS_NEAR = (0, 3, 2, 1)
+SUMS_FAR = (1, 0, 3, 2)
+
+
+def ordered(values, order):
+    return [values[d] for d in order]
+
+
+def restored(values, order):
+    return [values[order.index(d)] for d in range(NEAR)]
 
 
 class Place:
@@ -127,21 +141,28 @@
     return out
 
 
-def norm_rows(values, gain_col):
+def norm_rows(values, gain_col, valid=None):
     mean_val = jnp.mean(values, axis=0, keepdims=True)
     centered = values - mean_val
     variance = jnp.mean(centered * centered, axis=0, keepdims=True)
-    return (centered * lax.rsqrt(variance + EPSILON) * gain_col).astype(BF16)
+    scale = lax.rsqrt(variance + EPSILON)
+    if valid is not None:
+        scale = scale * valid
+    return (centered * scale * gain_col).astype(BF16)
 
 
 def turned(weight):
     return weight.astype(F32).T.astype(BF16)
 
 
-def project_chunk(normed, valid, chosen, lanes):
+def halved(weight):
+    return (weight.astype(F32) * 0.5).astype(BF16)
+
+
+def project_chunk(normed, chosen):
     out = jnp.dot(chosen, normed, preferred_element_type=F32)
     half = out.shape[0] // 2
-    return (jax.nn.sigmoid(out[half:]) * out[:half] * valid).astype(BF16)
+    return ((jnp.tanh(out[half:]) + 1.0) * out[:half]).astype(BF16)
 
 
 def chunks_of(total, size):
@@ -211,7 +232,7 @@
     copies[1].wait()
     for layer in range(2):
         for slot in range(4):
-            turned_ref[slot] = turned(proj_ref[layer, (0, 2, 1, 3)[slot]])
+            turned_ref[slot] = halved(turned(proj_ref[layer, (0, 2, 1, 3)[slot]]))
         for slot in range(4):
             for d in range(NEAR):
                 begin = (slot * NEAR + d) * ch
@@ -223,10 +244,10 @@
             ref[layer] = jnp.broadcast_to(gains[layer : layer + 1, :], (LANES, LANES)).T
     copies[4].wait()
     copies[5].wait()
-    gate_ref[0] = turned(gates_ref[0])
-    weight_ref[0] = turned(weights_ref[0])
-    gate_ref[1] = gates_ref[1]
-    weight_ref[1] = weights_ref[1]
+    gate_ref[0] = halved(turned(gates_ref[0]))
+    weight_ref[0] = halved(turned(weights_ref[0]))
+    gate_ref[1] = halved(gates_ref[1])
+    weight_ref[1] = halved(weights_ref[1])
     copies[6].wait()
 
 
@@ -261,20 +282,20 @@
     for lanes in chunks_of(total, chunk):
         pair = flat[lanes].T
         turned_pair_ref[:, lanes] = pair.astype(BF16)
-        normed = norm_rows(pair, gain_col)
+        normed = norm_rows(pair, gain_col[:, : lanes.stop - lanes.start], valid_ref[:, lanes])
         normed_ref[:, lanes] = normed
-        right = project_chunk(normed, valid_ref[:, lanes], chosen, lanes)
+        right = project_chunk(normed, chosen)
         for d in range(NEAR):
             far_refs[d][:, lanes] = right[d * ch : (d + 1) * ch]
 
 
-def first_near_kernel(chunk, normed_ref, valid_ref, chosen_ref, *rest):
+def first_near_kernel(chunk, normed_ref, chosen_ref, *rest):
     far_refs, near_refs = rest[:NEAR], rest[NEAR:]
     ch = far_refs[0].shape[0]
-    total = valid_ref.shape[1]
+    total = normed_ref.shape[1]
     chosen = chosen_rows(chosen_ref, 0, 0)
     for lanes in chunks_of(total, chunk):
-        left = project_chunk(normed_ref[:, lanes], valid_ref[:, lanes], chosen, lanes)
+        left = project_chunk(normed_ref[:, lanes], chosen)
         for d in range(NEAR):
             near_refs[d][:ch, lanes] = left[d * ch : (d + 1) * ch]
     for d in range(NEAR):
@@ -283,13 +304,14 @@
 
 def gate_rows(normed_ref, gate, gating_ref, chunk):
     for lanes in chunks_of(normed_ref.shape[1], chunk):
-        gating_ref[:, lanes] = jax.nn.sigmoid(
+        gating_ref[:, lanes] = 1.0 + jnp.tanh(
             jnp.dot(gate, normed_ref[:, lanes], preferred_element_type=F32)
         )
 
 
 def middle_kernel(chunk, *refs):
-    mine, other = refs[:NEAR], refs[NEAR : 2 * NEAR]
+    mine = restored(refs[:NEAR], OUTGOING)
+    other = restored(refs[NEAR : 2 * NEAR], OUTGOING)
     pair_ref, gating_ref, valid_ref, gain_ref, out_gain_ref = refs[2 * NEAR : 2 * NEAR + 5]
     chosen_ref, weight_ref = refs[2 * NEAR + 5 : 2 * NEAR + 7]
     near_refs = refs[2 * NEAR + 7 : 3 * NEAR + 7]
@@ -305,14 +327,18 @@
     gain_col = column_of(gain_ref, 1, chunk)
     sides = [chosen_rows(chosen_ref, 1, side) for side in range(2)]
     for lanes in chunks_of(total, chunk):
-        normed_out = norm_rows(mixed_ref[:, lanes].astype(F32), out_gain_col)
+        normed_out = norm_rows(
+            mixed_ref[:, lanes].astype(F32), out_gain_col[:, : lanes.stop - lanes.start]
+        )
         update = jnp.dot(weight, normed_out, preferred_element_type=F32)
         after = (pair_ref[:, lanes].astype(F32) + gating_ref[:, lanes] * update).astype(BF16)
         after_ref[:, lanes] = after
-        normed = norm_rows(after.astype(F32), gain_col)
+        normed = norm_rows(
+            after.astype(F32), gain_col[:, : lanes.stop - lanes.start], valid_ref[:, lanes]
+        )
         normed_ref[:, lanes] = normed
         for side in range(2):
-            out = project_chunk(normed, valid_ref[:, lanes], sides[side], lanes)
+            out = project_chunk(normed, sides[side])
             for d in range(NEAR):
                 near_refs[d][side * ch : (side + 1) * ch, lanes] = out[d * ch : (d + 1) * ch]
 
@@ -333,11 +359,12 @@
     for row in range(rows):
         here = pl.ds(row * 2 * cols + own_at, cols)
         own_ref[row * cols : (row + 1) * cols, :] = rows_ref[0, here, :]
-        gating_ref[row * cols : (row + 1) * cols, :] = jax.nn.sigmoid(rows_ref[1, here, :])
+        gating_ref[row * cols : (row + 1) * cols, :] = 1.0 + jnp.tanh(rows_ref[1, here, :])
 
 
 def sum_kernel(*refs):
-    near, far = refs[:NEAR], refs[NEAR : 2 * NEAR]
+    near = restored(refs[:NEAR], SUMS_NEAR)
+    far = restored(refs[NEAR : 2 * NEAR], SUMS_FAR)
     keep_ref, send_ref = refs[2 * NEAR :]
     place = Place()
     ch = near[0].shape[0]
@@ -399,7 +426,7 @@
 
 def channel_of(ref, c, ch, tall):
     return jnp.concatenate(
-        [ref[side, pl.ds(c, tall, stride=ch), :] for side in range(2)], axis=1
+        [ref[side, pl.ds(c, tall, stride=ch), :] for side in range(ref.shape[0])], axis=1
     ).astype(BF16)
 
 
@@ -416,10 +443,11 @@
 
 
 def outgoing_near_kernel(rows, width, *refs):
-    near, (normed_ref, gate_ref) = refs[:NEAR], refs[NEAR : NEAR + 2]
+    near = restored(refs[:NEAR], RIGHT_NEAR)
+    normed_ref, gate_ref = refs[NEAR : NEAR + 2]
     gating_ref, left_ref, *outs = refs[NEAR + 2 : NEAR + 6]
     right_ref, mixed_ref = refs[NEAR + 6 :]
-    gate_rows(normed_ref, gate_ref[0], gating_ref, 5 * LANES)
+    gate_rows(normed_ref, gate_ref[0], gating_ref, 13 * LANES)
     place = Place()
     ch = outs[0].shape[0]
     lane = lane_of(ch)
@@ -436,7 +464,8 @@
 
 
 def outgoing_far_kernel(rows, width, *refs):
-    far, left_ref, done = refs[:NEAR], refs[NEAR], refs[NEAR + 1 : NEAR + 3]
+    far = restored(refs[:NEAR], RIGHT_FAR)
+    left_ref, done = refs[NEAR], refs[NEAR + 1 : NEAR + 3]
     outs = refs[NEAR + 3 : 2 * NEAR + 3]
     right_ref, mixed_ref = refs[2 * NEAR + 3 :]
     place = Place()
@@ -458,10 +487,9 @@
                 pack(mixed_ref, dl * rows * ch, outs[2 * dl + 1 - dx], rows, width, lane)
 
 
-def incoming_kernel(rows, width, dh, *refs):
-    near = refs[:NEAR]
-    outs = refs[NEAR : 2 * NEAR]
-    left_ref, right_ref, mixed_ref = refs[2 * NEAR :]
+def incoming_kernel(rows, width, dh, sides, *refs):
+    near, outs, scratch = restored(refs[:NEAR], INCOMING), refs[NEAR:-3], refs[-3:]
+    left_ref, right_ref, mixed_ref = scratch
     place = Place()
     ch = outs[0].shape[0]
     lane = lane_of(ch)
@@ -469,7 +497,9 @@
     for d in range(NEAR):
         dl, dx = divmod(d, 2)
         begin = dl * rows * ch
-        unpack(near[d][ch:, :], right_ref.at[dx], begin, rows, width, lane)
+        if dx in sides:
+            at = right_ref.at[sides.index(dx)]
+            unpack(near[d][ch:, :], at, begin, rows, width, lane)
 
         @pl.when(wanted == dx)
         def _(d=d, begin=begin):
@@ -480,15 +510,16 @@
         right = channel_of(right_ref, c, ch, tall)
         left = left_ref[pl.ds(c, tall, stride=ch), :].astype(BF16)
         part = lax.dot_general(left, right, (((0,), (0,)), ((), ())), preferred_element_type=F32)
-        for side in range(2):
+        for side in range(len(sides)):
             mixed_ref[side, pl.ds(c, width, stride=ch), :] = part[
                 :width, side * LANES : (side + 1) * LANES
             ]
-    for d in range(NEAR):
-        dl, dx = divmod(d, 2)
+    for dl in range(2):
         low = jnp.bitwise_xor(lax.rem(place.z, 2), dl)
         begin = pl.multiple_of(low * (rows * ch), 16)
-        pack_halves(mixed_ref.at[dx], begin, outs[d], rows, width // 2, lane)
+        for side in range(len(sides)):
+            out_ref = outs[dl * len(sides) + side]
+            pack_halves(mixed_ref.at[side], begin, out_ref, rows, width // 2, lane)
 
 
 def call(kernel, micros, outs, scratch, *args, space=pltpu.VMEM):
@@ -516,7 +547,7 @@
     width = 2 * cols
     total = rows * width
     ch = channels // (2 * NEAR)
-    chunk = 5 * LANES
+    chunk = 13 * LANES
 
     def swap(value, dz, dx, core=0):
         flip = dz * n_col + dx * 2 + core
@@ -581,7 +612,6 @@
         [(2 * ch, total)] * NEAR,
         [],
         normed,
-        valid,
         chosen,
         *right,
     )
@@ -595,7 +625,7 @@
         2.0,
         [(wide, F32), sides] + [(ch, total)] * 2,
         [sides, side],
-        *near,
+        *ordered(near, RIGHT_NEAR),
         normed,
         gates,
     )
@@ -604,7 +634,7 @@
         1.2,
         [(ch, total)] * NEAR,
         [sides, side],
-        *far,
+        *ordered(far, RIGHT_FAR),
         left,
         *mixed,
     )
@@ -616,8 +646,8 @@
         2.3,
         [(2 * ch, total)] * NEAR + [wide, wide],
         [(wide, BF16)],
-        *mixed,
-        *other,
+        *ordered(mixed, OUTGOING),
+        *ordered(other, OUTGOING),
         pair,
         gating,
         valid,
@@ -628,16 +658,22 @@
     )
     near = swap_all(near, 0)
     half = rows * cols
-    parts = [
-        call(
-            functools.partial(incoming_kernel, rows, width, dh),
+
+    def incoming(dh, sides):
+        return call(
+            functools.partial(incoming_kernel, rows, width, dh, sides),
             2.0,
-            [(ch, total)] * NEAR,
-            [side, sides, ((2, width * ch, LANES), F32)],
-            *near,
+            [(ch, total)] * (2 * len(sides)),
+            [
+                side,
+                ((len(sides), tall * ch, LANES), F32),
+                ((len(sides), width * ch, LANES), F32),
+            ],
+            *ordered(near, INCOMING),
         )
-        for dh in range(2)
-    ]
+
+    first, second = incoming(1, (0,)), incoming(1, (1,))
+    parts = [incoming(0, (0, 1)), [first[0], second[0], first[1], second[1]]]
     own, gating = call(
         functools.partial(own_kernel, chunk, cols),
         2.0,
@@ -647,7 +683,7 @@
         normed,
         gates,
     )
-    mixed = swap_all(parts[0], 0) + swap_all(parts[1], NEAR)
+    mixed = ordered(swap_all(parts[0], 0), SUMS_NEAR) + ordered(swap_all(parts[1], NEAR), SUMS_FAR)
     keep, send = call(sum_kernel, 1.0, [(NEAR * ch, half)] * 2, [], *mixed)
     got = swap(send, 0, 0, 1)
     out = call(

time: 83.5 us -> 79.3 us (0.950)
  waiting for transfers between devices: 35.2 us -> 29.8 us
  starting transfers between devices: 32.2 us -> 33.1 us
    ppermute x26, waiting for transfers between devices: 35.2 us -> 29.8 us  [swap(): return lax.ppermute(value, ('row', 'col'), pairs)]
    ppermute x26, starting transfers between devices: 32.2 us -> 33.1 us  [swap(): return lax.ppermute(value, ('row', 'col'), pairs)]
    pallas_call x11 -> x12, Pallas kernels: 15.8 us -> 16.2 us  [call(): pl.pallas_call(kernel, out_shape=[jax.ShapeDtypeStruct(shape, dtype) for...]
  transfers between devices with their start and end apart: 26 -> 26, of which waited for: 16 -> 16; matrix products, arithmetic and copies ran while one was open for 0% -> 0% of each run, Pallas kernels for 8% -> 11%
where the time goes in v3:
time: 79.3 us; the launch traced here: 79.2 us
  starting transfers between devices  33.1 us (42%)
  waiting for transfers between devices  29.8 us (38%)
  Pallas kernels  16.2 us (20%)
    ppermute x26, starting transfers between devices, swap(): return lax.ppermute(value, ('row', 'col'), pairs)  33.1 us
    ppermute x26, waiting for transfers between devices, swap(): return lax.ppermute(value, ('row', 'col'), pairs)  29.8 us
    pallas_call x12, Pallas kernels, call(): pl.pallas_call(kernel, out_shape=[jax.ShapeDtypeStruct(shape, dtype) for...  16.2 us
  transfers between devices with their start and end apart: 26, of which 16 were waited for; matrix products, arithmetic and copies ran while one was open for 0% of the time, Pallas kernels for 11%

profile of v3, /device:TPU:0, one launch (start us, length us, event | category | flops | bytes accessed | tf_op | source)
XLA Modules:
  0.0 79.2 jit_solution(18393862053280890851)
XLA Ops:
  0.5 1.5 %shard_map.73 = (bf16[40,40,128]{2,1,0:T(8,128)(2,1)S(1)}, f32[1,3200]{1,0:T(1,128)S(1)}, bf16[2,256,128]{2,1,0:T(8,128)(2,1)S(1)}, bf16[2,128,128]{2,1,0:T(8,12...) custom-call(bf16[40,40,128]{2,1,0:T(8,128)(2,1)} %pair_in.1, ...), custom_call_target="tpu_custom_call" | custom-call | flops 1650000000 | tf_op jit(solution)/shard_map/pallas_call | solution.py:529
  2.0 1.1 %shard_map.74 = (bf16[16,3200]{1,0:T(8,128)(2,1)S(1)}, bf16[16,3200]{1,0:T(8,128)(2,1)S(1)}, bf16[16,3200]{1,0:T(8,128)(2,1)S(1)}, bf16[16,3200]{1,0:T(8,128)(2,...) custom-call(bf16[40,40,128]{2,1,0:T(8,128)(2,1)S(1)} %get-tuple-element.48.own_ref, ...), custom_call_target="tpu_custom_call" | custom-call | flops 1100000000 | tf_op jit(solution)/shard_map/pallas_call | solution.py:529
  3.6 2.9 %collective-permute-start.5 = (bf16[32,3200]{1,0:T(8,128)(2,1)S(1)}, bf16[32,3200]{1,0:T(8,128)(2,1)S(1)}, u32[]{:S(2)}, u32[]{:S(2)}) collective-permute-start(bf16[32,3200]{1,0:T(8,128)(2,1)S(1)} %get-tuple-element.58), channel_id=1, source_target_pairs={{0,2},{1,3},{2,0},{3,1},{4,6},{5,7},{6,4},{7,5},{8,10},{9,11},{10,... | collective-permute-start | bytes 614408 | tf_op jit(solution)/shard_map/ppermute | solution.py:555
  6.5 1.6 %collective-permute-start.6 = (bf16[32,3200]{1,0:T(8,128)(2,1)S(1)}, bf16[32,3200]{1,0:T(8,128)(2,1)S(1)}, u32[]{:S(2)}, u32[]{:S(2)}) collective-permute-start(bf16[32,3200]{1,0:T(8,128)(2,1)S(1)} %get-tuple-element.59), channel_id=1, source_target_pairs={{0,4},{1,5},{2,6},{3,7},{4,0},{5,1},{6,2},{7,3},{8,12},{9,13},{10,... | collective-permute-start | bytes 614408 | tf_op jit(solution)/shard_map/ppermute | solution.py:555
  8.1 3.0 %collective-permute-start.1 = (bf16[16,3200]{1,0:T(8,128)(2,1)S(1)}, bf16[16,3200]{1,0:T(8,128)(2,1)S(1)}, u32[]{:S(2)}, u32[]{:S(2)}) collective-permute-start(bf16[16,3200]{1,0:T(8,128)(2,1)S(1)} %get-tuple-element.52.rest_0_), channel_id=1, source_target_pairs={{0,8},{1,9},{2,10},{3,11},{4,12},{5,13},{6,14},{7,15},{8,0},{9,1},... | collective-permute-start | bytes 307208 | tf_op jit(solution)/shard_map/ppermute | solution.py:555
  11.1 1.3 %collective-permute-start.2 = (bf16[16,3200]{1,0:T(8,128)(2,1)S(1)}, bf16[16,3200]{1,0:T(8,128)(2,1)S(1)}, u32[]{:S(2)}, u32[]{:S(2)}) collective-permute-start(bf16[16,3200]{1,0:T(8,128)(2,1)S(1)} %get-tuple-element.53.rest_1_), channel_id=1, source_target_pairs={{0,10},{1,11},{2,8},{3,9},{4,14},{5,15},{6,12},{7,13},{8,2},{9,3},... | collective-permute-start | bytes 307208 | tf_op jit(solution)/shard_map/ppermute | solution.py:555
  12.3 3.6 %collective-permute-start.3 = (bf16[16,3200]{1,0:T(8,128)(2,1)S(1)}, bf16[16,3200]{1,0:T(8,128)(2,1)S(1)}, u32[]{:S(2)}, u32[]{:S(2)}) collective-permute-start(bf16[16,3200]{1,0:T(8,128)(2,1)S(1)} %get-tuple-element.54.rest_2_), channel_id=1, source_target_pairs={{0,12},{1,13},{2,14},{3,15},{4,8},{5,9},{6,10},{7,11},{8,4},{9,5},... | collective-permute-start | bytes 307208 | tf_op jit(solution)/shard_map/ppermute | solution.py:555
  15.9 2.9 %collective-permute-done.6.refs_2_ = bf16[32,3200]{1,0:T(8,128)(2,1)S(1)} collective-permute-done((bf16[32,3200]{1,0:T(8,128)(2,1)S(1)}, bf16[32,3200]{1,0:T(8,128)(2,1)S(1)}, u32[]{:S(2)}, u32[]{:S(2)}) %collective-permute-start.6) | collective-permute-done | bytes 204832 | tf_op jit(solution)/shard_map/ppermute | solution.py:555
  18.8 3.1 %collective-permute-start.4 = (bf16[16,3200]{1,0:T(8,128)(2,1)S(1)}, bf16[16,3200]{1,0:T(8,128)(2,1)S(1)}, u32[]{:S(2)}, u32[]{:S(2)}) collective-permute-start(bf16[16,3200]{1,0:T(8,128)(2,1)S(1)} %get-tuple-element.55.rest_3_), channel_id=1, source_target_pairs={{0,14},{1,15},{2,12},{3,13},{4,10},{5,11},{6,8},{7,9},{8,6},{9,7},... | collective-permute-start | bytes 307208 | tf_op jit(solution)/shard_map/ppermute | solution.py:555
  21.9 1.7 %shard_map.76 = (f32[128,3200]{1,0:T(8,128)S(1)}, f32[2,1280,128]{2,1,0:T(8,128)S(1)}, bf16[16,3200]{1,0:T(8,128)(2,1)S(1)}, bf16[16,3200]{1,0:T(8,128)(2,1)S(1)}) custom-call(bf16[32,3200]{1,0:T(8,128)(2,1)S(1)} %get-tuple-element.57.refs_0_, bf16[32,3200]{1,0:T(8,128)(2,1)S(1)} %collective-permute-done.5.refs_1_, ...), custom_call_target="tpu_custom_call" | custom-call | flops 2200000000 | tf_op jit(solution)/shard_map/pallas_call | solution.py:529
  23.6 3.9 %collective-permute-done.3.refs_2_ = bf16[16,3200]{1,0:T(8,128)(2,1)S(1)} collective-permute-done((bf16[16,3200]{1,0:T(8,128)(2,1)S(1)}, bf16[16,3200]{1,0:T(8,128)(2,1)S(1)}, u32[]{:S(2)}, u32[]{:S(2)}) %collective-permute-start.3) | collective-permute-done | bytes 102432 | tf_op jit(solution)/shard_map/ppermute | solution.py:555
  27.5 1.1 %collective-permute-done.4.refs_3_ = bf16[16,3200]{1,0:T(8,128)(2,1)S(1)} collective-permute-done((bf16[16,3200]{1,0:T(8,128)(2,1)S(1)}, bf16[16,3200]{1,0:T(8,128)(2,1)S(1)}, u32[]{:S(2)}, u32[]{:S(2)}) %collective-permute-start.4) | collective-permute-done | bytes 102432 | tf_op jit(solution)/shard_map/ppermute | solution.py:555
  28.6 1.4 %shard_map.77 = (bf16[16,3200]{1,0:T(8,128)(2,1)S(1)}, bf16[16,3200]{1,0:T(8,128)(2,1)S(1)}, bf16[16,3200]{1,0:T(8,128)(2,1)S(1)}, bf16[16,3200]{1,0:T(8,128)(2,1)S(1)}) custom-call(bf16[16,3200]{1,0:T(8,128)(2,1)S(1)} %collective-permute-done.1.refs_0_, bf16[16,3200]{1,0:T(8,128)(2,1)S(1)} %collective-permute-done.2.refs_1_, ...), custom_call_target="tpu_custom_call" | custom-call | flops 1320000000 | tf_op jit(solution)/shard_map/pallas_call | solution.py:529
  30.0 2.9 %collective-permute-start.8 = (bf16[16,3200]{1,0:T(8,128)(2,1)S(1)}, bf16[16,3200]{1,0:T(8,128)(2,1)S(1)}, u32[]{:S(2)}, u32[]{:S(2)}) collective-permute-start(bf16[16,3200]{1,0:T(8,128)(2,1)S(1)} %get-tuple-element.66), channel_id=1, source_target_pairs={{0,6},{1,7},{2,4},{3,5},{4,2},{5,3},{6,0},{7,1},{8,14},{9,15},{10,... | collective-permute-start | bytes 307208 | tf_op jit(solution)/shard_map/ppermute | solution.py:555
  33.9 2.4 %collective-permute-done.8.refs_1_ = bf16[16,3200]{1,0:T(8,128)(2,1)S(1)} collective-permute-done((bf16[16,3200]{1,0:T(8,128)(2,1)S(1)}, bf16[16,3200]{1,0:T(8,128)(2,1)S(1)}, u32[]{:S(2)}, u32[]{:S(2)}) %collective-permute-start.8) | collective-permute-done | bytes 102432 | tf_op jit(solution)/shard_map/ppermute | solution.py:555
  36.3 1.3 %collective-permute-done.9.refs_2_ = bf16[16,3200]{1,0:T(8,128)(2,1)S(1)} collective-permute-done((bf16[16,3200]{1,0:T(8,128)(2,1)S(1)}, bf16[16,3200]{1,0:T(8,128)(2,1)S(1)}, u32[]{:S(2)}, u32[]{:S(2)}) %collective-permute-start.9) | collective-permute-done | bytes 102432 | tf_op jit(solution)/shard_map/ppermute | solution.py:555
  39.1 2.0 %shard_map.78 = (bf16[32,3200]{1,0:T(8,128)(2,1)S(1)}, bf16[32,3200]{1,0:T(8,128)(2,1)S(1)}, bf16[32,3200]{1,0:T(8,128)(2,1)S(1)}, bf16[32,3200]{1,0:T(8,128)(2,...) custom-call(bf16[16,3200]{1,0:T(8,128)(2,1)S(1)} %get-tuple-element.65.refs_0_, ...), custom_call_target="tpu_custom_call" | custom-call | flops 2529999872 | tf_op jit(solution)/shard_map/pallas_call | solution.py:529
  41.1 1.8 %collective-permute-start.15 = (bf16[32,3200]{1,0:T(8,128)(2,1)S(1)}, bf16[32,3200]{1,0:T(8,128)(2,1)S(1)}, u32[]{:S(2)}, u32[]{:S(2)}) collective-permute-start(bf16[32,3200]{1,0:T(8,128)(2,1)S(1)} %get-tuple-element.74), channel_id=1, source_target_pairs={{0,4},{1,5},{2,6},{3,7},{4,0},{5,1},{6,2},{7,3},{8,12},{9,13},{10,... | collective-permute-start | bytes 614408 | tf_op jit(solution)/shard_map/ppermute | solution.py:555
  44.7 4.4 %collective-permute-done.15.refs_1_ = bf16[32,3200]{1,0:T(8,128)(2,1)S(1)} collective-permute-done((bf16[32,3200]{1,0:T(8,128)(2,1)S(1)}, bf16[32,3200]{1,0:T(8,128)(2,1)S(1)}, u32[]{:S(2)}, u32[]{:S(2)}) %collective-permute-start.15) | collective-permute-done | bytes 204832 | tf_op jit(solution)/shard_map/ppermute | solution.py:555
  49.1 5.1 %collective-permute-done.16.refs_2_ = bf16[32,3200]{1,0:T(8,128)(2,1)S(1)} collective-permute-done((bf16[32,3200]{1,0:T(8,128)(2,1)S(1)}, bf16[32,3200]{1,0:T(8,128)(2,1)S(1)}, u32[]{:S(2)}, u32[]{:S(2)}) %collective-permute-start.16) | collective-permute-done | bytes 204832 | tf_op jit(solution)/shard_map/ppermute | solution.py:555
  54.1 1.5 %shard_map.81 = (bf16[16,3200]{1,0:T(8,128)(2,1)S(1)}, bf16[16,3200]{1,0:T(8,128)(2,1)S(1)}) custom-call(bf16[32,3200]{1,0:T(8,128)(2,1)S(1)} %get-tuple-element.73.refs_0_, bf16[32,3200]{1,0:T(8,128)(2,1)S(1)} %collective-permute-done.15.refs_1_, bf16[32,3200]{1,0:T(8,128)(2,1)S(1)} %collective-permute-done.16.refs_2_, ...), custom_call_target="tpu_custom_call" | custom-call | flops 2200000000 | tf_op jit(solution)/shard_map/pallas_call | solution.py:529
  55.6 2.3 %collective-permute-start.22 = (bf16[16,3200]{1,0:T(8,128)(2,1)S(1)}, bf16[16,3200]{1,0:T(8,128)(2,1)S(1)}, u32[]{:S(2)}, u32[]{:S(2)}) collective-permute-start(bf16[16,3200]{1,0:T(8,128)(2,1)S(1)} %get-tuple-element.82), channel_id=1, source_target_pairs={{0,8},{1,9},{2,10},{3,11},{4,12},{5,13},{6,14},{7,15},{8,0},{9,1},... | collective-permute-start | bytes 307208 | tf_op jit(solution)/shard_map/ppermute | solution.py:555
  58.8 1.4 %shard_map.80 = (bf16[16,3200]{1,0:T(8,128)(2,1)S(1)}, bf16[16,3200]{1,0:T(8,128)(2,1)S(1)}) custom-call(bf16[32,3200]{1,0:T(8,128)(2,1)S(1)} %get-tuple-element.73.refs_0_, bf16[32,3200]{1,0:T(8,128)(2,1)S(1)} %collective-permute-done.15.refs_1_, bf16[32,3200]{1,0:T(8,128)(2,1)S(1)} %collective-permute-done.16.refs_2_, ...), custom_call_target="tpu_custom_call" | custom-call | flops 2200000000 | tf_op jit(solution)/shard_map/pallas_call | solution.py:529
  60.2 2.5 %collective-permute-start.21 = (bf16[16,3200]{1,0:T(8,128)(2,1)S(1)}, bf16[16,3200]{1,0:T(8,128)(2,1)S(1)}, u32[]{:S(2)}, u32[]{:S(2)}) collective-permute-start(bf16[16,3200]{1,0:T(8,128)(2,1)S(1)} %get-tuple-element.81), channel_id=1, source_target_pairs={{0,10},{1,11},{2,8},{3,9},{4,14},{5,15},{6,12},{7,13},{8,2},{9,3},... | collective-permute-start | bytes 307208 | tf_op jit(solution)/shard_map/ppermute | solution.py:555
  62.7 1.2 %collective-permute-start.23 = (bf16[16,3200]{1,0:T(8,128)(2,1)S(1)}, bf16[16,3200]{1,0:T(8,128)(2,1)S(1)}, u32[]{:S(2)}, u32[]{:S(2)}) collective-permute-start(bf16[16,3200]{1,0:T(8,128)(2,1)S(1)} %get-tuple-element.83), channel_id=1, source_target_pairs={{0,14},{1,15},{2,12},{3,13},{4,10},{5,11},{6,8},{7,9},{8,6},{9,7},... | collective-permute-start | bytes 307208 | tf_op jit(solution)/shard_map/ppermute | solution.py:555
  63.9 2.5 %shard_map.79 = (bf16[16,3200]{1,0:T(8,128)(2,1)S(1)}, bf16[16,3200]{1,0:T(8,128)(2,1)S(1)}, bf16[16,3200]{1,0:T(8,128)(2,1)S(1)}, bf16[16,3200]{1,0:T(8,128)(2,1)S(1)}) custom-call(bf16[32,3200]{1,0:T(8,128)(2,1)S(1)} %get-tuple-element.73.refs_0_, bf16[32,3200]{1,0:T(8,128)(2,1)S(1)} %collective-permute-done.15.refs_1_, ...), custom_call_target="tpu_custom_call" | custom-call | flops 2200000000 | tf_op jit(solution)/shard_map/pallas_call | solution.py:529
  66.5 1.3 %collective-permute-start.18 = (bf16[16,3200]{1,0:T(8,128)(2,1)S(1)}, bf16[16,3200]{1,0:T(8,128)(2,1)S(1)}, u32[]{:S(2)}, u32[]{:S(2)}) collective-permute-start(bf16[16,3200]{1,0:T(8,128)(2,1)S(1)} %get-tuple-element.78), channel_id=1, source_target_pairs={{0,6},{1,7},{2,4},{3,5},{4,2},{5,3},{6,0},{7,1},{8,14},{9,15},{10,... | collective-permute-start | bytes 307208 | tf_op jit(solution)/shard_map/ppermute | solution.py:555
  67.8 2.3 %collective-permute-done.22.refs_5_ = bf16[16,3200]{1,0:T(8,128)(2,1)S(1)} collective-permute-done((bf16[16,3200]{1,0:T(8,128)(2,1)S(1)}, bf16[16,3200]{1,0:T(8,128)(2,1)S(1)}, u32[]{:S(2)}, u32[]{:S(2)}) %collective-permute-start.22) | collective-permute-done | bytes 102432 | tf_op jit(solution)/shard_map/ppermute | solution.py:555
  71.1 3.8 %collective-permute-done.21.refs_4_ = bf16[16,3200]{1,0:T(8,128)(2,1)S(1)} collective-permute-done((bf16[16,3200]{1,0:T(8,128)(2,1)S(1)}, bf16[16,3200]{1,0:T(8,128)(2,1)S(1)}, u32[]{:S(2)}, u32[]{:S(2)}) %collective-permute-start.21) | collective-permute-done | bytes 102432 | tf_op jit(solution)/shard_map/ppermute | solution.py:555
  75.1 1.0 %collective-permute-done.19.refs_2_ = bf16[16,3200]{1,0:T(8,128)(2,1)S(1)} collective-permute-done((bf16[16,3200]{1,0:T(8,128)(2,1)S(1)}, bf16[16,3200]{1,0:T(8,128)(2,1)S(1)}, u32[]{:S(2)}, u32[]{:S(2)}) %collective-permute-start.19) | collective-permute-done | bytes 102432 | tf_op jit(solution)/shard_map/ppermute | solution.py:555
  76.5 1.3 %shard_map.83 = (f32[1600,128]{1,0:T(8,128)S(1)}, f32[1600,128]{1,0:T(8,128)S(1)}) custom-call(bf16[128,3200]{1,0:T(8,128)(2,1)S(1)} %get-tuple-element.87.after_ref, bf16[128,3200]{1,0:T(8,128)(2,1)S(1)} %get-tuple-element.88.normed_ref, bf16[2,128,128]{2,1,0:T(8,128)(2,1)S(1)} %get-tuple-element.61.refs_5_.gate_ref), custom_call_target="tpu_custom_call" | custom-call | flops 2200000000 | tf_op jit(solution)/shard_map/pallas_call | solution.py:529
  77.9 1.3 %shard_map.84 = bf16[1600,128]{1,0:T(8,128)(2,1)} custom-call(bf16[64,1600]{1,0:T(8,128)(2,1)S(1)} %get-tuple-element.85.keep_ref, bf16[64,1600]{1,0:T(8,128)(2,1)S(1)} %collective-permute-done.25.got_ref, f32[1600,128]{1,0:T(8,128)S(1)} %get-tuple-element.89.own_ref, f32[1600,128]{1,0:T(8,128)S(1)} %get-tuple-element.90.gating_ref, ...), custom_call_target="tpu_custom_call" | custom-call | flops 1100000000 | tf_op jit(solution)/shard_map/pallas_call | solution.py:529
  (32 shorter events, 7.7 us)
Async XLA Ops:
  0.0 2.0 %collective-permute-start = (bf16[40,40,128]{2,1,0:T(8,128)(2,1)}, bf16[40,40,128]{2,1,0:T(8,128)(2,1)S(1)}, u32[]{:S(2)}, u32[]{:S(2)}) collective-permute-start(bf16[40,40,128]{2,1,0:T(8,128)(2,1)} %pair_in.1), channel_id=1, source_target_pairs={{0,1},{1,0},{2,3},{3,2},{4,5},{5,4},{6,7},{7,6},{8,9},{9,8},{10,11... | collective-permute-start | bytes 1228808 | tf_op jit(solution)/shard_map/ppermute | solution.py:555
  3.6 8.8 %collective-permute-start.5 = (bf16[32,3200]{1,0:T(8,128)(2,1)S(1)}, bf16[32,3200]{1,0:T(8,128)(2,1)S(1)}, u32[]{:S(2)}, u32[]{:S(2)}) collective-permute-start(bf16[32,3200]{1,0:T(8,128)(2,1)S(1)} %get-tuple-element.58), channel_id=1, source_target_pairs={{0,2},{1,3},{2,0},{3,1},{4,6},{5,7},{6,4},{7,5},{8,10},{9,11},{10,... | collective-permute-start | bytes 614408 | tf_op jit(solution)/shard_map/ppermute | solution.py:555
  6.5 12.3 %collective-permute-start.6 = (bf16[32,3200]{1,0:T(8,128)(2,1)S(1)}, bf16[32,3200]{1,0:T(8,128)(2,1)S(1)}, u32[]{:S(2)}, u32[]{:S(2)}) collective-permute-start(bf16[32,3200]{1,0:T(8,128)(2,1)S(1)} %get-tuple-element.59), channel_id=1, source_target_pairs={{0,4},{1,5},{2,6},{3,7},{4,0},{5,1},{6,2},{7,3},{8,12},{9,13},{10,... | collective-permute-start | bytes 614408 | tf_op jit(solution)/shard_map/ppermute | solution.py:555
  8.1 13.9 %collective-permute-start.7 = (bf16[32,3200]{1,0:T(8,128)(2,1)S(1)}, bf16[32,3200]{1,0:T(8,128)(2,1)S(1)}, u32[]{:S(2)}, u32[]{:S(2)}) collective-permute-start(bf16[32,3200]{1,0:T(8,128)(2,1)S(1)} %get-tuple-element.60), channel_id=1, source_target_pairs={{0,6},{1,7},{2,4},{3,5},{4,2},{5,3},{6,0},{7,1},{8,14},{9,15},{10,... | collective-permute-start | bytes 614408 | tf_op jit(solution)/shard_map/ppermute | solution.py:555
  8.1 15.6 %collective-permute-start.1 = (bf16[16,3200]{1,0:T(8,128)(2,1)S(1)}, bf16[16,3200]{1,0:T(8,128)(2,1)S(1)}, u32[]{:S(2)}, u32[]{:S(2)}) collective-permute-start(bf16[16,3200]{1,0:T(8,128)(2,1)S(1)} %get-tuple-element.52.rest_0_), channel_id=1, source_target_pairs={{0,8},{1,9},{2,10},{3,11},{4,12},{5,13},{6,14},{7,15},{8,0},{9,1},... | collective-permute-start | bytes 307208 | tf_op jit(solution)/shard_map/ppermute | solution.py:555
  11.1 12.6 %collective-permute-start.2 = (bf16[16,3200]{1,0:T(8,128)(2,1)S(1)}, bf16[16,3200]{1,0:T(8,128)(2,1)S(1)}, u32[]{:S(2)}, u32[]{:S(2)}) collective-permute-start(bf16[16,3200]{1,0:T(8,128)(2,1)S(1)} %get-tuple-element.53.rest_1_), channel_id=1, source_target_pairs={{0,10},{1,11},{2,8},{3,9},{4,14},{5,15},{6,12},{7,13},{8,2},{9,3},... | collective-permute-start | bytes 307208 | tf_op jit(solution)/shard_map/ppermute | solution.py:555
  12.3 15.2 %collective-permute-start.3 = (bf16[16,3200]{1,0:T(8,128)(2,1)S(1)}, bf16[16,3200]{1,0:T(8,128)(2,1)S(1)}, u32[]{:S(2)}, u32[]{:S(2)}) collective-permute-start(bf16[16,3200]{1,0:T(8,128)(2,1)S(1)} %get-tuple-element.54.rest_2_), channel_id=1, source_target_pairs={{0,12},{1,13},{2,14},{3,15},{4,8},{5,9},{6,10},{7,11},{8,4},{9,5},... | collective-permute-start | bytes 307208 | tf_op jit(solution)/shard_map/ppermute | solution.py:555
  18.8 9.8 %collective-permute-start.4 = (bf16[16,3200]{1,0:T(8,128)(2,1)S(1)}, bf16[16,3200]{1,0:T(8,128)(2,1)S(1)}, u32[]{:S(2)}, u32[]{:S(2)}) collective-permute-start(bf16[16,3200]{1,0:T(8,128)(2,1)S(1)} %get-tuple-element.55.rest_3_), channel_id=1, source_target_pairs={{0,14},{1,15},{2,12},{3,13},{4,10},{5,11},{6,8},{7,9},{8,6},{9,7},... | collective-permute-start | bytes 307208 | tf_op jit(solution)/shard_map/ppermute | solution.py:555
  30.0 6.3 %collective-permute-start.8 = (bf16[16,3200]{1,0:T(8,128)(2,1)S(1)}, bf16[16,3200]{1,0:T(8,128)(2,1)S(1)}, u32[]{:S(2)}, u32[]{:S(2)}) collective-permute-start(bf16[16,3200]{1,0:T(8,128)(2,1)S(1)} %get-tuple-element.66), channel_id=1, source_target_pairs={{0,6},{1,7},{2,4},{3,5},{4,2},{5,3},{6,0},{7,1},{8,14},{9,15},{10,... | collective-permute-start | bytes 307208 | tf_op jit(solution)/shard_map/ppermute | solution.py:555
  32.8 4.8 %collective-permute-start.9 = (bf16[16,3200]{1,0:T(8,128)(2,1)S(1)}, bf16[16,3200]{1,0:T(8,128)(2,1)S(1)}, u32[]{:S(2)}, u32[]{:S(2)}) collective-permute-start(bf16[16,3200]{1,0:T(8,128)(2,1)S(1)} %get-tuple-element.67), channel_id=1, source_target_pairs={{0,4},{1,5},{2,6},{3,7},{4,0},{5,1},{6,2},{7,3},{8,12},{9,13},{10,... | collective-permute-start | bytes 307208 | tf_op jit(solution)/shard_map/ppermute | solution.py:555
  33.0 4.7 %collective-permute-start.10 = (bf16[16,3200]{1,0:T(8,128)(2,1)S(1)}, bf16[16,3200]{1,0:T(8,128)(2,1)S(1)}, u32[]{:S(2)}, u32[]{:S(2)}) collective-permute-start(bf16[16,3200]{1,0:T(8,128)(2,1)S(1)} %get-tuple-element.68), channel_id=1, source_target_pairs={{0,2},{1,3},{2,0},{3,1},{4,6},{5,7},{6,4},{7,5},{8,10},{9,11},{10,... | collective-permute-start | bytes 307208 | tf_op jit(solution)/shard_map/ppermute | solution.py:555
  33.9 4.3 %collective-permute-start.11 = (bf16[16,3200]{1,0:T(8,128)(2,1)S(1)}, bf16[16,3200]{1,0:T(8,128)(2,1)S(1)}, u32[]{:S(2)}, u32[]{:S(2)}) collective-permute-start(bf16[16,3200]{1,0:T(8,128)(2,1)S(1)} %get-tuple-element.65.refs_0_), channel_id=1, source_target_pairs={{0,1},{1,0},{2,3},{3,2},{4,5},{5,4},{6,7},{7,6},{8,9},{9,8},{10,11... | collective-permute-start | bytes 307208 | tf_op jit(solution)/shard_map/ppermute | solution.py:555
  36.3 1.9 %collective-permute-start.12 = (bf16[16,3200]{1,0:T(8,128)(2,1)S(1)}, bf16[16,3200]{1,0:T(8,128)(2,1)S(1)}, u32[]{:S(2)}, u32[]{:S(2)}) collective-permute-start(bf16[16,3200]{1,0:T(8,128)(2,1)S(1)} %collective-permute-done.8.refs_1_), channel_id=1, source_target_pairs={{0,1},{1,0},{2,3},{3,2},{4,5},{5,4},{6,7},{7,6},{8,9},{9,8},{10,11... | collective-permute-start | bytes 307208 | tf_op jit(solution)/shard_map/ppermute | solution.py:555
  37.6 1.3 %collective-permute-start.13 = (bf16[16,3200]{1,0:T(8,128)(2,1)S(1)}, bf16[16,3200]{1,0:T(8,128)(2,1)S(1)}, u32[]{:S(2)}, u32[]{:S(2)}) collective-permute-start(bf16[16,3200]{1,0:T(8,128)(2,1)S(1)} %collective-permute-done.9.refs_2_), channel_id=1, source_target_pairs={{0,1},{1,0},{2,3},{3,2},{4,5},{5,4},{6,7},{7,6},{8,9},{9,8},{10,11... | collective-permute-start | bytes 307208 | tf_op jit(solution)/shard_map/ppermute | solution.py:555
  37.7 1.4 %collective-permute-start.14 = (bf16[16,3200]{1,0:T(8,128)(2,1)S(1)}, bf16[16,3200]{1,0:T(8,128)(2,1)S(1)}, u32[]{:S(2)}, u32[]{:S(2)}) collective-permute-start(bf16[16,3200]{1,0:T(8,128)(2,1)S(1)} %collective-permute-done.10.refs_3_), channel_id=1, source_target_pairs={{0,1},{1,0},{2,3},{3,2},{4,5},{5,4},{6,7},{7,6},{8,9},{9,8},{10,11... | collective-permute-start | bytes 307208 | tf_op jit(solution)/shard_map/ppermute | solution.py:555
  41.1 8.0 %collective-permute-start.15 = (bf16[32,3200]{1,0:T(8,128)(2,1)S(1)}, bf16[32,3200]{1,0:T(8,128)(2,1)S(1)}, u32[]{:S(2)}, u32[]{:S(2)}) collective-permute-start(bf16[32,3200]{1,0:T(8,128)(2,1)S(1)} %get-tuple-element.74), channel_id=1, source_target_pairs={{0,4},{1,5},{2,6},{3,7},{4,0},{5,1},{6,2},{7,3},{8,12},{9,13},{10,... | collective-permute-start | bytes 614408 | tf_op jit(solution)/shard_map/ppermute | solution.py:555
  42.9 11.2 %collective-permute-start.16 = (bf16[32,3200]{1,0:T(8,128)(2,1)S(1)}, bf16[32,3200]{1,0:T(8,128)(2,1)S(1)}, u32[]{:S(2)}, u32[]{:S(2)}) collective-permute-start(bf16[32,3200]{1,0:T(8,128)(2,1)S(1)} %get-tuple-element.75), channel_id=1, source_target_pairs={{0,2},{1,3},{2,0},{3,1},{4,6},{5,7},{6,4},{7,5},{8,10},{9,11},{10,... | collective-permute-start | bytes 614408 | tf_op jit(solution)/shard_map/ppermute | solution.py:555
  43.9 10.2 %collective-permute-start.17 = (bf16[32,3200]{1,0:T(8,128)(2,1)S(1)}, bf16[32,3200]{1,0:T(8,128)(2,1)S(1)}, u32[]{:S(2)}, u32[]{:S(2)}) collective-permute-start(bf16[32,3200]{1,0:T(8,128)(2,1)S(1)} %get-tuple-element.76), channel_id=1, source_target_pairs={{0,6},{1,7},{2,4},{3,5},{4,2},{5,3},{6,0},{7,1},{8,14},{9,15},{10,... | collective-permute-start | bytes 614408 | tf_op jit(solution)/shard_map/ppermute | solution.py:555
  55.6 14.5 %collective-permute-start.22 = (bf16[16,3200]{1,0:T(8,128)(2,1)S(1)}, bf16[16,3200]{1,0:T(8,128)(2,1)S(1)}, u32[]{:S(2)}, u32[]{:S(2)}) collective-permute-start(bf16[16,3200]{1,0:T(8,128)(2,1)S(1)} %get-tuple-element.82), channel_id=1, source_target_pairs={{0,8},{1,9},{2,10},{3,11},{4,12},{5,13},{6,14},{7,15},{8,0},{9,1},... | collective-permute-start | bytes 307208 | tf_op jit(solution)/shard_map/ppermute | solution.py:555
  58.0 12.1 %collective-permute-start.24 = (bf16[16,3200]{1,0:T(8,128)(2,1)S(1)}, bf16[16,3200]{1,0:T(8,128)(2,1)S(1)}, u32[]{:S(2)}, u32[]{:S(2)}) collective-permute-start(bf16[16,3200]{1,0:T(8,128)(2,1)S(1)} %get-tuple-element.84), channel_id=1, source_target_pairs={{0,12},{1,13},{2,14},{3,15},{4,8},{5,9},{6,10},{7,11},{8,4},{9,5},... | collective-permute-start | bytes 307208 | tf_op jit(solution)/shard_map/ppermute | solution.py:555
  60.2 14.6 %collective-permute-start.21 = (bf16[16,3200]{1,0:T(8,128)(2,1)S(1)}, bf16[16,3200]{1,0:T(8,128)(2,1)S(1)}, u32[]{:S(2)}, u32[]{:S(2)}) collective-permute-start(bf16[16,3200]{1,0:T(8,128)(2,1)S(1)} %get-tuple-element.81), channel_id=1, source_target_pairs={{0,10},{1,11},{2,8},{3,9},{4,14},{5,15},{6,12},{7,13},{8,2},{9,3},... | collective-permute-start | bytes 307208 | tf_op jit(solution)/shard_map/ppermute | solution.py:555
  62.7 12.1 %collective-permute-start.23 = (bf16[16,3200]{1,0:T(8,128)(2,1)S(1)}, bf16[16,3200]{1,0:T(8,128)(2,1)S(1)}, u32[]{:S(2)}, u32[]{:S(2)}) collective-permute-start(bf16[16,3200]{1,0:T(8,128)(2,1)S(1)} %get-tuple-element.83), channel_id=1, source_target_pairs={{0,14},{1,15},{2,12},{3,13},{4,10},{5,11},{6,8},{7,9},{8,6},{9,7},... | collective-permute-start | bytes 307208 | tf_op jit(solution)/shard_map/ppermute | solution.py:555
  66.5 8.7 %collective-permute-start.18 = (bf16[16,3200]{1,0:T(8,128)(2,1)S(1)}, bf16[16,3200]{1,0:T(8,128)(2,1)S(1)}, u32[]{:S(2)}, u32[]{:S(2)}) collective-permute-start(bf16[16,3200]{1,0:T(8,128)(2,1)S(1)} %get-tuple-element.78), channel_id=1, source_target_pairs={{0,6},{1,7},{2,4},{3,5},{4,2},{5,3},{6,0},{7,1},{8,14},{9,15},{10,... | collective-permute-start | bytes 307208 | tf_op jit(solution)/shard_map/ppermute | solution.py:555
  70.1 6.1 %collective-permute-start.19 = (bf16[16,3200]{1,0:T(8,128)(2,1)S(1)}, bf16[16,3200]{1,0:T(8,128)(2,1)S(1)}, u32[]{:S(2)}, u32[]{:S(2)}) collective-permute-start(bf16[16,3200]{1,0:T(8,128)(2,1)S(1)} %get-tuple-element.79), channel_id=1, source_target_pairs={{0,4},{1,5},{2,6},{3,7},{4,0},{5,1},{6,2},{7,3},{8,12},{9,13},{10,... | collective-permute-start | bytes 307208 | tf_op jit(solution)/shard_map/ppermute | solution.py:555
  70.1 6.1 %collective-permute-start.20 = (bf16[16,3200]{1,0:T(8,128)(2,1)S(1)}, bf16[16,3200]{1,0:T(8,128)(2,1)S(1)}, u32[]{:S(2)}, u32[]{:S(2)}) collective-permute-start(bf16[16,3200]{1,0:T(8,128)(2,1)S(1)} %get-tuple-element.80), channel_id=1, source_target_pairs={{0,2},{1,3},{2,0},{3,1},{4,6},{5,7},{6,4},{7,5},{8,10},{9,11},{10,... | collective-permute-start | bytes 307208 | tf_op jit(solution)/shard_map/ppermute | solution.py:555
  76.4 1.5 %collective-permute-start.25 = (bf16[64,1600]{1,0:T(8,128)(2,1)S(1)}, bf16[64,1600]{1,0:T(8,128)(2,1)S(1)}, u32[]{:S(2)}, u32[]{:S(2)}) collective-permute-start(bf16[64,1600]{1,0:T(8,128)(2,1)S(1)} %get-tuple-element.86), channel_id=1, source_target_pairs={{0,1},{1,0},{2,3},{3,2},{4,5},{5,4},{6,7},{7,6},{8,9},{9,8},{10,11... | collective-permute-start | bytes 614408 | tf_op jit(solution)/shard_map/ppermute | solution.py:555

commit v4 on v3

--- a/solution.py
+++ b/solution.py
@@ -81,10 +81,9 @@
 
 
 NEAR = 4
+INCOMING = (0, 1, 2, 3)
 RIGHT_NEAR = (0, 1, 2, 3)
-RIGHT_FAR = (0, 1, 2, 3)
 OUTGOING = (0, 3, 2, 1)
-INCOMING = (0, 2, 1, 3)
 SUMS_NEAR = (0, 3, 2, 1)
 SUMS_FAR = (1, 0, 3, 2)
 
@@ -424,22 +423,25 @@
         out_ref[:, lanes] = join_pieces(piece, 2 * rows, cols, tile, lane)
 
 
-def channel_of(ref, c, ch, tall):
-    return jnp.concatenate(
-        [ref[side, pl.ds(c, tall, stride=ch), :] for side in range(ref.shape[0])], axis=1
-    ).astype(BF16)
+def channel_of(blocks, c, ch):
+    parts = []
+    for column in blocks:
+        rows = [ref[pl.ds(c, ref.shape[0] // ch, stride=ch), :] for ref in column]
+        parts.append(jnp.concatenate(rows, axis=0))
+    return jnp.concatenate(parts, axis=1).astype(BF16)
 
 
 def widen(part):
     return jnp.pad(part, ((0, 0), (0, LANES - part.shape[1])))
 
 
-def outgoing_multiply(left_ref, right_ref, mixed_ref, ch, tall):
+def outgoing_multiply(left_ref, right, mixed_ref, ch):
     for c in range(ch):
-        left = channel_of(left_ref, c, ch, tall)
-        right = channel_of(right_ref, c, ch, tall)
-        part = lax.dot_general(left, right, (((1,), (1,)), ((), ())), preferred_element_type=F32)
-        mixed_ref[pl.ds(c, tall, stride=ch), :] = widen(part)
+        left = channel_of([[left_ref.at[0]], [left_ref.at[1]]], c, ch)
+        part = lax.dot_general(
+            left, channel_of(right, c, ch), (((1,), (1,)), ((), ())), preferred_element_type=F32
+        )
+        mixed_ref[pl.ds(c, left.shape[0], stride=ch), :] = widen(part)
 
 
 def outgoing_near_kernel(rows, width, *refs):
@@ -458,14 +460,20 @@
         low = jnp.bitwise_xor(lax.rem(place.z, 2), dl)
         begin = pl.multiple_of(low * (rows * ch), 16)
         unpack(value[ch:], right_ref.at[dx], begin, rows, width, lane)
-    outgoing_multiply(left_ref, right_ref, mixed_ref, ch, 2 * rows)
+    outgoing_multiply(left_ref, [[right_ref.at[0]], [right_ref.at[1]]], mixed_ref, ch)
     for dl in range(2):
         pack(mixed_ref, dl * rows * ch, outs[dl], rows, width, lane)
 
 
+def unpack_kernel(rows, width, value_ref, earlier_ref, *outs):
+    ch = value_ref.shape[0] // len(outs)
+    lane = lane_of(ch)
+    for side, out_ref in enumerate(outs):
+        unpack(value_ref[side * ch : (side + 1) * ch, :], out_ref, 0, rows, width, lane)
+
+
 def outgoing_far_kernel(rows, width, *refs):
-    far = restored(refs[:NEAR], RIGHT_FAR)
-    left_ref, done = refs[NEAR], refs[NEAR + 1 : NEAR + 3]
+    far, left_ref, done = refs[:NEAR], refs[NEAR], refs[NEAR + 1 : NEAR + 3]
     outs = refs[NEAR + 3 : 2 * NEAR + 3]
     right_ref, mixed_ref = refs[2 * NEAR + 3 :]
     place = Place()
@@ -476,7 +484,7 @@
         low = jnp.bitwise_xor(lax.rem(place.z, 2), dl)
         begin = pl.multiple_of(low * (rows * ch), 16)
         unpack(far[d][...], right_ref.at[dx], begin, rows, width, lane)
-    outgoing_multiply(left_ref, right_ref, mixed_ref, ch, 2 * rows)
+    outgoing_multiply(left_ref, [[right_ref.at[0]], [right_ref.at[1]]], mixed_ref, ch)
     same = jnp.bitwise_xor(place.half, place.x)
     for dx in range(2):
 
@@ -487,39 +495,36 @@
                 pack(mixed_ref, dl * rows * ch, outs[2 * dl + 1 - dx], rows, width, lane)
 
 
-def incoming_kernel(rows, width, dh, sides, *refs):
-    near, outs, scratch = restored(refs[:NEAR], INCOMING), refs[NEAR:-3], refs[-3:]
-    left_ref, right_ref, mixed_ref = scratch
+def incoming_kernel(rows, width, jobs, *refs):
+    lefts, rights, outs, mixed_ref = refs[:NEAR], refs[NEAR : 2 * NEAR], refs[2 * NEAR : -1], refs[-1]
     place = Place()
     ch = outs[0].shape[0]
     lane = lane_of(ch)
-    wanted = jnp.bitwise_xor(jnp.bitwise_xor(place.half, dh), place.x)
-    for d in range(NEAR):
-        dl, dx = divmod(d, 2)
-        begin = dl * rows * ch
-        if dx in sides:
-            at = right_ref.at[sides.index(dx)]
-            unpack(near[d][ch:, :], at, begin, rows, width, lane)
-
-        @pl.when(wanted == dx)
-        def _(d=d, begin=begin):
-            unpack(near[d][:ch, :], left_ref, begin, rows, width, lane)
-
-    tall = 2 * rows
-    for c in range(ch):
-        right = channel_of(right_ref, c, ch, tall)
-        left = left_ref[pl.ds(c, tall, stride=ch), :].astype(BF16)
-        part = lax.dot_general(left, right, (((0,), (0,)), ((), ())), preferred_element_type=F32)
-        for side in range(len(sides)):
-            mixed_ref[side, pl.ds(c, width, stride=ch), :] = part[
-                :width, side * LANES : (side + 1) * LANES
-            ]
-    for dl in range(2):
-        low = jnp.bitwise_xor(lax.rem(place.z, 2), dl)
-        begin = pl.multiple_of(low * (rows * ch), 16)
-        for side in range(len(sides)):
-            out_ref = outs[dl * len(sides) + side]
-            pack_halves(mixed_ref.at[side], begin, out_ref, rows, width // 2, lane)
+    for dh, sides in jobs:
+        wanted = jnp.bitwise_xor(jnp.bitwise_xor(place.half, dh), place.x)
+        right = [[rights[dx], rights[2 + dx]] for dx in sides]
+        for dx in range(2):
+
+            @pl.when(wanted == dx)
+            def _(dx=dx, right=right, sides=sides):
+                for c in range(ch):
+                    part = lax.dot_general(
+                        channel_of([[lefts[dx], lefts[2 + dx]]], c, ch),
+                        channel_of(right, c, ch),
+                        (((0,), (0,)), ((), ())),
+                        preferred_element_type=F32,
+                    )
+                    for side in range(len(sides)):
+                        mixed_ref[side, pl.ds(c, width, stride=ch), :] = part[
+                            :width, side * LANES : (side + 1) * LANES
+                        ]
+
+        for dl in range(2):
+            low = jnp.bitwise_xor(lax.rem(place.z, 2), dl)
+            begin = pl.multiple_of(low * (rows * ch), 16)
+            for side in range(len(sides)):
+                out_ref, *outs = outs
+                pack_halves(mixed_ref.at[side], begin, out_ref, rows, width // 2, lane)
 
 
 def call(kernel, micros, outs, scratch, *args, space=pltpu.VMEM):
@@ -629,12 +634,19 @@
         normed,
         gates,
     )
+    block = ((rows * ch, LANES), F32)
+
+    def unpacked(value, operands, earlier):
+        return call(
+            functools.partial(unpack_kernel, rows, width), 0.2, [block] * operands, [], value, earlier
+        )
+
     mixed = call(
         functools.partial(outgoing_far_kernel, rows, width),
         1.2,
         [(ch, total)] * NEAR,
         [sides, side],
-        *ordered(far, RIGHT_FAR),
+        *far,
         left,
         *mixed,
     )
@@ -659,21 +671,26 @@
     near = swap_all(near, 0)
     half = rows * cols
 
-    def incoming(dh, sides):
+    got = [None] * NEAR
+    earlier = valid
+    for d in INCOMING:
+        got[d] = unpacked(near[d], 2, earlier)
+        earlier = got[d][0]
+    lefts, rights = zip(*got, strict=True)
+
+    def incoming(micros, *jobs):
         return call(
-            functools.partial(incoming_kernel, rows, width, dh, sides),
-            2.0,
-            [(ch, total)] * (2 * len(sides)),
-            [
-                side,
-                ((len(sides), tall * ch, LANES), F32),
-                ((len(sides), width * ch, LANES), F32),
-            ],
-            *ordered(near, INCOMING),
-        )
-
-    first, second = incoming(1, (0,)), incoming(1, (1,))
-    parts = [incoming(0, (0, 1)), [first[0], second[0], first[1], second[1]]]
+            functools.partial(incoming_kernel, rows, width, jobs),
+            micros,
+            [(ch, total)] * sum(2 * len(sides) for dh, sides in jobs),
+            [((2, width * ch, LANES), F32)],
+            *lefts,
+            *rights,
+        )
+
+    first = incoming(1.0, (1, (0,)))
+    second = incoming(2.5, (1, (1,)), (0, (0, 1)))
+    parts = [second[2:], [first[0], second[0], first[1], second[1]]]
     own, gating = call(
         functools.partial(own_kernel, chunk, cols),
         2.0,

time: 79.3 us -> 78.6 us (level)
  starting transfers between devices: 33.1 us -> 35 us
  waiting for transfers between devices: 29.8 us -> 28.1 us
  Pallas kernels: 16.2 us -> 15.2 us
    ppermute x26, starting transfers between devices: 33.1 us -> 35 us  [swap(): return lax.ppermute(value, ('row', 'col'), pairs)]
    ppermute x26, waiting for transfers between devices: 29.8 us -> 28.1 us  [swap(): return lax.ppermute(value, ('row', 'col'), pairs)]
    pallas_call x12 -> x15, Pallas kernels: 16.2 us -> 15.2 us  [call(): pl.pallas_call(kernel, out_shape=[jax.ShapeDtypeStruct(shape, dtype) for...]
  transfers between devices with their start and end apart: 26 -> 26, of which waited for: 16 -> 15; matrix products, arithmetic and copies ran while one was open for 0% -> 0% of each run, Pallas kernels for 11% -> 10%
where the time goes in v4:
time: 78.6 us; the launch traced here: 78.4 us
  starting transfers between devices  35 us (45%)
  waiting for transfers between devices  28.1 us (36%)
  Pallas kernels  15.2 us (19%)
    ppermute x26, starting transfers between devices, swap(): return lax.ppermute(value, ('row', 'col'), pairs)  35 us
    ppermute x26, waiting for transfers between devices, swap(): return lax.ppermute(value, ('row', 'col'), pairs)  28.1 us
    pallas_call x15, Pallas kernels, call(): pl.pallas_call(kernel, out_shape=[jax.ShapeDtypeStruct(shape, dtype) for...  15.2 us
  transfers between devices with their start and end apart: 26, of which 15 were waited for; matrix products, arithmetic and copies ran while one was open for 0% of the time, Pallas kernels for 10%

profile of v4, /device:TPU:0, one launch (start us, length us, event | category | flops | bytes accessed | tf_op | source)
XLA Modules:
  0.0 78.4 jit_solution(4591735174113079214)
XLA Ops:
  0.5 1.5 %shard_map.73 = (bf16[40,40,128]{2,1,0:T(8,128)(2,1)S(1)}, f32[1,3200]{1,0:T(1,128)S(1)}, bf16[2,256,128]{2,1,0:T(8,128)(2,1)S(1)}, bf16[2,128,128]{2,1,0:T(8,12...) custom-call(bf16[40,40,128]{2,1,0:T(8,128)(2,1)} %pair_in.1, ...), custom_call_target="tpu_custom_call" | custom-call | flops 1650000000 | tf_op jit(solution)/shard_map/pallas_call | solution.py:534
  2.0 1.1 %shard_map.74 = (bf16[16,3200]{1,0:T(8,128)(2,1)S(1)}, bf16[16,3200]{1,0:T(8,128)(2,1)S(1)}, bf16[16,3200]{1,0:T(8,128)(2,1)S(1)}, bf16[16,3200]{1,0:T(8,128)(2,...) custom-call(bf16[40,40,128]{2,1,0:T(8,128)(2,1)S(1)} %get-tuple-element.56.own_ref, ...), custom_call_target="tpu_custom_call" | custom-call | flops 1100000000 | tf_op jit(solution)/shard_map/pallas_call | solution.py:534
  3.6 2.9 %collective-permute-start.5 = (bf16[32,3200]{1,0:T(8,128)(2,1)S(1)}, bf16[32,3200]{1,0:T(8,128)(2,1)S(1)}, u32[]{:S(2)}, u32[]{:S(2)}) collective-permute-start(bf16[32,3200]{1,0:T(8,128)(2,1)S(1)} %get-tuple-element.66), channel_id=1, source_target_pairs={{0,2},{1,3},{2,0},{3,1},{4,6},{5,7},{6,4},{7,5},{8,10},{9,11},{10,... | collective-permute-start | bytes 614408 | tf_op jit(solution)/shard_map/ppermute | solution.py:560
  6.5 1.6 %collective-permute-start.6 = (bf16[32,3200]{1,0:T(8,128)(2,1)S(1)}, bf16[32,3200]{1,0:T(8,128)(2,1)S(1)}, u32[]{:S(2)}, u32[]{:S(2)}) collective-permute-start(bf16[32,3200]{1,0:T(8,128)(2,1)S(1)} %get-tuple-element.67), channel_id=1, source_target_pairs={{0,4},{1,5},{2,6},{3,7},{4,0},{5,1},{6,2},{7,3},{8,12},{9,13},{10,... | collective-permute-start | bytes 614408 | tf_op jit(solution)/shard_map/ppermute | solution.py:560
  8.1 3.0 %collective-permute-start.1 = (bf16[16,3200]{1,0:T(8,128)(2,1)S(1)}, bf16[16,3200]{1,0:T(8,128)(2,1)S(1)}, u32[]{:S(2)}, u32[]{:S(2)}) collective-permute-start(bf16[16,3200]{1,0:T(8,128)(2,1)S(1)} %get-tuple-element.60.rest_0_), channel_id=1, source_target_pairs={{0,8},{1,9},{2,10},{3,11},{4,12},{5,13},{6,14},{7,15},{8,0},{9,1},... | collective-permute-start | bytes 307208 | tf_op jit(solution)/shard_map/ppermute | solution.py:560
  11.1 1.3 %collective-permute-start.2 = (bf16[16,3200]{1,0:T(8,128)(2,1)S(1)}, bf16[16,3200]{1,0:T(8,128)(2,1)S(1)}, u32[]{:S(2)}, u32[]{:S(2)}) collective-permute-start(bf16[16,3200]{1,0:T(8,128)(2,1)S(1)} %get-tuple-element.61.rest_1_), channel_id=1, source_target_pairs={{0,10},{1,11},{2,8},{3,9},{4,14},{5,15},{6,12},{7,13},{8,2},{9,3},... | collective-permute-start | bytes 307208 | tf_op jit(solution)/shard_map/ppermute | solution.py:560
  12.3 3.6 %collective-permute-start.3 = (bf16[16,3200]{1,0:T(8,128)(2,1)S(1)}, bf16[16,3200]{1,0:T(8,128)(2,1)S(1)}, u32[]{:S(2)}, u32[]{:S(2)}) collective-permute-start(bf16[16,3200]{1,0:T(8,128)(2,1)S(1)} %get-tuple-element.62.rest_2_), channel_id=1, source_target_pairs={{0,12},{1,13},{2,14},{3,15},{4,8},{5,9},{6,10},{7,11},{8,4},{9,5},... | collective-permute-start | bytes 307208 | tf_op jit(solution)/shard_map/ppermute | solution.py:560
  15.9 2.9 %collective-permute-done.6.refs_2_ = bf16[32,3200]{1,0:T(8,128)(2,1)S(1)} collective-permute-done((bf16[32,3200]{1,0:T(8,128)(2,1)S(1)}, bf16[32,3200]{1,0:T(8,128)(2,1)S(1)}, u32[]{:S(2)}, u32[]{:S(2)}) %collective-permute-start.6) | collective-permute-done | bytes 204832 | tf_op jit(solution)/shard_map/ppermute | solution.py:560
  18.8 3.1 %collective-permute-start.4 = (bf16[16,3200]{1,0:T(8,128)(2,1)S(1)}, bf16[16,3200]{1,0:T(8,128)(2,1)S(1)}, u32[]{:S(2)}, u32[]{:S(2)}) collective-permute-start(bf16[16,3200]{1,0:T(8,128)(2,1)S(1)} %get-tuple-element.63.rest_3_), channel_id=1, source_target_pairs={{0,14},{1,15},{2,12},{3,13},{4,10},{5,11},{6,8},{7,9},{8,6},{9,7},... | collective-permute-start | bytes 307208 | tf_op jit(solution)/shard_map/ppermute | solution.py:560
  21.9 1.7 %shard_map.76 = (f32[128,3200]{1,0:T(8,128)S(1)}, f32[2,1280,128]{2,1,0:T(8,128)S(1)}, bf16[16,3200]{1,0:T(8,128)(2,1)S(1)}, bf16[16,3200]{1,0:T(8,128)(2,1)S(1)}) custom-call(bf16[32,3200]{1,0:T(8,128)(2,1)S(1)} %get-tuple-element.65.refs_0_, bf16[32,3200]{1,0:T(8,128)(2,1)S(1)} %collective-permute-done.5.refs_1_, ...), custom_call_target="tpu_custom_call" | custom-call | flops 2200000000 | tf_op jit(solution)/shard_map/pallas_call | solution.py:534
  23.6 3.9 %collective-permute-done.3.refs_2_ = bf16[16,3200]{1,0:T(8,128)(2,1)S(1)} collective-permute-done((bf16[16,3200]{1,0:T(8,128)(2,1)S(1)}, bf16[16,3200]{1,0:T(8,128)(2,1)S(1)}, u32[]{:S(2)}, u32[]{:S(2)}) %collective-permute-start.3) | collective-permute-done | bytes 102432 | tf_op jit(solution)/shard_map/ppermute | solution.py:560
  27.5 1.1 %collective-permute-done.4.refs_3_ = bf16[16,3200]{1,0:T(8,128)(2,1)S(1)} collective-permute-done((bf16[16,3200]{1,0:T(8,128)(2,1)S(1)}, bf16[16,3200]{1,0:T(8,128)(2,1)S(1)}, u32[]{:S(2)}, u32[]{:S(2)}) %collective-permute-start.4) | collective-permute-done | bytes 102432 | tf_op jit(solution)/shard_map/ppermute | solution.py:560
  28.6 1.4 %shard_map.77 = (bf16[16,3200]{1,0:T(8,128)(2,1)S(1)}, bf16[16,3200]{1,0:T(8,128)(2,1)S(1)}, bf16[16,3200]{1,0:T(8,128)(2,1)S(1)}, bf16[16,3200]{1,0:T(8,128)(2,1)S(1)}) custom-call(bf16[16,3200]{1,0:T(8,128)(2,1)S(1)} %collective-permute-done.1.refs_0_, bf16[16,3200]{1,0:T(8,128)(2,1)S(1)} %collective-permute-done.2.refs_1_, ...), custom_call_target="tpu_custom_call" | custom-call | flops 1320000000 | tf_op jit(solution)/shard_map/pallas_call | solution.py:534
  30.0 2.9 %collective-permute-start.8 = (bf16[16,3200]{1,0:T(8,128)(2,1)S(1)}, bf16[16,3200]{1,0:T(8,128)(2,1)S(1)}, u32[]{:S(2)}, u32[]{:S(2)}) collective-permute-start(bf16[16,3200]{1,0:T(8,128)(2,1)S(1)} %get-tuple-element.74), channel_id=1, source_target_pairs={{0,6},{1,7},{2,4},{3,5},{4,2},{5,3},{6,0},{7,1},{8,14},{9,15},{10,... | collective-permute-start | bytes 307208 | tf_op jit(solution)/shard_map/ppermute | solution.py:560
  33.9 2.4 %collective-permute-done.8.refs_1_ = bf16[16,3200]{1,0:T(8,128)(2,1)S(1)} collective-permute-done((bf16[16,3200]{1,0:T(8,128)(2,1)S(1)}, bf16[16,3200]{1,0:T(8,128)(2,1)S(1)}, u32[]{:S(2)}, u32[]{:S(2)}) %collective-permute-start.8) | collective-permute-done | bytes 102432 | tf_op jit(solution)/shard_map/ppermute | solution.py:560
  36.3 1.3 %collective-permute-done.9.refs_2_ = bf16[16,3200]{1,0:T(8,128)(2,1)S(1)} collective-permute-done((bf16[16,3200]{1,0:T(8,128)(2,1)S(1)}, bf16[16,3200]{1,0:T(8,128)(2,1)S(1)}, u32[]{:S(2)}, u32[]{:S(2)}) %collective-permute-start.9) | collective-permute-done | bytes 102432 | tf_op jit(solution)/shard_map/ppermute | solution.py:560
  39.1 2.0 %shard_map.78 = (bf16[32,3200]{1,0:T(8,128)(2,1)S(1)}, bf16[32,3200]{1,0:T(8,128)(2,1)S(1)}, bf16[32,3200]{1,0:T(8,128)(2,1)S(1)}, bf16[32,3200]{1,0:T(8,128)(2,...) custom-call(bf16[16,3200]{1,0:T(8,128)(2,1)S(1)} %get-tuple-element.73.refs_0_, ...), custom_call_target="tpu_custom_call" | custom-call | flops 2529999872 | tf_op jit(solution)/shard_map/pallas_call | solution.py:534
  41.1 1.2 %collective-permute-start.15 = (bf16[32,3200]{1,0:T(8,128)(2,1)S(1)}, bf16[32,3200]{1,0:T(8,128)(2,1)S(1)}, u32[]{:S(2)}, u32[]{:S(2)}) collective-permute-start(bf16[32,3200]{1,0:T(8,128)(2,1)S(1)} %get-tuple-element.83), channel_id=1, source_target_pairs={{0,2},{1,3},{2,0},{3,1},{4,6},{5,7},{6,4},{7,5},{8,10},{9,11},{10,... | collective-permute-start | bytes 614408 | tf_op jit(solution)/shard_map/ppermute | solution.py:560
  42.3 1.6 %collective-permute-start.16 = (bf16[32,3200]{1,0:T(8,128)(2,1)S(1)}, bf16[32,3200]{1,0:T(8,128)(2,1)S(1)}, u32[]{:S(2)}, u32[]{:S(2)}) collective-permute-start(bf16[32,3200]{1,0:T(8,128)(2,1)S(1)} %get-tuple-element.85), channel_id=1, source_target_pairs={{0,4},{1,5},{2,6},{3,7},{4,0},{5,1},{6,2},{7,3},{8,12},{9,13},{10,... | collective-permute-start | bytes 614408 | tf_op jit(solution)/shard_map/ppermute | solution.py:560
  44.8 3.6 %collective-permute-done.15.value_ref = bf16[32,3200]{1,0:T(8,128)(2,1)S(1)} collective-permute-done((bf16[32,3200]{1,0:T(8,128)(2,1)S(1)}, bf16[32,3200]{1,0:T(8,128)(2,1)S(1)}, u32[]{:S(2)}, u32[]{:S(2)}) %collective-permute-start.15) | collective-permute-done | bytes 204832 | tf_op jit(solution)/shard_map/ppermute | solution.py:560
  48.7 1.5 %collective-permute-done.16.value_ref = bf16[32,3200]{1,0:T(8,128)(2,1)S(1)} collective-permute-done((bf16[32,3200]{1,0:T(8,128)(2,1)S(1)}, bf16[32,3200]{1,0:T(8,128)(2,1)S(1)}, u32[]{:S(2)}, u32[]{:S(2)}) %collective-permute-start.16) | collective-permute-done | bytes 204832 | tf_op jit(solution)/shard_map/ppermute | solution.py:560
  50.4 3.7 %collective-permute-done.17.value_ref = bf16[32,3200]{1,0:T(8,128)(2,1)S(1)} collective-permute-done((bf16[32,3200]{1,0:T(8,128)(2,1)S(1)}, bf16[32,3200]{1,0:T(8,128)(2,1)S(1)}, u32[]{:S(2)}, u32[]{:S(2)}) %collective-permute-start.17) | collective-permute-done | bytes 204832 | tf_op jit(solution)/shard_map/ppermute | solution.py:560
  55.2 2.7 %collective-permute-start.22 = (bf16[16,3200]{1,0:T(8,128)(2,1)S(1)}, bf16[16,3200]{1,0:T(8,128)(2,1)S(1)}, u32[]{:S(2)}, u32[]{:S(2)}) collective-permute-start(bf16[16,3200]{1,0:T(8,128)(2,1)S(1)} %get-tuple-element.98), channel_id=1, source_target_pairs={{0,8},{1,9},{2,10},{3,11},{4,12},{5,13},{6,14},{7,15},{8,0},{9,1},... | collective-permute-start | bytes 307208 | tf_op jit(solution)/shard_map/ppermute | solution.py:560
  57.9 1.3 %collective-permute-start.24 = (bf16[16,3200]{1,0:T(8,128)(2,1)S(1)}, bf16[16,3200]{1,0:T(8,128)(2,1)S(1)}, u32[]{:S(2)}, u32[]{:S(2)}) collective-permute-start(bf16[16,3200]{1,0:T(8,128)(2,1)S(1)} %get-tuple-element.100), channel_id=1, source_target_pairs={{0,12},{1,13},{2,14},{3,15},{4,8},{5,9},{6,10},{7,11},{8,4},{9,5},... | collective-permute-start | bytes 307208 | tf_op jit(solution)/shard_map/ppermute | solution.py:560
  59.2 2.7 %shard_map.83 = (bf16[16,3200]{1,0:T(8,128)(2,1)S(1)}, bf16[16,3200]{1,0:T(8,128)(2,1)S(1)}, bf16[16,3200]{1,0:T(8,128)(2,1)S(1)}, bf16[16,3200]{1,0:T(8,128)(2,...) custom-call(f32[640,128]{1,0:T(8,128)S(1)} %get-tuple-element.82.earlier_ref.refs_0_, ...), custom_call_target="tpu_custom_call" | custom-call | flops 2750000128 | tf_op jit(solution)/shard_map/pallas_call | solution.py:534
  62.3 2.2 %collective-permute-start.19 = (bf16[16,3200]{1,0:T(8,128)(2,1)S(1)}, bf16[16,3200]{1,0:T(8,128)(2,1)S(1)}, u32[]{:S(2)}, u32[]{:S(2)}) collective-permute-start(bf16[16,3200]{1,0:T(8,128)(2,1)S(1)} %get-tuple-element.95), channel_id=1, source_target_pairs={{0,4},{1,5},{2,6},{3,7},{4,0},{5,1},{6,2},{7,3},{8,12},{9,13},{10,... | collective-permute-start | bytes 307208 | tf_op jit(solution)/shard_map/ppermute | solution.py:560
  65.5 2.0 %collective-permute-start.21 = (bf16[16,3200]{1,0:T(8,128)(2,1)S(1)}, bf16[16,3200]{1,0:T(8,128)(2,1)S(1)}, u32[]{:S(2)}, u32[]{:S(2)}) collective-permute-start(bf16[16,3200]{1,0:T(8,128)(2,1)S(1)} %get-tuple-element.97), channel_id=1, source_target_pairs={{0,10},{1,11},{2,8},{3,9},{4,14},{5,15},{6,12},{7,13},{8,2},{9,3},... | collective-permute-start | bytes 307208 | tf_op jit(solution)/shard_map/ppermute | solution.py:560
  67.5 1.5 %collective-permute-start.23 = (bf16[16,3200]{1,0:T(8,128)(2,1)S(1)}, bf16[16,3200]{1,0:T(8,128)(2,1)S(1)}, u32[]{:S(2)}, u32[]{:S(2)}) collective-permute-start(bf16[16,3200]{1,0:T(8,128)(2,1)S(1)} %get-tuple-element.99), channel_id=1, source_target_pairs={{0,14},{1,15},{2,12},{3,13},{4,10},{5,11},{6,8},{7,9},{8,6},{9,7},... | collective-permute-start | bytes 307208 | tf_op jit(solution)/shard_map/ppermute | solution.py:560
  69.8 1.6 %collective-permute-done.19.refs_2_ = bf16[16,3200]{1,0:T(8,128)(2,1)S(1)} collective-permute-done((bf16[16,3200]{1,0:T(8,128)(2,1)S(1)}, bf16[16,3200]{1,0:T(8,128)(2,1)S(1)}, u32[]{:S(2)}, u32[]{:S(2)}) %collective-permute-start.19) | collective-permute-done | bytes 102432 | tf_op jit(solution)/shard_map/ppermute | solution.py:560
  71.4 4.1 %collective-permute-done.21.refs_4_ = bf16[16,3200]{1,0:T(8,128)(2,1)S(1)} collective-permute-done((bf16[16,3200]{1,0:T(8,128)(2,1)S(1)}, bf16[16,3200]{1,0:T(8,128)(2,1)S(1)}, u32[]{:S(2)}, u32[]{:S(2)}) %collective-permute-start.21) | collective-permute-done | bytes 102432 | tf_op jit(solution)/shard_map/ppermute | solution.py:560
  75.7 1.3 %shard_map.86 = (f32[1600,128]{1,0:T(8,128)S(1)}, f32[1600,128]{1,0:T(8,128)S(1)}) custom-call(bf16[128,3200]{1,0:T(8,128)(2,1)S(1)} %get-tuple-element.103.after_ref, bf16[128,3200]{1,0:T(8,128)(2,1)S(1)} %get-tuple-element.104.normed_ref, bf16[2,128,128]{2,1,0:T(8,128)(2,1)S(1)} %get-tuple-element.69.refs_5_.gate_ref), custom_call_target="tpu_custom_call" | custom-call | flops 2200000000 | tf_op jit(solution)/shard_map/pallas_call | solution.py:534
  77.2 1.3 %shard_map.87 = bf16[1600,128]{1,0:T(8,128)(2,1)} custom-call(bf16[64,1600]{1,0:T(8,128)(2,1)S(1)} %get-tuple-element.101.keep_ref, bf16[64,1600]{1,0:T(8,128)(2,1)S(1)} %collective-permute-done.25.got_ref, f32[1600,128]{1,0:T(8,128)S(1)} %get-tuple-element.105.own_ref, f32[1600,128]{1,0:T(8,128)S(1)} %get-tuple-element.106.gating_ref, ...), custom_call_target="tpu_custom_call" | custom-call | flops 1100000000 | tf_op jit(solution)/shard_map/pallas_call | solution.py:534
  (35 shorter events, 8.4 us)
Async XLA Ops:
  0.0 2.0 %collective-permute-start = (bf16[40,40,128]{2,1,0:T(8,128)(2,1)}, bf16[40,40,128]{2,1,0:T(8,128)(2,1)S(1)}, u32[]{:S(2)}, u32[]{:S(2)}) collective-permute-start(bf16[40,40,128]{2,1,0:T(8,128)(2,1)} %pair_in.1), channel_id=1, source_target_pairs={{0,1},{1,0},{2,3},{3,2},{4,5},{5,4},{6,7},{7,6},{8,9},{9,8},{10,11... | collective-permute-start | bytes 1228808 | tf_op jit(solution)/shard_map/ppermute | solution.py:560
  3.6 8.8 %collective-permute-start.5 = (bf16[32,3200]{1,0:T(8,128)(2,1)S(1)}, bf16[32,3200]{1,0:T(8,128)(2,1)S(1)}, u32[]{:S(2)}, u32[]{:S(2)}) collective-permute-start(bf16[32,3200]{1,0:T(8,128)(2,1)S(1)} %get-tuple-element.66), channel_id=1, source_target_pairs={{0,2},{1,3},{2,0},{3,1},{4,6},{5,7},{6,4},{7,5},{8,10},{9,11},{10,... | collective-permute-start | bytes 614408 | tf_op jit(solution)/shard_map/ppermute | solution.py:560
  6.5 12.3 %collective-permute-start.6 = (bf16[32,3200]{1,0:T(8,128)(2,1)S(1)}, bf16[32,3200]{1,0:T(8,128)(2,1)S(1)}, u32[]{:S(2)}, u32[]{:S(2)}) collective-permute-start(bf16[32,3200]{1,0:T(8,128)(2,1)S(1)} %get-tuple-element.67), channel_id=1, source_target_pairs={{0,4},{1,5},{2,6},{3,7},{4,0},{5,1},{6,2},{7,3},{8,12},{9,13},{10,... | collective-permute-start | bytes 614408 | tf_op jit(solution)/shard_map/ppermute | solution.py:560
  8.1 13.9 %collective-permute-start.7 = (bf16[32,3200]{1,0:T(8,128)(2,1)S(1)}, bf16[32,3200]{1,0:T(8,128)(2,1)S(1)}, u32[]{:S(2)}, u32[]{:S(2)}) collective-permute-start(bf16[32,3200]{1,0:T(8,128)(2,1)S(1)} %get-tuple-element.68), channel_id=1, source_target_pairs={{0,6},{1,7},{2,4},{3,5},{4,2},{5,3},{6,0},{7,1},{8,14},{9,15},{10,... | collective-permute-start | bytes 614408 | tf_op jit(solution)/shard_map/ppermute | solution.py:560
  8.1 15.6 %collective-permute-start.1 = (bf16[16,3200]{1,0:T(8,128)(2,1)S(1)}, bf16[16,3200]{1,0:T(8,128)(2,1)S(1)}, u32[]{:S(2)}, u32[]{:S(2)}) collective-permute-start(bf16[16,3200]{1,0:T(8,128)(2,1)S(1)} %get-tuple-element.60.rest_0_), channel_id=1, source_target_pairs={{0,8},{1,9},{2,10},{3,11},{4,12},{5,13},{6,14},{7,15},{8,0},{9,1},... | collective-permute-start | bytes 307208 | tf_op jit(solution)/shard_map/ppermute | solution.py:560
  11.1 12.6 %collective-permute-start.2 = (bf16[16,3200]{1,0:T(8,128)(2,1)S(1)}, bf16[16,3200]{1,0:T(8,128)(2,1)S(1)}, u32[]{:S(2)}, u32[]{:S(2)}) collective-permute-start(bf16[16,3200]{1,0:T(8,128)(2,1)S(1)} %get-tuple-element.61.rest_1_), channel_id=1, source_target_pairs={{0,10},{1,11},{2,8},{3,9},{4,14},{5,15},{6,12},{7,13},{8,2},{9,3},... | collective-permute-start | bytes 307208 | tf_op jit(solution)/shard_map/ppermute | solution.py:560
  12.3 15.2 %collective-permute-start.3 = (bf16[16,3200]{1,0:T(8,128)(2,1)S(1)}, bf16[16,3200]{1,0:T(8,128)(2,1)S(1)}, u32[]{:S(2)}, u32[]{:S(2)}) collective-permute-start(bf16[16,3200]{1,0:T(8,128)(2,1)S(1)} %get-tuple-element.62.rest_2_), channel_id=1, source_target_pairs={{0,12},{1,13},{2,14},{3,15},{4,8},{5,9},{6,10},{7,11},{8,4},{9,5},... | collective-permute-start | bytes 307208 | tf_op jit(solution)/shard_map/ppermute | solution.py:560
  18.8 9.8 %collective-permute-start.4 = (bf16[16,3200]{1,0:T(8,128)(2,1)S(1)}, bf16[16,3200]{1,0:T(8,128)(2,1)S(1)}, u32[]{:S(2)}, u32[]{:S(2)}) collective-permute-start(bf16[16,3200]{1,0:T(8,128)(2,1)S(1)} %get-tuple-element.63.rest_3_), channel_id=1, source_target_pairs={{0,14},{1,15},{2,12},{3,13},{4,10},{5,11},{6,8},{7,9},{8,6},{9,7},... | collective-permute-start | bytes 307208 | tf_op jit(solution)/shard_map/ppermute | solution.py:560
  30.0 6.3 %collective-permute-start.8 = (bf16[16,3200]{1,0:T(8,128)(2,1)S(1)}, bf16[16,3200]{1,0:T(8,128)(2,1)S(1)}, u32[]{:S(2)}, u32[]{:S(2)}) collective-permute-start(bf16[16,3200]{1,0:T(8,128)(2,1)S(1)} %get-tuple-element.74), channel_id=1, source_target_pairs={{0,6},{1,7},{2,4},{3,5},{4,2},{5,3},{6,0},{7,1},{8,14},{9,15},{10,... | collective-permute-start | bytes 307208 | tf_op jit(solution)/shard_map/ppermute | solution.py:560
  32.8 4.8 %collective-permute-start.9 = (bf16[16,3200]{1,0:T(8,128)(2,1)S(1)}, bf16[16,3200]{1,0:T(8,128)(2,1)S(1)}, u32[]{:S(2)}, u32[]{:S(2)}) collective-permute-start(bf16[16,3200]{1,0:T(8,128)(2,1)S(1)} %get-tuple-element.75), channel_id=1, source_target_pairs={{0,4},{1,5},{2,6},{3,7},{4,0},{5,1},{6,2},{7,3},{8,12},{9,13},{10,... | collective-permute-start | bytes 307208 | tf_op jit(solution)/shard_map/ppermute | solution.py:560
  33.0 4.7 %collective-permute-start.10 = (bf16[16,3200]{1,0:T(8,128)(2,1)S(1)}, bf16[16,3200]{1,0:T(8,128)(2,1)S(1)}, u32[]{:S(2)}, u32[]{:S(2)}) collective-permute-start(bf16[16,3200]{1,0:T(8,128)(2,1)S(1)} %get-tuple-element.76), channel_id=1, source_target_pairs={{0,2},{1,3},{2,0},{3,1},{4,6},{5,7},{6,4},{7,5},{8,10},{9,11},{10,... | collective-permute-start | bytes 307208 | tf_op jit(solution)/shard_map/ppermute | solution.py:560
  33.9 4.3 %collective-permute-start.11 = (bf16[16,3200]{1,0:T(8,128)(2,1)S(1)}, bf16[16,3200]{1,0:T(8,128)(2,1)S(1)}, u32[]{:S(2)}, u32[]{:S(2)}) collective-permute-start(bf16[16,3200]{1,0:T(8,128)(2,1)S(1)} %get-tuple-element.73.refs_0_), channel_id=1, source_target_pairs={{0,1},{1,0},{2,3},{3,2},{4,5},{5,4},{6,7},{7,6},{8,9},{9,8},{10,11... | collective-permute-start | bytes 307208 | tf_op jit(solution)/shard_map/ppermute | solution.py:560
  36.3 1.9 %collective-permute-start.12 = (bf16[16,3200]{1,0:T(8,128)(2,1)S(1)}, bf16[16,3200]{1,0:T(8,128)(2,1)S(1)}, u32[]{:S(2)}, u32[]{:S(2)}) collective-permute-start(bf16[16,3200]{1,0:T(8,128)(2,1)S(1)} %collective-permute-done.8.refs_1_), channel_id=1, source_target_pairs={{0,1},{1,0},{2,3},{3,2},{4,5},{5,4},{6,7},{7,6},{8,9},{9,8},{10,11... | collective-permute-start | bytes 307208 | tf_op jit(solution)/shard_map/ppermute | solution.py:560
  37.6 1.3 %collective-permute-start.13 = (bf16[16,3200]{1,0:T(8,128)(2,1)S(1)}, bf16[16,3200]{1,0:T(8,128)(2,1)S(1)}, u32[]{:S(2)}, u32[]{:S(2)}) collective-permute-start(bf16[16,3200]{1,0:T(8,128)(2,1)S(1)} %collective-permute-done.9.refs_2_), channel_id=1, source_target_pairs={{0,1},{1,0},{2,3},{3,2},{4,5},{5,4},{6,7},{7,6},{8,9},{9,8},{10,11... | collective-permute-start | bytes 307208 | tf_op jit(solution)/shard_map/ppermute | solution.py:560
  37.7 1.4 %collective-permute-start.14 = (bf16[16,3200]{1,0:T(8,128)(2,1)S(1)}, bf16[16,3200]{1,0:T(8,128)(2,1)S(1)}, u32[]{:S(2)}, u32[]{:S(2)}) collective-permute-start(bf16[16,3200]{1,0:T(8,128)(2,1)S(1)} %collective-permute-done.10.refs_3_), channel_id=1, source_target_pairs={{0,1},{1,0},{2,3},{3,2},{4,5},{5,4},{6,7},{7,6},{8,9},{9,8},{10,11... | collective-permute-start | bytes 307208 | tf_op jit(solution)/shard_map/ppermute | solution.py:560
  41.1 7.4 %collective-permute-start.15 = (bf16[32,3200]{1,0:T(8,128)(2,1)S(1)}, bf16[32,3200]{1,0:T(8,128)(2,1)S(1)}, u32[]{:S(2)}, u32[]{:S(2)}) collective-permute-start(bf16[32,3200]{1,0:T(8,128)(2,1)S(1)} %get-tuple-element.83), channel_id=1, source_target_pairs={{0,2},{1,3},{2,0},{3,1},{4,6},{5,7},{6,4},{7,5},{8,10},{9,11},{10,... | collective-permute-start | bytes 614408 | tf_op jit(solution)/shard_map/ppermute | solution.py:560
  42.3 8.0 %collective-permute-start.16 = (bf16[32,3200]{1,0:T(8,128)(2,1)S(1)}, bf16[32,3200]{1,0:T(8,128)(2,1)S(1)}, u32[]{:S(2)}, u32[]{:S(2)}) collective-permute-start(bf16[32,3200]{1,0:T(8,128)(2,1)S(1)} %get-tuple-element.85), channel_id=1, source_target_pairs={{0,4},{1,5},{2,6},{3,7},{4,0},{5,1},{6,2},{7,3},{8,12},{9,13},{10,... | collective-permute-start | bytes 614408 | tf_op jit(solution)/shard_map/ppermute | solution.py:560
  43.9 10.2 %collective-permute-start.17 = (bf16[32,3200]{1,0:T(8,128)(2,1)S(1)}, bf16[32,3200]{1,0:T(8,128)(2,1)S(1)}, u32[]{:S(2)}, u32[]{:S(2)}) collective-permute-start(bf16[32,3200]{1,0:T(8,128)(2,1)S(1)} %get-tuple-element.87), channel_id=1, source_target_pairs={{0,6},{1,7},{2,4},{3,5},{4,2},{5,3},{6,0},{7,1},{8,14},{9,15},{10,... | collective-permute-start | bytes 614408 | tf_op jit(solution)/shard_map/ppermute | solution.py:560
  55.2 10.3 %collective-permute-start.22 = (bf16[16,3200]{1,0:T(8,128)(2,1)S(1)}, bf16[16,3200]{1,0:T(8,128)(2,1)S(1)}, u32[]{:S(2)}, u32[]{:S(2)}) collective-permute-start(bf16[16,3200]{1,0:T(8,128)(2,1)S(1)} %get-tuple-element.98), channel_id=1, source_target_pairs={{0,8},{1,9},{2,10},{3,11},{4,12},{5,13},{6,14},{7,15},{8,0},{9,1},... | collective-permute-start | bytes 307208 | tf_op jit(solution)/shard_map/ppermute | solution.py:560
  57.9 9.6 %collective-permute-start.24 = (bf16[16,3200]{1,0:T(8,128)(2,1)S(1)}, bf16[16,3200]{1,0:T(8,128)(2,1)S(1)}, u32[]{:S(2)}, u32[]{:S(2)}) collective-permute-start(bf16[16,3200]{1,0:T(8,128)(2,1)S(1)} %get-tuple-element.100), channel_id=1, source_target_pairs={{0,12},{1,13},{2,14},{3,15},{4,8},{5,9},{6,10},{7,11},{8,4},{9,5},... | collective-permute-start | bytes 307208 | tf_op jit(solution)/shard_map/ppermute | solution.py:560
  61.9 7.9 %collective-permute-start.18 = (bf16[16,3200]{1,0:T(8,128)(2,1)S(1)}, bf16[16,3200]{1,0:T(8,128)(2,1)S(1)}, u32[]{:S(2)}, u32[]{:S(2)}) collective-permute-start(bf16[16,3200]{1,0:T(8,128)(2,1)S(1)} %get-tuple-element.94), channel_id=1, source_target_pairs={{0,6},{1,7},{2,4},{3,5},{4,2},{5,3},{6,0},{7,1},{8,14},{9,15},{10,... | collective-permute-start | bytes 307208 | tf_op jit(solution)/shard_map/ppermute | solution.py:560
  62.3 9.1 %collective-permute-start.19 = (bf16[16,3200]{1,0:T(8,128)(2,1)S(1)}, bf16[16,3200]{1,0:T(8,128)(2,1)S(1)}, u32[]{:S(2)}, u32[]{:S(2)}) collective-permute-start(bf16[16,3200]{1,0:T(8,128)(2,1)S(1)} %get-tuple-element.95), channel_id=1, source_target_pairs={{0,4},{1,5},{2,6},{3,7},{4,0},{5,1},{6,2},{7,3},{8,12},{9,13},{10,... | collective-permute-start | bytes 307208 | tf_op jit(solution)/shard_map/ppermute | solution.py:560
  64.5 6.9 %collective-permute-start.20 = (bf16[16,3200]{1,0:T(8,128)(2,1)S(1)}, bf16[16,3200]{1,0:T(8,128)(2,1)S(1)}, u32[]{:S(2)}, u32[]{:S(2)}) collective-permute-start(bf16[16,3200]{1,0:T(8,128)(2,1)S(1)} %get-tuple-element.96), channel_id=1, source_target_pairs={{0,2},{1,3},{2,0},{3,1},{4,6},{5,7},{6,4},{7,5},{8,10},{9,11},{10,... | collective-permute-start | bytes 307208 | tf_op jit(solution)/shard_map/ppermute | solution.py:560
  65.5 9.9 %collective-permute-start.21 = (bf16[16,3200]{1,0:T(8,128)(2,1)S(1)}, bf16[16,3200]{1,0:T(8,128)(2,1)S(1)}, u32[]{:S(2)}, u32[]{:S(2)}) collective-permute-start(bf16[16,3200]{1,0:T(8,128)(2,1)S(1)} %get-tuple-element.97), channel_id=1, source_target_pairs={{0,10},{1,11},{2,8},{3,9},{4,14},{5,15},{6,12},{7,13},{8,2},{9,3},... | collective-permute-start | bytes 307208 | tf_op jit(solution)/shard_map/ppermute | solution.py:560
  67.5 7.9 %collective-permute-start.23 = (bf16[16,3200]{1,0:T(8,128)(2,1)S(1)}, bf16[16,3200]{1,0:T(8,128)(2,1)S(1)}, u32[]{:S(2)}, u32[]{:S(2)}) collective-permute-start(bf16[16,3200]{1,0:T(8,128)(2,1)S(1)} %get-tuple-element.99), channel_id=1, source_target_pairs={{0,14},{1,15},{2,12},{3,13},{4,10},{5,11},{6,8},{7,9},{8,6},{9,7},... | collective-permute-start | bytes 307208 | tf_op jit(solution)/shard_map/ppermute | solution.py:560
  75.6 1.5 %collective-permute-start.25 = (bf16[64,1600]{1,0:T(8,128)(2,1)S(1)}, bf16[64,1600]{1,0:T(8,128)(2,1)S(1)}, u32[]{:S(2)}, u32[]{:S(2)}) collective-permute-start(bf16[64,1600]{1,0:T(8,128)(2,1)S(1)} %get-tuple-element.102), channel_id=1, source_target_pairs={{0,1},{1,0},{2,3},{3,2},{4,5},{5,4},{6,7},{7,6},{8,9},{9,8},{10,11... | collective-permute-start | bytes 614408 | tf_op jit(solution)/shard_map/ppermute | solution.py:560

commit v5 on v4

--- a/solution.py
+++ b/solution.py
@@ -83,6 +83,7 @@
 NEAR = 4
 INCOMING = (0, 1, 2, 3)
 RIGHT_NEAR = (0, 1, 2, 3)
+RIGHT_FAR = (0, 1, 2, 3)
 OUTGOING = (0, 3, 2, 1)
 SUMS_NEAR = (0, 3, 2, 1)
 SUMS_FAR = (1, 0, 3, 2)
@@ -262,11 +263,11 @@
     )
 
 
-def first_far_kernel(
+def first_kernel(
     chunk, own_ref, sibling_ref, valid_ref, gain_ref, chosen_ref, *rest
 ):
-    far_refs = rest[:NEAR]
-    turned_pair_ref, normed_ref, pair_ref = rest[NEAR:]
+    far_refs, near_refs = rest[:NEAR], rest[NEAR : 2 * NEAR]
+    turned_pair_ref, normed_ref, pair_ref = rest[2 * NEAR :]
     place = Place()
     cols = own_ref.shape[1]
     ch = far_refs[0].shape[0]
@@ -277,28 +278,18 @@
     pair_ref[:, pl.ds(sibling_at, cols), :] = sibling_ref[...].astype(F32)
     gain_col = column_of(gain_ref, 0, chunk)
     flat = pair_ref[...].reshape(total, LANES)
-    chosen = chosen_rows(chosen_ref, 0, 1)
+    sides = [chosen_rows(chosen_ref, 0, side) for side in range(2)]
     for lanes in chunks_of(total, chunk):
         pair = flat[lanes].T
         turned_pair_ref[:, lanes] = pair.astype(BF16)
         normed = norm_rows(pair, gain_col[:, : lanes.stop - lanes.start], valid_ref[:, lanes])
         normed_ref[:, lanes] = normed
-        right = project_chunk(normed, chosen)
+        left, right = [project_chunk(normed, chosen) for chosen in sides]
         for d in range(NEAR):
-            far_refs[d][:, lanes] = right[d * ch : (d + 1) * ch]
-
-
-def first_near_kernel(chunk, normed_ref, chosen_ref, *rest):
-    far_refs, near_refs = rest[:NEAR], rest[NEAR:]
-    ch = far_refs[0].shape[0]
-    total = normed_ref.shape[1]
-    chosen = chosen_rows(chosen_ref, 0, 0)
-    for lanes in chunks_of(total, chunk):
-        left = project_chunk(normed_ref[:, lanes], chosen)
-        for d in range(NEAR):
-            near_refs[d][:ch, lanes] = left[d * ch : (d + 1) * ch]
-    for d in range(NEAR):
-        near_refs[d][ch:, :] = far_refs[d][...]
+            rows = slice(d * ch, (d + 1) * ch)
+            far_refs[d][:, lanes] = right[rows]
+            near_refs[d][:ch, lanes] = left[rows]
+            near_refs[d][ch:, lanes] = right[rows]
 
 
 def gate_rows(normed_ref, gate, gating_ref, chunk):
@@ -473,7 +464,8 @@
 
 
 def outgoing_far_kernel(rows, width, *refs):
-    far, left_ref, done = refs[:NEAR], refs[NEAR], refs[NEAR + 1 : NEAR + 3]
+    far = restored(refs[:NEAR], RIGHT_FAR)
+    left_ref, done = refs[NEAR], refs[NEAR + 1 : NEAR + 3]
     outs = refs[NEAR + 3 : 2 * NEAR + 3]
     right_ref, mixed_ref = refs[2 * NEAR + 3 :]
     place = Place()
@@ -552,7 +544,7 @@
     width = 2 * cols
     total = rows * width
     ch = channels // (2 * NEAR)
-    chunk = 13 * LANES
+    chunk = 25 * LANES
 
     def swap(value, dz, dx, core=0):
         flip = dz * n_col + dx * 2 + core
@@ -600,10 +592,10 @@
         out_gain,
         space=pltpu.HBM,
     )
-    *right, pair, normed = call(
-        functools.partial(first_far_kernel, chunk),
-        1.0,
-        [(ch, total)] * NEAR + [wide, wide],
+    out = call(
+        functools.partial(first_kernel, chunk),
+        1.4,
+        [(ch, total)] * NEAR + [(2 * ch, total)] * NEAR + [wide, wide],
         [((rows, width, channels), F32)],
         own,
         sibling,
@@ -611,15 +603,7 @@
         gains,
         chosen,
     )
-    near = call(
-        functools.partial(first_near_kernel, chunk),
-        0.6,
-        [(2 * ch, total)] * NEAR,
-        [],
-        normed,
-        chosen,
-        *right,
-    )
+    right, near, (pair, normed) = out[:NEAR], out[NEAR : 2 * NEAR], out[2 * NEAR :]
     far = swap_all(right, NEAR)
     near = swap_all(near, 0)
     tall = 2 * rows
@@ -646,7 +630,7 @@
         1.2,
         [(ch, total)] * NEAR,
         [sides, side],
-        *far,
+        *ordered(far, RIGHT_FAR),
         left,
         *mixed,
     )

time: 78.6 us -> 78.5 us (level)
    pallas_call x15 -> x14, Pallas kernels: 15.2 us -> 15 us  [call(): pl.pallas_call(kernel, out_shape=[jax.ShapeDtypeStruct(shape, dtype) for...]
where the time goes in v5:
time: 78.5 us; the launch traced here: 78.3 us
  starting transfers between devices  34.9 us (44%)
  waiting for transfers between devices  28.2 us (36%)
  Pallas kernels  15 us (19%)
    ppermute x26, starting transfers between devices, swap(): return lax.ppermute(value, ('row', 'col'), pairs)  34.9 us
    ppermute x26, waiting for transfers between devices, swap(): return lax.ppermute(value, ('row', 'col'), pairs)  28.2 us
    pallas_call x14, Pallas kernels, call(): pl.pallas_call(kernel, out_shape=[jax.ShapeDtypeStruct(shape, dtype) for...  15 us
  transfers between devices with their start and end apart: 26, of which 15 were waited for; matrix products, arithmetic and copies ran while one was open for 0% of the time, Pallas kernels for 10%

profile of v5, /device:TPU:0, one launch (start us, length us, event | category | flops | bytes accessed | tf_op | source)
XLA Modules:
  0.0 78.3 jit_solution(15942991924748169654)
XLA Ops:
  0.5 1.5 %shard_map.73 = (bf16[40,40,128]{2,1,0:T(8,128)(2,1)S(1)}, f32[1,3200]{1,0:T(1,128)S(1)}, bf16[2,256,128]{2,1,0:T(8,128)(2,1)S(1)}, bf16[2,128,128]{2,1,0:T(8,12...) custom-call(bf16[40,40,128]{2,1,0:T(8,128)(2,1)} %pair_in.1, ...), custom_call_target="tpu_custom_call" | custom-call | flops 1650000000 | tf_op jit(solution)/shard_map/pallas_call | solution.py:526
  2.0 1.4 %shard_map.74 = (bf16[16,3200]{1,0:T(8,128)(2,1)S(1)}, bf16[16,3200]{1,0:T(8,128)(2,1)S(1)}, bf16[16,3200]{1,0:T(8,128)(2,1)S(1)}, bf16[16,3200]{1,0:T(8,128)(2,...) custom-call(bf16[40,40,128]{2,1,0:T(8,128)(2,1)S(1)} %get-tuple-elem, ...), custom_call_target="tpu_custom_call" | custom-call | flops 1540000000 | tf_op jit(solution)/shard_map/pallas_call | solution.py:526
  3.4 2.9 %collective-permute-start.5 = (bf16[32,3200]{1,0:T(8,128)(2,1)S(1)}, bf16[32,3200]{1,0:T(8,128)(2,1)S(1)}, u32[]{:S(2)}, u32[]{:S(2)}) collective-permute-start(bf16[32,3200]{1,0:T(8,128)(2,1)S(1)} %get-tuple-element.65), channel_id=1, source_target_pairs={{0,2},{1,3},{2,0},{3,1},{4,6},{5,7},{6,4},{7,5},{8,10},{9,11},{10,... | collective-permute-start | bytes 614408 | tf_op jit(solution)/shard_map/ppermute | solution.py:552
  6.3 1.6 %collective-permute-start.6 = (bf16[32,3200]{1,0:T(8,128)(2,1)S(1)}, bf16[32,3200]{1,0:T(8,128)(2,1)S(1)}, u32[]{:S(2)}, u32[]{:S(2)}) collective-permute-start(bf16[32,3200]{1,0:T(8,128)(2,1)S(1)} %get-tuple-element.66), channel_id=1, source_target_pairs={{0,4},{1,5},{2,6},{3,7},{4,0},{5,1},{6,2},{7,3},{8,12},{9,13},{10,... | collective-permute-start | bytes 614408 | tf_op jit(solution)/shard_map/ppermute | solution.py:552
  7.9 3.0 %collective-permute-start.1 = (bf16[16,3200]{1,0:T(8,128)(2,1)S(1)}, bf16[16,3200]{1,0:T(8,128)(2,1)S(1)}, u32[]{:S(2)}, u32[]{:S(2)}) collective-permute-start(bf16[16,3200]{1,0:T(8,128)(2,1)S(1)} %get-tuple-element.60), channel_id=1, source_target_pairs={{0,8},{1,9},{2,10},{3,11},{4,12},{5,13},{6,14},{7,15},{8,0},{9,1},... | collective-permute-start | bytes 307208 | tf_op jit(solution)/shard_map/ppermute | solution.py:552
  10.9 1.3 %collective-permute-start.2 = (bf16[16,3200]{1,0:T(8,128)(2,1)S(1)}, bf16[16,3200]{1,0:T(8,128)(2,1)S(1)}, u32[]{:S(2)}, u32[]{:S(2)}) collective-permute-start(bf16[16,3200]{1,0:T(8,128)(2,1)S(1)} %get-tuple-element.61), channel_id=1, source_target_pairs={{0,10},{1,11},{2,8},{3,9},{4,14},{5,15},{6,12},{7,13},{8,2},{9,3},... | collective-permute-start | bytes 307208 | tf_op jit(solution)/shard_map/ppermute | solution.py:552
  12.2 3.6 %collective-permute-start.3 = (bf16[16,3200]{1,0:T(8,128)(2,1)S(1)}, bf16[16,3200]{1,0:T(8,128)(2,1)S(1)}, u32[]{:S(2)}, u32[]{:S(2)}) collective-permute-start(bf16[16,3200]{1,0:T(8,128)(2,1)S(1)} %get-tuple-element.62), channel_id=1, source_target_pairs={{0,12},{1,13},{2,14},{3,15},{4,8},{5,9},{6,10},{7,11},{8,4},{9,5},... | collective-permute-start | bytes 307208 | tf_op jit(solution)/shard_map/ppermute | solution.py:552
  15.8 2.9 %collective-permute-done.6.refs_2_ = bf16[32,3200]{1,0:T(8,128)(2,1)S(1)} collective-permute-done((bf16[32,3200]{1,0:T(8,128)(2,1)S(1)}, bf16[32,3200]{1,0:T(8,128)(2,1)S(1)}, u32[]{:S(2)}, u32[]{:S(2)}) %collective-permute-start.6) | collective-permute-done | bytes 204832 | tf_op jit(solution)/shard_map/ppermute | solution.py:552
  18.7 3.1 %collective-permute-start.4 = (bf16[16,3200]{1,0:T(8,128)(2,1)S(1)}, bf16[16,3200]{1,0:T(8,128)(2,1)S(1)}, u32[]{:S(2)}, u32[]{:S(2)}) collective-permute-start(bf16[16,3200]{1,0:T(8,128)(2,1)S(1)} %get-tuple-element.63), channel_id=1, source_target_pairs={{0,14},{1,15},{2,12},{3,13},{4,10},{5,11},{6,8},{7,9},{8,6},{9,7},... | collective-permute-start | bytes 307208 | tf_op jit(solution)/shard_map/ppermute | solution.py:552
  21.8 1.7 %shard_map.75 = (f32[128,3200]{1,0:T(8,128)S(1)}, f32[2,1280,128]{2,1,0:T(8,128)S(1)}, bf16[16,3200]{1,0:T(8,128)(2,1)S(1)}, bf16[16,3200]{1,0:T(8,128)(2,1)S(1)}) custom-call(bf16[32,3200]{1,0:T(8,128)(2,1)S(1)} %get-tuple-element.64.refs_0_, bf16[32,3200]{1,0:T(8,128)(2,1)S(1)} %collective-permute-done.5.refs_1_, ...), custom_call_target="tpu_custom_call" | custom-call | flops 2200000000 | tf_op jit(solution)/shard_map/pallas_call | solution.py:526
  23.5 3.9 %collective-permute-done.3.refs_2_ = bf16[16,3200]{1,0:T(8,128)(2,1)S(1)} collective-permute-done((bf16[16,3200]{1,0:T(8,128)(2,1)S(1)}, bf16[16,3200]{1,0:T(8,128)(2,1)S(1)}, u32[]{:S(2)}, u32[]{:S(2)}) %collective-permute-start.3) | collective-permute-done | bytes 102432 | tf_op jit(solution)/shard_map/ppermute | solution.py:552
  27.4 1.1 %collective-permute-done.4.refs_3_ = bf16[16,3200]{1,0:T(8,128)(2,1)S(1)} collective-permute-done((bf16[16,3200]{1,0:T(8,128)(2,1)S(1)}, bf16[16,3200]{1,0:T(8,128)(2,1)S(1)}, u32[]{:S(2)}, u32[]{:S(2)}) %collective-permute-start.4) | collective-permute-done | bytes 102432 | tf_op jit(solution)/shard_map/ppermute | solution.py:552
  28.5 1.4 %shard_map.76 = (bf16[16,3200]{1,0:T(8,128)(2,1)S(1)}, bf16[16,3200]{1,0:T(8,128)(2,1)S(1)}, bf16[16,3200]{1,0:T(8,128)(2,1)S(1)}, bf16[16,3200]{1,0:T(8,128)(2,1)S(1)}) custom-call(bf16[16,3200]{1,0:T(8,128)(2,1)S(1)} %collective-permute-done.1.refs_0_, bf16[16,3200]{1,0:T(8,128)(2,1)S(1)} %collective-permute-done.2.refs_1_, ...), custom_call_target="tpu_custom_call" | custom-call | flops 1320000000 | tf_op jit(solution)/shard_map/pallas_call | solution.py:526
  29.8 2.9 %collective-permute-start.8 = (bf16[16,3200]{1,0:T(8,128)(2,1)S(1)}, bf16[16,3200]{1,0:T(8,128)(2,1)S(1)}, u32[]{:S(2)}, u32[]{:S(2)}) collective-permute-start(bf16[16,3200]{1,0:T(8,128)(2,1)S(1)} %get-tuple-element.74), channel_id=1, source_target_pairs={{0,6},{1,7},{2,4},{3,5},{4,2},{5,3},{6,0},{7,1},{8,14},{9,15},{10,... | collective-permute-start | bytes 307208 | tf_op jit(solution)/shard_map/ppermute | solution.py:552
  33.7 2.4 %collective-permute-done.8.refs_1_ = bf16[16,3200]{1,0:T(8,128)(2,1)S(1)} collective-permute-done((bf16[16,3200]{1,0:T(8,128)(2,1)S(1)}, bf16[16,3200]{1,0:T(8,128)(2,1)S(1)}, u32[]{:S(2)}, u32[]{:S(2)}) %collective-permute-start.8) | collective-permute-done | bytes 102432 | tf_op jit(solution)/shard_map/ppermute | solution.py:552
  36.1 1.3 %collective-permute-done.9.refs_2_ = bf16[16,3200]{1,0:T(8,128)(2,1)S(1)} collective-permute-done((bf16[16,3200]{1,0:T(8,128)(2,1)S(1)}, bf16[16,3200]{1,0:T(8,128)(2,1)S(1)}, u32[]{:S(2)}, u32[]{:S(2)}) %collective-permute-start.9) | collective-permute-done | bytes 102432 | tf_op jit(solution)/shard_map/ppermute | solution.py:552
  38.9 2.0 %shard_map.77 = (bf16[32,3200]{1,0:T(8,128)(2,1)S(1)}, bf16[32,3200]{1,0:T(8,128)(2,1)S(1)}, bf16[32,3200]{1,0:T(8,128)(2,1)S(1)}, bf16[32,3200]{1,0:T(8,128)(2,...) custom-call(bf16[16,3200]{1,0:T(8,128)(2,1)S(1)} %get-tuple-element.73.refs_0_, ...), custom_call_target="tpu_custom_call" | custom-call | flops 2529999872 | tf_op jit(solution)/shard_map/pallas_call | solution.py:526
  41.0 1.2 %collective-permute-start.15 = (bf16[32,3200]{1,0:T(8,128)(2,1)S(1)}, bf16[32,3200]{1,0:T(8,128)(2,1)S(1)}, u32[]{:S(2)}, u32[]{:S(2)}) collective-permute-start(bf16[32,3200]{1,0:T(8,128)(2,1)S(1)} %get-tuple-element.83), channel_id=1, source_target_pairs={{0,2},{1,3},{2,0},{3,1},{4,6},{5,7},{6,4},{7,5},{8,10},{9,11},{10,... | collective-permute-start | bytes 614408 | tf_op jit(solution)/shard_map/ppermute | solution.py:552
  42.1 1.6 %collective-permute-start.16 = (bf16[32,3200]{1,0:T(8,128)(2,1)S(1)}, bf16[32,3200]{1,0:T(8,128)(2,1)S(1)}, u32[]{:S(2)}, u32[]{:S(2)}) collective-permute-start(bf16[32,3200]{1,0:T(8,128)(2,1)S(1)} %get-tuple-element.85), channel_id=1, source_target_pairs={{0,4},{1,5},{2,6},{3,7},{4,0},{5,1},{6,2},{7,3},{8,12},{9,13},{10,... | collective-permute-start | bytes 614408 | tf_op jit(solution)/shard_map/ppermute | solution.py:552
  44.7 3.6 %collective-permute-done.15.value_ref = bf16[32,3200]{1,0:T(8,128)(2,1)S(1)} collective-permute-done((bf16[32,3200]{1,0:T(8,128)(2,1)S(1)}, bf16[32,3200]{1,0:T(8,128)(2,1)S(1)}, u32[]{:S(2)}, u32[]{:S(2)}) %collective-permute-start.15) | collective-permute-done | bytes 204832 | tf_op jit(solution)/shard_map/ppermute | solution.py:552
  48.5 1.6 %collective-permute-done.16.value_ref = bf16[32,3200]{1,0:T(8,128)(2,1)S(1)} collective-permute-done((bf16[32,3200]{1,0:T(8,128)(2,1)S(1)}, bf16[32,3200]{1,0:T(8,128)(2,1)S(1)}, u32[]{:S(2)}, u32[]{:S(2)}) %collective-permute-start.16) | collective-permute-done | bytes 204832 | tf_op jit(solution)/shard_map/ppermute | solution.py:552
  50.3 3.6 %collective-permute-done.17.value_ref = bf16[32,3200]{1,0:T(8,128)(2,1)S(1)} collective-permute-done((bf16[32,3200]{1,0:T(8,128)(2,1)S(1)}, bf16[32,3200]{1,0:T(8,128)(2,1)S(1)}, u32[]{:S(2)}, u32[]{:S(2)}) %collective-permute-start.17) | collective-permute-done | bytes 204832 | tf_op jit(solution)/shard_map/ppermute | solution.py:552
  55.1 2.7 %collective-permute-start.22 = (bf16[16,3200]{1,0:T(8,128)(2,1)S(1)}, bf16[16,3200]{1,0:T(8,128)(2,1)S(1)}, u32[]{:S(2)}, u32[]{:S(2)}) collective-permute-start(bf16[16,3200]{1,0:T(8,128)(2,1)S(1)} %get-tuple-element.98), channel_id=1, source_target_pairs={{0,8},{1,9},{2,10},{3,11},{4,12},{5,13},{6,14},{7,15},{8,0},{9,1},... | collective-permute-start | bytes 307208 | tf_op jit(solution)/shard_map/ppermute | solution.py:552
  57.8 1.3 %collective-permute-start.24 = (bf16[16,3200]{1,0:T(8,128)(2,1)S(1)}, bf16[16,3200]{1,0:T(8,128)(2,1)S(1)}, u32[]{:S(2)}, u32[]{:S(2)}) collective-permute-start(bf16[16,3200]{1,0:T(8,128)(2,1)S(1)} %get-tuple-element.100), channel_id=1, source_target_pairs={{0,12},{1,13},{2,14},{3,15},{4,8},{5,9},{6,10},{7,11},{8,4},{9,5},... | collective-permute-start | bytes 307208 | tf_op jit(solution)/shard_map/ppermute | solution.py:552
  59.1 2.7 %shard_map.82 = (bf16[16,3200]{1,0:T(8,128)(2,1)S(1)}, bf16[16,3200]{1,0:T(8,128)(2,1)S(1)}, bf16[16,3200]{1,0:T(8,128)(2,1)S(1)}, bf16[16,3200]{1,0:T(8,128)(2,...) custom-call(f32[640,128]{1,0:T(8,128)S(1)} %get-tuple-element.82.earlier_ref.refs_0_, ...), custom_call_target="tpu_custom_call" | custom-call | flops 2750000128 | tf_op jit(solution)/shard_map/pallas_call | solution.py:526
  62.2 2.2 %collective-permute-start.19 = (bf16[16,3200]{1,0:T(8,128)(2,1)S(1)}, bf16[16,3200]{1,0:T(8,128)(2,1)S(1)}, u32[]{:S(2)}, u32[]{:S(2)}) collective-permute-start(bf16[16,3200]{1,0:T(8,128)(2,1)S(1)} %get-tuple-element.95), channel_id=1, source_target_pairs={{0,4},{1,5},{2,6},{3,7},{4,0},{5,1},{6,2},{7,3},{8,12},{9,13},{10,... | collective-permute-start | bytes 307208 | tf_op jit(solution)/shard_map/ppermute | solution.py:552
  65.4 2.0 %collective-permute-start.21 = (bf16[16,3200]{1,0:T(8,128)(2,1)S(1)}, bf16[16,3200]{1,0:T(8,128)(2,1)S(1)}, u32[]{:S(2)}, u32[]{:S(2)}) collective-permute-start(bf16[16,3200]{1,0:T(8,128)(2,1)S(1)} %get-tuple-element.97), channel_id=1, source_target_pairs={{0,10},{1,11},{2,8},{3,9},{4,14},{5,15},{6,12},{7,13},{8,2},{9,3},... | collective-permute-start | bytes 307208 | tf_op jit(solution)/shard_map/ppermute | solution.py:552
  67.4 1.5 %collective-permute-start.23 = (bf16[16,3200]{1,0:T(8,128)(2,1)S(1)}, bf16[16,3200]{1,0:T(8,128)(2,1)S(1)}, u32[]{:S(2)}, u32[]{:S(2)}) collective-permute-start(bf16[16,3200]{1,0:T(8,128)(2,1)S(1)} %get-tuple-element.99), channel_id=1, source_target_pairs={{0,14},{1,15},{2,12},{3,13},{4,10},{5,11},{6,8},{7,9},{8,6},{9,7},... | collective-permute-start | bytes 307208 | tf_op jit(solution)/shard_map/ppermute | solution.py:552
  69.7 1.6 %collective-permute-done.19.refs_2_ = bf16[16,3200]{1,0:T(8,128)(2,1)S(1)} collective-permute-done((bf16[16,3200]{1,0:T(8,128)(2,1)S(1)}, bf16[16,3200]{1,0:T(8,128)(2,1)S(1)}, u32[]{:S(2)}, u32[]{:S(2)}) %collective-permute-start.19) | collective-permute-done | bytes 102432 | tf_op jit(solution)/shard_map/ppermute | solution.py:552
  71.3 4.1 %collective-permute-done.21.refs_4_ = bf16[16,3200]{1,0:T(8,128)(2,1)S(1)} collective-permute-done((bf16[16,3200]{1,0:T(8,128)(2,1)S(1)}, bf16[16,3200]{1,0:T(8,128)(2,1)S(1)}, u32[]{:S(2)}, u32[]{:S(2)}) %collective-permute-start.21) | collective-permute-done | bytes 102432 | tf_op jit(solution)/shard_map/ppermute | solution.py:552
  75.6 1.2 %shard_map.85 = (f32[1600,128]{1,0:T(8,128)S(1)}, f32[1600,128]{1,0:T(8,128)S(1)}) custom-call(bf16[128,3200]{1,0:T(8,128)(2,1)S(1)} %get-tuple-element.103.after_ref, bf16[128,3200]{1,0:T(8,128)(2,1)S(1)} %get-tuple-element.104.normed_ref, bf16[2,128,128]{2,1,0:T(8,128)(2,1)S(1)} %get-tuple-element.69.refs_5_.gate_ref), custom_call_target="tpu_custom_call" | custom-call | flops 2200000000 | tf_op jit(solution)/shard_map/pallas_call | solution.py:526
  77.0 1.3 %shard_map.86 = bf16[1600,128]{1,0:T(8,128)(2,1)} custom-call(bf16[64,1600]{1,0:T(8,128)(2,1)S(1)} %get-tuple-element.101.keep_ref, bf16[64,1600]{1,0:T(8,128)(2,1)S(1)} %collective-permute-done.25.got_ref, f32[1600,128]{1,0:T(8,128)S(1)} %get-tuple-element.105.own_ref, f32[1600,128]{1,0:T(8,128)S(1)} %get-tuple-element.106.gating_ref, ...), custom_call_target="tpu_custom_call" | custom-call | flops 1100000000 | tf_op jit(solution)/shard_map/pallas_call | solution.py:526
  (34 shorter events, 8.1 us)
Async XLA Ops:
  0.0 2.0 %collective-permute-start = (bf16[40,40,128]{2,1,0:T(8,128)(2,1)}, bf16[40,40,128]{2,1,0:T(8,128)(2,1)S(1)}, u32[]{:S(2)}, u32[]{:S(2)}) collective-permute-start(bf16[40,40,128]{2,1,0:T(8,128)(2,1)} %pair_in.1), channel_id=1, source_target_pairs={{0,1},{1,0},{2,3},{3,2},{4,5},{5,4},{6,7},{7,6},{8,9},{9,8},{10,11... | collective-permute-start | bytes 1228808 | tf_op jit(solution)/shard_map/ppermute | solution.py:552
  3.4 8.8 %collective-permute-start.5 = (bf16[32,3200]{1,0:T(8,128)(2,1)S(1)}, bf16[32,3200]{1,0:T(8,128)(2,1)S(1)}, u32[]{:S(2)}, u32[]{:S(2)}) collective-permute-start(bf16[32,3200]{1,0:T(8,128)(2,1)S(1)} %get-tuple-element.65), channel_id=1, source_target_pairs={{0,2},{1,3},{2,0},{3,1},{4,6},{5,7},{6,4},{7,5},{8,10},{9,11},{10,... | collective-permute-start | bytes 614408 | tf_op jit(solution)/shard_map/ppermute | solution.py:552
  6.3 12.3 %collective-permute-start.6 = (bf16[32,3200]{1,0:T(8,128)(2,1)S(1)}, bf16[32,3200]{1,0:T(8,128)(2,1)S(1)}, u32[]{:S(2)}, u32[]{:S(2)}) collective-permute-start(bf16[32,3200]{1,0:T(8,128)(2,1)S(1)} %get-tuple-element.66), channel_id=1, source_target_pairs={{0,4},{1,5},{2,6},{3,7},{4,0},{5,1},{6,2},{7,3},{8,12},{9,13},{10,... | collective-permute-start | bytes 614408 | tf_op jit(solution)/shard_map/ppermute | solution.py:552
  7.9 13.8 %collective-permute-start.7 = (bf16[32,3200]{1,0:T(8,128)(2,1)S(1)}, bf16[32,3200]{1,0:T(8,128)(2,1)S(1)}, u32[]{:S(2)}, u32[]{:S(2)}) collective-permute-start(bf16[32,3200]{1,0:T(8,128)(2,1)S(1)} %get-tuple-element.67), channel_id=1, source_target_pairs={{0,6},{1,7},{2,4},{3,5},{4,2},{5,3},{6,0},{7,1},{8,14},{9,15},{10,... | collective-permute-start | bytes 614408 | tf_op jit(solution)/shard_map/ppermute | solution.py:552
  7.9 15.5 %collective-permute-start.1 = (bf16[16,3200]{1,0:T(8,128)(2,1)S(1)}, bf16[16,3200]{1,0:T(8,128)(2,1)S(1)}, u32[]{:S(2)}, u32[]{:S(2)}) collective-permute-start(bf16[16,3200]{1,0:T(8,128)(2,1)S(1)} %get-tuple-element.60), channel_id=1, source_target_pairs={{0,8},{1,9},{2,10},{3,11},{4,12},{5,13},{6,14},{7,15},{8,0},{9,1},... | collective-permute-start | bytes 307208 | tf_op jit(solution)/shard_map/ppermute | solution.py:552
  10.9 12.5 %collective-permute-start.2 = (bf16[16,3200]{1,0:T(8,128)(2,1)S(1)}, bf16[16,3200]{1,0:T(8,128)(2,1)S(1)}, u32[]{:S(2)}, u32[]{:S(2)}) collective-permute-start(bf16[16,3200]{1,0:T(8,128)(2,1)S(1)} %get-tuple-element.61), channel_id=1, source_target_pairs={{0,10},{1,11},{2,8},{3,9},{4,14},{5,15},{6,12},{7,13},{8,2},{9,3},... | collective-permute-start | bytes 307208 | tf_op jit(solution)/shard_map/ppermute | solution.py:552
  12.2 15.2 %collective-permute-start.3 = (bf16[16,3200]{1,0:T(8,128)(2,1)S(1)}, bf16[16,3200]{1,0:T(8,128)(2,1)S(1)}, u32[]{:S(2)}, u32[]{:S(2)}) collective-permute-start(bf16[16,3200]{1,0:T(8,128)(2,1)S(1)} %get-tuple-element.62), channel_id=1, source_target_pairs={{0,12},{1,13},{2,14},{3,15},{4,8},{5,9},{6,10},{7,11},{8,4},{9,5},... | collective-permute-start | bytes 307208 | tf_op jit(solution)/shard_map/ppermute | solution.py:552
  18.7 9.8 %collective-permute-start.4 = (bf16[16,3200]{1,0:T(8,128)(2,1)S(1)}, bf16[16,3200]{1,0:T(8,128)(2,1)S(1)}, u32[]{:S(2)}, u32[]{:S(2)}) collective-permute-start(bf16[16,3200]{1,0:T(8,128)(2,1)S(1)} %get-tuple-element.63), channel_id=1, source_target_pairs={{0,14},{1,15},{2,12},{3,13},{4,10},{5,11},{6,8},{7,9},{8,6},{9,7},... | collective-permute-start | bytes 307208 | tf_op jit(solution)/shard_map/ppermute | solution.py:552
  29.8 6.3 %collective-permute-start.8 = (bf16[16,3200]{1,0:T(8,128)(2,1)S(1)}, bf16[16,3200]{1,0:T(8,128)(2,1)S(1)}, u32[]{:S(2)}, u32[]{:S(2)}) collective-permute-start(bf16[16,3200]{1,0:T(8,128)(2,1)S(1)} %get-tuple-element.74), channel_id=1, source_target_pairs={{0,6},{1,7},{2,4},{3,5},{4,2},{5,3},{6,0},{7,1},{8,14},{9,15},{10,... | collective-permute-start | bytes 307208 | tf_op jit(solution)/shard_map/ppermute | solution.py:552
  32.7 4.8 %collective-permute-start.9 = (bf16[16,3200]{1,0:T(8,128)(2,1)S(1)}, bf16[16,3200]{1,0:T(8,128)(2,1)S(1)}, u32[]{:S(2)}, u32[]{:S(2)}) collective-permute-start(bf16[16,3200]{1,0:T(8,128)(2,1)S(1)} %get-tuple-element.75), channel_id=1, source_target_pairs={{0,4},{1,5},{2,6},{3,7},{4,0},{5,1},{6,2},{7,3},{8,12},{9,13},{10,... | collective-permute-start | bytes 307208 | tf_op jit(solution)/shard_map/ppermute | solution.py:552
  32.9 4.7 %collective-permute-start.10 = (bf16[16,3200]{1,0:T(8,128)(2,1)S(1)}, bf16[16,3200]{1,0:T(8,128)(2,1)S(1)}, u32[]{:S(2)}, u32[]{:S(2)}) collective-permute-start(bf16[16,3200]{1,0:T(8,128)(2,1)S(1)} %get-tuple-element.76), channel_id=1, source_target_pairs={{0,2},{1,3},{2,0},{3,1},{4,6},{5,7},{6,4},{7,5},{8,10},{9,11},{10,... | collective-permute-start | bytes 307208 | tf_op jit(solution)/shard_map/ppermute | solution.py:552
  33.7 4.3 %collective-permute-start.11 = (bf16[16,3200]{1,0:T(8,128)(2,1)S(1)}, bf16[16,3200]{1,0:T(8,128)(2,1)S(1)}, u32[]{:S(2)}, u32[]{:S(2)}) collective-permute-start(bf16[16,3200]{1,0:T(8,128)(2,1)S(1)} %get-tuple-element.73.refs_0_), channel_id=1, source_target_pairs={{0,1},{1,0},{2,3},{3,2},{4,5},{5,4},{6,7},{7,6},{8,9},{9,8},{10,11... | collective-permute-start | bytes 307208 | tf_op jit(solution)/shard_map/ppermute | solution.py:552
  36.1 1.9 %collective-permute-start.12 = (bf16[16,3200]{1,0:T(8,128)(2,1)S(1)}, bf16[16,3200]{1,0:T(8,128)(2,1)S(1)}, u32[]{:S(2)}, u32[]{:S(2)}) collective-permute-start(bf16[16,3200]{1,0:T(8,128)(2,1)S(1)} %collective-permute-done.8.refs_1_), channel_id=1, source_target_pairs={{0,1},{1,0},{2,3},{3,2},{4,5},{5,4},{6,7},{7,6},{8,9},{9,8},{10,11... | collective-permute-start | bytes 307208 | tf_op jit(solution)/shard_map/ppermute | solution.py:552
  37.5 1.3 %collective-permute-start.13 = (bf16[16,3200]{1,0:T(8,128)(2,1)S(1)}, bf16[16,3200]{1,0:T(8,128)(2,1)S(1)}, u32[]{:S(2)}, u32[]{:S(2)}) collective-permute-start(bf16[16,3200]{1,0:T(8,128)(2,1)S(1)} %collective-permute-done.9.refs_2_), channel_id=1, source_target_pairs={{0,1},{1,0},{2,3},{3,2},{4,5},{5,4},{6,7},{7,6},{8,9},{9,8},{10,11... | collective-permute-start | bytes 307208 | tf_op jit(solution)/shard_map/ppermute | solution.py:552
  37.5 1.4 %collective-permute-start.14 = (bf16[16,3200]{1,0:T(8,128)(2,1)S(1)}, bf16[16,3200]{1,0:T(8,128)(2,1)S(1)}, u32[]{:S(2)}, u32[]{:S(2)}) collective-permute-start(bf16[16,3200]{1,0:T(8,128)(2,1)S(1)} %collective-permute-done.10.refs_3_), channel_id=1, source_target_pairs={{0,1},{1,0},{2,3},{3,2},{4,5},{5,4},{6,7},{7,6},{8,9},{9,8},{10,11... | collective-permute-start | bytes 307208 | tf_op jit(solution)/shard_map/ppermute | solution.py:552
  41.0 7.4 %collective-permute-start.15 = (bf16[32,3200]{1,0:T(8,128)(2,1)S(1)}, bf16[32,3200]{1,0:T(8,128)(2,1)S(1)}, u32[]{:S(2)}, u32[]{:S(2)}) collective-permute-start(bf16[32,3200]{1,0:T(8,128)(2,1)S(1)} %get-tuple-element.83), channel_id=1, source_target_pairs={{0,2},{1,3},{2,0},{3,1},{4,6},{5,7},{6,4},{7,5},{8,10},{9,11},{10,... | collective-permute-start | bytes 614408 | tf_op jit(solution)/shard_map/ppermute | solution.py:552
  42.1 8.0 %collective-permute-start.16 = (bf16[32,3200]{1,0:T(8,128)(2,1)S(1)}, bf16[32,3200]{1,0:T(8,128)(2,1)S(1)}, u32[]{:S(2)}, u32[]{:S(2)}) collective-permute-start(bf16[32,3200]{1,0:T(8,128)(2,1)S(1)} %get-tuple-element.85), channel_id=1, source_target_pairs={{0,4},{1,5},{2,6},{3,7},{4,0},{5,1},{6,2},{7,3},{8,12},{9,13},{10,... | collective-permute-start | bytes 614408 | tf_op jit(solution)/shard_map/ppermute | solution.py:552
  43.8 10.1 %collective-permute-start.17 = (bf16[32,3200]{1,0:T(8,128)(2,1)S(1)}, bf16[32,3200]{1,0:T(8,128)(2,1)S(1)}, u32[]{:S(2)}, u32[]{:S(2)}) collective-permute-start(bf16[32,3200]{1,0:T(8,128)(2,1)S(1)} %get-tuple-element.87), channel_id=1, source_target_pairs={{0,6},{1,7},{2,4},{3,5},{4,2},{5,3},{6,0},{7,1},{8,14},{9,15},{10,... | collective-permute-start | bytes 614408 | tf_op jit(solution)/shard_map/ppermute | solution.py:552
  55.1 10.3 %collective-permute-start.22 = (bf16[16,3200]{1,0:T(8,128)(2,1)S(1)}, bf16[16,3200]{1,0:T(8,128)(2,1)S(1)}, u32[]{:S(2)}, u32[]{:S(2)}) collective-permute-start(bf16[16,3200]{1,0:T(8,128)(2,1)S(1)} %get-tuple-element.98), channel_id=1, source_target_pairs={{0,8},{1,9},{2,10},{3,11},{4,12},{5,13},{6,14},{7,15},{8,0},{9,1},... | collective-permute-start | bytes 307208 | tf_op jit(solution)/shard_map/ppermute | solution.py:552
  57.8 9.6 %collective-permute-start.24 = (bf16[16,3200]{1,0:T(8,128)(2,1)S(1)}, bf16[16,3200]{1,0:T(8,128)(2,1)S(1)}, u32[]{:S(2)}, u32[]{:S(2)}) collective-permute-start(bf16[16,3200]{1,0:T(8,128)(2,1)S(1)} %get-tuple-element.100), channel_id=1, source_target_pairs={{0,12},{1,13},{2,14},{3,15},{4,8},{5,9},{6,10},{7,11},{8,4},{9,5},... | collective-permute-start | bytes 307208 | tf_op jit(solution)/shard_map/ppermute | solution.py:552
  61.8 7.9 %collective-permute-start.18 = (bf16[16,3200]{1,0:T(8,128)(2,1)S(1)}, bf16[16,3200]{1,0:T(8,128)(2,1)S(1)}, u32[]{:S(2)}, u32[]{:S(2)}) collective-permute-start(bf16[16,3200]{1,0:T(8,128)(2,1)S(1)} %get-tuple-element.94), channel_id=1, source_target_pairs={{0,6},{1,7},{2,4},{3,5},{4,2},{5,3},{6,0},{7,1},{8,14},{9,15},{10,... | collective-permute-start | bytes 307208 | tf_op jit(solution)/shard_map/ppermute | solution.py:552
  62.2 9.1 %collective-permute-start.19 = (bf16[16,3200]{1,0:T(8,128)(2,1)S(1)}, bf16[16,3200]{1,0:T(8,128)(2,1)S(1)}, u32[]{:S(2)}, u32[]{:S(2)}) collective-permute-start(bf16[16,3200]{1,0:T(8,128)(2,1)S(1)} %get-tuple-element.95), channel_id=1, source_target_pairs={{0,4},{1,5},{2,6},{3,7},{4,0},{5,1},{6,2},{7,3},{8,12},{9,13},{10,... | collective-permute-start | bytes 307208 | tf_op jit(solution)/shard_map/ppermute | solution.py:552
  64.3 6.9 %collective-permute-start.20 = (bf16[16,3200]{1,0:T(8,128)(2,1)S(1)}, bf16[16,3200]{1,0:T(8,128)(2,1)S(1)}, u32[]{:S(2)}, u32[]{:S(2)}) collective-permute-start(bf16[16,3200]{1,0:T(8,128)(2,1)S(1)} %get-tuple-element.96), channel_id=1, source_target_pairs={{0,2},{1,3},{2,0},{3,1},{4,6},{5,7},{6,4},{7,5},{8,10},{9,11},{10,... | collective-permute-start | bytes 307208 | tf_op jit(solution)/shard_map/ppermute | solution.py:552
  65.4 9.9 %collective-permute-start.21 = (bf16[16,3200]{1,0:T(8,128)(2,1)S(1)}, bf16[16,3200]{1,0:T(8,128)(2,1)S(1)}, u32[]{:S(2)}, u32[]{:S(2)}) collective-permute-start(bf16[16,3200]{1,0:T(8,128)(2,1)S(1)} %get-tuple-element.97), channel_id=1, source_target_pairs={{0,10},{1,11},{2,8},{3,9},{4,14},{5,15},{6,12},{7,13},{8,2},{9,3},... | collective-permute-start | bytes 307208 | tf_op jit(solution)/shard_map/ppermute | solution.py:552
  67.4 7.9 %collective-permute-start.23 = (bf16[16,3200]{1,0:T(8,128)(2,1)S(1)}, bf16[16,3200]{1,0:T(8,128)(2,1)S(1)}, u32[]{:S(2)}, u32[]{:S(2)}) collective-permute-start(bf16[16,3200]{1,0:T(8,128)(2,1)S(1)} %get-tuple-element.99), channel_id=1, source_target_pairs={{0,14},{1,15},{2,12},{3,13},{4,10},{5,11},{6,8},{7,9},{8,6},{9,7},... | collective-permute-start | bytes 307208 | tf_op jit(solution)/shard_map/ppermute | solution.py:552
  75.5 1.5 %collective-permute-start.25 = (bf16[64,1600]{1,0:T(8,128)(2,1)S(1)}, bf16[64,1600]{1,0:T(8,128)(2,1)S(1)}, u32[]{:S(2)}, u32[]{:S(2)}) collective-permute-start(bf16[64,1600]{1,0:T(8,128)(2,1)S(1)} %get-tuple-element.102), channel_id=1, source_target_pairs={{0,1},{1,0},{2,3},{3,2},{4,5},{5,4},{6,7},{7,6},{8,9},{9,8},{10,11... | collective-permute-start | bytes 614408 | tf_op jit(solution)/shard_map/ppermute | solution.py:552

commit v6 on v5

--- a/solution.py
+++ b/solution.py
@@ -464,19 +464,20 @@
 
 
 def outgoing_far_kernel(rows, width, *refs):
-    far = restored(refs[:NEAR], RIGHT_FAR)
-    left_ref, done = refs[NEAR], refs[NEAR + 1 : NEAR + 3]
+    far, left_ref, done = refs[:NEAR], refs[NEAR], refs[NEAR + 1 : NEAR + 3]
     outs = refs[NEAR + 3 : 2 * NEAR + 3]
-    right_ref, mixed_ref = refs[2 * NEAR + 3 :]
-    place = Place()
-    ch = far[0].shape[0]
+    mixed_ref = refs[2 * NEAR + 3]
+    place = Place()
+    ch = outs[0].shape[0]
     lane = lane_of(ch)
-    for d in range(NEAR):
-        dl, dx = divmod(d, 2)
-        low = jnp.bitwise_xor(lax.rem(place.z, 2), dl)
-        begin = pl.multiple_of(low * (rows * ch), 16)
-        unpack(far[d][...], right_ref.at[dx], begin, rows, width, lane)
-    outgoing_multiply(left_ref, [[right_ref.at[0]], [right_ref.at[1]]], mixed_ref, ch)
+    low = lax.rem(place.z, 2)
+    for flip in range(2):
+
+        @pl.when(low == flip)
+        def _(flip=flip):
+            right = [[far[2 * (zl ^ flip) + dx] for zl in range(2)] for dx in range(2)]
+            outgoing_multiply(left_ref, right, mixed_ref, ch)
+
     same = jnp.bitwise_xor(place.half, place.x)
     for dx in range(2):
 
@@ -625,12 +626,17 @@
             functools.partial(unpack_kernel, rows, width), 0.2, [block] * operands, [], value, earlier
         )
 
+    blocks = []
+    earlier = gating
+    for value in far:
+        blocks.append(unpacked(value, 1, earlier)[0])
+        earlier = blocks[-1]
     mixed = call(
         functools.partial(outgoing_far_kernel, rows, width),
-        1.2,
+        1.0,
         [(ch, total)] * NEAR,
-        [sides, side],
-        *ordered(far, RIGHT_FAR),
+        [side],
+        *blocks,
         left,
         *mixed,
     )
@@ -638,7 +644,7 @@
     other = [swap(part, 0, 0, 1) for part in mixed]
 
     *near, pair, normed = call(
-        functools.partial(middle_kernel, chunk),
+        functools.partial(middle_kernel, 13 * LANES),
         2.3,
         [(2 * ch, total)] * NEAR + [wide, wide],
         [(wide, BF16)],

time: 78.5 us -> 78.5 us (level)
    pallas_call x14 -> x18, Pallas kernels: 15 us -> 15 us  [call(): pl.pallas_call(kernel, out_shape=[jax.ShapeDtypeStruct(shape, dtype) for...]
  transfers between devices with their start and end apart: 26 -> 26, of which waited for: 15 -> 17; matrix products, arithmetic and copies ran while one was open for 0% -> 0% of each run, Pallas kernels for 10% -> 10%
where the time goes in v6:
time: 78.5 us; the launch traced here: 78.3 us
  starting transfers between devices  34.8 us (44%)
  waiting for transfers between devices  28.3 us (36%)
  Pallas kernels  15 us (19%)
    ppermute x26, starting transfers between devices, swap(): return lax.ppermute(value, ('row', 'col'), pairs)  34.8 us
    ppermute x26, waiting for transfers between devices, swap(): return lax.ppermute(value, ('row', 'col'), pairs)  28.3 us
    pallas_call x18, Pallas kernels, call(): pl.pallas_call(kernel, out_shape=[jax.ShapeDtypeStruct(shape, dtype) for...  15 us
  transfers between devices with their start and end apart: 26, of which 17 were waited for; matrix products, arithmetic and copies ran while one was open for 0% of the time, Pallas kernels for 10%

profile of v6, /device:TPU:0, one launch (start us, length us, event | category | flops | bytes accessed | tf_op | source)
XLA Modules:
  0.0 78.3 jit_solution(631419704300303634)
XLA Ops:
  0.5 1.5 %shard_map.73 = (bf16[40,40,128]{2,1,0:T(8,128)(2,1)S(1)}, f32[1,3200]{1,0:T(1,128)S(1)}, bf16[2,256,128]{2,1,0:T(8,128)(2,1)S(1)}, bf16[2,128,128]{2,1,0:T(8,12...) custom-call(bf16[40,40,128]{2,1,0:T(8,128)(2,1)} %pair_in.1, ...), custom_call_target="tpu_custom_call" | custom-call | flops 1650000000 | tf_op jit(solution)/shard_map/pallas_call | solution.py:527
  2.0 1.4 %shard_map.74 = (bf16[16,3200]{1,0:T(8,128)(2,1)S(1)}, bf16[16,3200]{1,0:T(8,128)(2,1)S(1)}, bf16[16,3200]{1,0:T(8,128)(2,1)S(1)}, bf16[16,3200]{1,0:T(8,128)(2,...) custom-call(bf16[40,40,128]{2,1,0:T(8,128)(2,1)S(1)} %get-tuple-elem, ...), custom_call_target="tpu_custom_call" | custom-call | flops 1540000000 | tf_op jit(solution)/shard_map/pallas_call | solution.py:527
  3.4 2.9 %collective-permute-start.2 = (bf16[32,3200]{1,0:T(8,128)(2,1)S(1)}, bf16[32,3200]{1,0:T(8,128)(2,1)S(1)}, u32[]{:S(2)}, u32[]{:S(2)}) collective-permute-start(bf16[32,3200]{1,0:T(8,128)(2,1)S(1)} %get-tuple-element.62), channel_id=1, source_target_pairs={{0,2},{1,3},{2,0},{3,1},{4,6},{5,7},{6,4},{7,5},{8,10},{9,11},{10,... | collective-permute-start | bytes 614408 | tf_op jit(solution)/shard_map/ppermute | solution.py:553
  6.4 1.6 %collective-permute-start.3 = (bf16[32,3200]{1,0:T(8,128)(2,1)S(1)}, bf16[32,3200]{1,0:T(8,128)(2,1)S(1)}, u32[]{:S(2)}, u32[]{:S(2)}) collective-permute-start(bf16[32,3200]{1,0:T(8,128)(2,1)S(1)} %get-tuple-element.63), channel_id=1, source_target_pairs={{0,4},{1,5},{2,6},{3,7},{4,0},{5,1},{6,2},{7,3},{8,12},{9,13},{10,... | collective-permute-start | bytes 614408 | tf_op jit(solution)/shard_map/ppermute | solution.py:553
  7.9 3.0 %collective-permute-start.1 = (bf16[16,3200]{1,0:T(8,128)(2,1)S(1)}, bf16[16,3200]{1,0:T(8,128)(2,1)S(1)}, u32[]{:S(2)}, u32[]{:S(2)}) collective-permute-start(bf16[16,3200]{1,0:T(8,128)(2,1)S(1)} %get-tuple-element.60), channel_id=1, source_target_pairs={{0,8},{1,9},{2,10},{3,11},{4,12},{5,13},{6,14},{7,15},{8,0},{9,1},... | collective-permute-start | bytes 307208 | tf_op jit(solution)/shard_map/ppermute | solution.py:553
  10.9 1.3 %collective-permute-start.5 = (bf16[16,3200]{1,0:T(8,128)(2,1)S(1)}, bf16[16,3200]{1,0:T(8,128)(2,1)S(1)}, u32[]{:S(2)}, u32[]{:S(2)}) collective-permute-start(bf16[16,3200]{1,0:T(8,128)(2,1)S(1)} %get-tuple-element.68), channel_id=1, source_target_pairs={{0,10},{1,11},{2,8},{3,9},{4,14},{5,15},{6,12},{7,13},{8,2},{9,3},... | collective-permute-start | bytes 307208 | tf_op jit(solution)/shard_map/ppermute | solution.py:553
  12.2 3.6 %collective-permute-start.6 = (bf16[16,3200]{1,0:T(8,128)(2,1)S(1)}, bf16[16,3200]{1,0:T(8,128)(2,1)S(1)}, u32[]{:S(2)}, u32[]{:S(2)}) collective-permute-start(bf16[16,3200]{1,0:T(8,128)(2,1)S(1)} %get-tuple-element.69), channel_id=1, source_target_pairs={{0,12},{1,13},{2,14},{3,15},{4,8},{5,9},{6,10},{7,11},{8,4},{9,5},... | collective-permute-start | bytes 307208 | tf_op jit(solution)/shard_map/ppermute | solution.py:553
  15.8 2.9 %collective-permute-done.3.refs_2_ = bf16[32,3200]{1,0:T(8,128)(2,1)S(1)} collective-permute-done((bf16[32,3200]{1,0:T(8,128)(2,1)S(1)}, bf16[32,3200]{1,0:T(8,128)(2,1)S(1)}, u32[]{:S(2)}, u32[]{:S(2)}) %collective-permute-start.3) | collective-permute-done | bytes 204832 | tf_op jit(solution)/shard_map/ppermute | solution.py:553
  18.7 3.1 %collective-permute-start.7 = (bf16[16,3200]{1,0:T(8,128)(2,1)S(1)}, bf16[16,3200]{1,0:T(8,128)(2,1)S(1)}, u32[]{:S(2)}, u32[]{:S(2)}) collective-permute-start(bf16[16,3200]{1,0:T(8,128)(2,1)S(1)} %get-tuple-element.70), channel_id=1, source_target_pairs={{0,14},{1,15},{2,12},{3,13},{4,10},{5,11},{6,8},{7,9},{8,6},{9,7},... | collective-permute-start | bytes 307208 | tf_op jit(solution)/shard_map/ppermute | solution.py:553
  21.8 1.7 %shard_map.75 = (f32[128,3200]{1,0:T(8,128)S(1)}, f32[2,1280,128]{2,1,0:T(8,128)S(1)}, bf16[16,3200]{1,0:T(8,128)(2,1)S(1)}, bf16[16,3200]{1,0:T(8,128)(2,1)S(1)}) custom-call(bf16[32,3200]{1,0:T(8,128)(2,1)S(1)} %get-tuple-element.61.refs_0_, bf16[32,3200]{1,0:T(8,128)(2,1)S(1)} %collective-permute-done.2.refs_1_, ...), custom_call_target="tpu_custom_call" | custom-call | flops 2200000000 | tf_op jit(solution)/shard_map/pallas_call | solution.py:527
  23.8 3.6 %collective-permute-done.6.value_ref = bf16[16,3200]{1,0:T(8,128)(2,1)S(1)} collective-permute-done((bf16[16,3200]{1,0:T(8,128)(2,1)S(1)}, bf16[16,3200]{1,0:T(8,128)(2,1)S(1)}, u32[]{:S(2)}, u32[]{:S(2)}) %collective-permute-start.6) | collective-permute-done | bytes 102432 | tf_op jit(solution)/shard_map/ppermute | solution.py:553
  28.6 1.1 %shard_map.80 = (bf16[16,3200]{1,0:T(8,128)(2,1)S(1)}, bf16[16,3200]{1,0:T(8,128)(2,1)S(1)}, bf16[16,3200]{1,0:T(8,128)(2,1)S(1)}, bf16[16,3200]{1,0:T(8,128)(2,1)S(1)}) custom-call(f32[640,128]{1,0:T(8,128)S(1)} %shard_map.76.earlier_ref.refs_0_, f32[640,128]{1,0:T(8,128)S(1)} %shard_map.77.earlier_ref.refs_1_, ...), custom_call_target="tpu_custom_call" | custom-call | flops 1100000000 | tf_op jit(solution)/shard_map/pallas_call | solution.py:527
  29.7 2.9 %collective-permute-start.8 = (bf16[16,3200]{1,0:T(8,128)(2,1)S(1)}, bf16[16,3200]{1,0:T(8,128)(2,1)S(1)}, u32[]{:S(2)}, u32[]{:S(2)}) collective-permute-start(bf16[16,3200]{1,0:T(8,128)(2,1)S(1)} %get-tuple-element.75), channel_id=1, source_target_pairs={{0,6},{1,7},{2,4},{3,5},{4,2},{5,3},{6,0},{7,1},{8,14},{9,15},{10,... | collective-permute-start | bytes 307208 | tf_op jit(solution)/shard_map/ppermute | solution.py:553
  33.6 2.3 %collective-permute-done.8.refs_1_ = bf16[16,3200]{1,0:T(8,128)(2,1)S(1)} collective-permute-done((bf16[16,3200]{1,0:T(8,128)(2,1)S(1)}, bf16[16,3200]{1,0:T(8,128)(2,1)S(1)}, u32[]{:S(2)}, u32[]{:S(2)}) %collective-permute-start.8) | collective-permute-done | bytes 102432 | tf_op jit(solution)/shard_map/ppermute | solution.py:553
  36.0 1.4 %collective-permute-done.9.refs_2_ = bf16[16,3200]{1,0:T(8,128)(2,1)S(1)} collective-permute-done((bf16[16,3200]{1,0:T(8,128)(2,1)S(1)}, bf16[16,3200]{1,0:T(8,128)(2,1)S(1)}, u32[]{:S(2)}, u32[]{:S(2)}) %collective-permute-start.9) | collective-permute-done | bytes 102432 | tf_op jit(solution)/shard_map/ppermute | solution.py:553
  38.8 1.9 %shard_map.81 = (bf16[32,3200]{1,0:T(8,128)(2,1)S(1)}, bf16[32,3200]{1,0:T(8,128)(2,1)S(1)}, bf16[32,3200]{1,0:T(8,128)(2,1)S(1)}, bf16[32,3200]{1,0:T(8,128)(2,...) custom-call(bf16[16,3200]{1,0:T(8,128)(2,1)S(1)} %get-tuple-element.74.refs_0_, ...), custom_call_target="tpu_custom_call" | custom-call | flops 2529999872 | tf_op jit(solution)/shard_map/pallas_call | solution.py:527
  40.7 1.2 %collective-permute-start.15 = (bf16[32,3200]{1,0:T(8,128)(2,1)S(1)}, bf16[32,3200]{1,0:T(8,128)(2,1)S(1)}, u32[]{:S(2)}, u32[]{:S(2)}) collective-permute-start(bf16[32,3200]{1,0:T(8,128)(2,1)S(1)} %get-tuple-element.83), channel_id=1, source_target_pairs={{0,2},{1,3},{2,0},{3,1},{4,6},{5,7},{6,4},{7,5},{8,10},{9,11},{10,... | collective-permute-start | bytes 614408 | tf_op jit(solution)/shard_map/ppermute | solution.py:553
  42.0 1.6 %collective-permute-start.16 = (bf16[32,3200]{1,0:T(8,128)(2,1)S(1)}, bf16[32,3200]{1,0:T(8,128)(2,1)S(1)}, u32[]{:S(2)}, u32[]{:S(2)}) collective-permute-start(bf16[32,3200]{1,0:T(8,128)(2,1)S(1)} %get-tuple-element.85), channel_id=1, source_target_pairs={{0,4},{1,5},{2,6},{3,7},{4,0},{5,1},{6,2},{7,3},{8,12},{9,13},{10,... | collective-permute-start | bytes 614408 | tf_op jit(solution)/shard_map/ppermute | solution.py:553
  44.5 3.6 %collective-permute-done.15.value_ref = bf16[32,3200]{1,0:T(8,128)(2,1)S(1)} collective-permute-done((bf16[32,3200]{1,0:T(8,128)(2,1)S(1)}, bf16[32,3200]{1,0:T(8,128)(2,1)S(1)}, u32[]{:S(2)}, u32[]{:S(2)}) %collective-permute-start.15) | collective-permute-done | bytes 204832 | tf_op jit(solution)/shard_map/ppermute | solution.py:553
  48.3 1.6 %collective-permute-done.16.value_ref = bf16[32,3200]{1,0:T(8,128)(2,1)S(1)} collective-permute-done((bf16[32,3200]{1,0:T(8,128)(2,1)S(1)}, bf16[32,3200]{1,0:T(8,128)(2,1)S(1)}, u32[]{:S(2)}, u32[]{:S(2)}) %collective-permute-start.16) | collective-permute-done | bytes 204832 | tf_op jit(solution)/shard_map/ppermute | solution.py:553
  50.1 3.6 %collective-permute-done.17.value_ref = bf16[32,3200]{1,0:T(8,128)(2,1)S(1)} collective-permute-done((bf16[32,3200]{1,0:T(8,128)(2,1)S(1)}, bf16[32,3200]{1,0:T(8,128)(2,1)S(1)}, u32[]{:S(2)}, u32[]{:S(2)}) %collective-permute-start.17) | collective-permute-done | bytes 204832 | tf_op jit(solution)/shard_map/ppermute | solution.py:553
  54.9 2.7 %collective-permute-start.22 = (bf16[16,3200]{1,0:T(8,128)(2,1)S(1)}, bf16[16,3200]{1,0:T(8,128)(2,1)S(1)}, u32[]{:S(2)}, u32[]{:S(2)}) collective-permute-start(bf16[16,3200]{1,0:T(8,128)(2,1)S(1)} %get-tuple-element.98), channel_id=1, source_target_pairs={{0,8},{1,9},{2,10},{3,11},{4,12},{5,13},{6,14},{7,15},{8,0},{9,1},... | collective-permute-start | bytes 307208 | tf_op jit(solution)/shard_map/ppermute | solution.py:553
  57.6 1.3 %collective-permute-start.24 = (bf16[16,3200]{1,0:T(8,128)(2,1)S(1)}, bf16[16,3200]{1,0:T(8,128)(2,1)S(1)}, u32[]{:S(2)}, u32[]{:S(2)}) collective-permute-start(bf16[16,3200]{1,0:T(8,128)(2,1)S(1)} %get-tuple-element.100), channel_id=1, source_target_pairs={{0,12},{1,13},{2,14},{3,15},{4,8},{5,9},{6,10},{7,11},{8,4},{9,5},... | collective-permute-start | bytes 307208 | tf_op jit(solution)/shard_map/ppermute | solution.py:553
  58.9 2.6 %shard_map.86 = (bf16[16,3200]{1,0:T(8,128)(2,1)S(1)}, bf16[16,3200]{1,0:T(8,128)(2,1)S(1)}, bf16[16,3200]{1,0:T(8,128)(2,1)S(1)}, bf16[16,3200]{1,0:T(8,128)(2,...) custom-call(f32[640,128]{1,0:T(8,128)S(1)} %get-tuple-element.82.earlier_ref.refs_0_, ...), custom_call_target="tpu_custom_call" | custom-call | flops 2750000128 | tf_op jit(solution)/shard_map/pallas_call | solution.py:527
  61.8 2.2 %collective-permute-start.19 = (bf16[16,3200]{1,0:T(8,128)(2,1)S(1)}, bf16[16,3200]{1,0:T(8,128)(2,1)S(1)}, u32[]{:S(2)}, u32[]{:S(2)}) collective-permute-start(bf16[16,3200]{1,0:T(8,128)(2,1)S(1)} %get-tuple-element.95), channel_id=1, source_target_pairs={{0,4},{1,5},{2,6},{3,7},{4,0},{5,1},{6,2},{7,3},{8,12},{9,13},{10,... | collective-permute-start | bytes 307208 | tf_op jit(solution)/shard_map/ppermute | solution.py:553
  64.0 1.0 %collective-permute-start.20 = (bf16[16,3200]{1,0:T(8,128)(2,1)S(1)}, bf16[16,3200]{1,0:T(8,128)(2,1)S(1)}, u32[]{:S(2)}, u32[]{:S(2)}) collective-permute-start(bf16[16,3200]{1,0:T(8,128)(2,1)S(1)} %get-tuple-element.96), channel_id=1, source_target_pairs={{0,2},{1,3},{2,0},{3,1},{4,6},{5,7},{6,4},{7,5},{8,10},{9,11},{10,... | collective-permute-start | bytes 307208 | tf_op jit(solution)/shard_map/ppermute | solution.py:553
  65.2 1.8 %collective-permute-start.21 = (bf16[16,3200]{1,0:T(8,128)(2,1)S(1)}, bf16[16,3200]{1,0:T(8,128)(2,1)S(1)}, u32[]{:S(2)}, u32[]{:S(2)}) collective-permute-start(bf16[16,3200]{1,0:T(8,128)(2,1)S(1)} %get-tuple-element.97), channel_id=1, source_target_pairs={{0,10},{1,11},{2,8},{3,9},{4,14},{5,15},{6,12},{7,13},{8,2},{9,3},... | collective-permute-start | bytes 307208 | tf_op jit(solution)/shard_map/ppermute | solution.py:553
  67.0 1.6 %collective-permute-start.23 = (bf16[16,3200]{1,0:T(8,128)(2,1)S(1)}, bf16[16,3200]{1,0:T(8,128)(2,1)S(1)}, u32[]{:S(2)}, u32[]{:S(2)}) collective-permute-start(bf16[16,3200]{1,0:T(8,128)(2,1)S(1)} %get-tuple-element.99), channel_id=1, source_target_pairs={{0,14},{1,15},{2,12},{3,13},{4,10},{5,11},{6,8},{7,9},{8,6},{9,7},... | collective-permute-start | bytes 307208 | tf_op jit(solution)/shard_map/ppermute | solution.py:553
  69.3 1.8 %collective-permute-done.19.refs_2_ = bf16[16,3200]{1,0:T(8,128)(2,1)S(1)} collective-permute-done((bf16[16,3200]{1,0:T(8,128)(2,1)S(1)}, bf16[16,3200]{1,0:T(8,128)(2,1)S(1)}, u32[]{:S(2)}, u32[]{:S(2)}) %collective-permute-start.19) | collective-permute-done | bytes 102432 | tf_op jit(solution)/shard_map/ppermute | solution.py:553
  71.1 4.2 %collective-permute-done.21.refs_4_ = bf16[16,3200]{1,0:T(8,128)(2,1)S(1)} collective-permute-done((bf16[16,3200]{1,0:T(8,128)(2,1)S(1)}, bf16[16,3200]{1,0:T(8,128)(2,1)S(1)}, u32[]{:S(2)}, u32[]{:S(2)}) %collective-permute-start.21) | collective-permute-done | bytes 102432 | tf_op jit(solution)/shard_map/ppermute | solution.py:553
  75.6 1.2 %shard_map.89 = (f32[1600,128]{1,0:T(8,128)S(1)}, f32[1600,128]{1,0:T(8,128)S(1)}) custom-call(bf16[128,3200]{1,0:T(8,128)(2,1)S(1)} %get-tuple-element.103.after_ref, bf16[128,3200]{1,0:T(8,128)(2,1)S(1)} %get-tuple-element.104.normed_ref, bf16[2,128,128]{2,1,0:T(8,128)(2,1)S(1)} %get-tuple-element.66.refs_5_.gate_ref), custom_call_target="tpu_custom_call" | custom-call | flops 2200000000 | tf_op jit(solution)/shard_map/pallas_call | solution.py:527
  77.0 1.3 %shard_map.90 = bf16[1600,128]{1,0:T(8,128)(2,1)} custom-call(bf16[64,1600]{1,0:T(8,128)(2,1)S(1)} %get-tuple-element.101.keep_ref, bf16[64,1600]{1,0:T(8,128)(2,1)S(1)} %collective-permute-done.25.got_ref, f32[1600,128]{1,0:T(8,128)S(1)} %get-tuple-element.105.own_ref, f32[1600,128]{1,0:T(8,128)S(1)} %get-tuple-element.106.gating_ref, ...), custom_call_target="tpu_custom_call" | custom-call | flops 1100000000 | tf_op jit(solution)/shard_map/pallas_call | solution.py:527
  (38 shorter events, 8.6 us)
Async XLA Ops:
  0.0 2.0 %collective-permute-start = (bf16[40,40,128]{2,1,0:T(8,128)(2,1)}, bf16[40,40,128]{2,1,0:T(8,128)(2,1)S(1)}, u32[]{:S(2)}, u32[]{:S(2)}) collective-permute-start(bf16[40,40,128]{2,1,0:T(8,128)(2,1)} %pair_in.1), channel_id=1, source_target_pairs={{0,1},{1,0},{2,3},{3,2},{4,5},{5,4},{6,7},{7,6},{8,9},{9,8},{10,11... | collective-permute-start | bytes 1228808 | tf_op jit(solution)/shard_map/ppermute | solution.py:553
  3.4 8.8 %collective-permute-start.2 = (bf16[32,3200]{1,0:T(8,128)(2,1)S(1)}, bf16[32,3200]{1,0:T(8,128)(2,1)S(1)}, u32[]{:S(2)}, u32[]{:S(2)}) collective-permute-start(bf16[32,3200]{1,0:T(8,128)(2,1)S(1)} %get-tuple-element.62), channel_id=1, source_target_pairs={{0,2},{1,3},{2,0},{3,1},{4,6},{5,7},{6,4},{7,5},{8,10},{9,11},{10,... | collective-permute-start | bytes 614408 | tf_op jit(solution)/shard_map/ppermute | solution.py:553
  6.4 12.4 %collective-permute-start.3 = (bf16[32,3200]{1,0:T(8,128)(2,1)S(1)}, bf16[32,3200]{1,0:T(8,128)(2,1)S(1)}, u32[]{:S(2)}, u32[]{:S(2)}) collective-permute-start(bf16[32,3200]{1,0:T(8,128)(2,1)S(1)} %get-tuple-element.63), channel_id=1, source_target_pairs={{0,4},{1,5},{2,6},{3,7},{4,0},{5,1},{6,2},{7,3},{8,12},{9,13},{10,... | collective-permute-start | bytes 614408 | tf_op jit(solution)/shard_map/ppermute | solution.py:553
  7.9 13.8 %collective-permute-start.4 = (bf16[32,3200]{1,0:T(8,128)(2,1)S(1)}, bf16[32,3200]{1,0:T(8,128)(2,1)S(1)}, u32[]{:S(2)}, u32[]{:S(2)}) collective-permute-start(bf16[32,3200]{1,0:T(8,128)(2,1)S(1)} %get-tuple-element.64), channel_id=1, source_target_pairs={{0,6},{1,7},{2,4},{3,5},{4,2},{5,3},{6,0},{7,1},{8,14},{9,15},{10,... | collective-permute-start | bytes 614408 | tf_op jit(solution)/shard_map/ppermute | solution.py:553
  7.9 15.5 %collective-permute-start.1 = (bf16[16,3200]{1,0:T(8,128)(2,1)S(1)}, bf16[16,3200]{1,0:T(8,128)(2,1)S(1)}, u32[]{:S(2)}, u32[]{:S(2)}) collective-permute-start(bf16[16,3200]{1,0:T(8,128)(2,1)S(1)} %get-tuple-element.60), channel_id=1, source_target_pairs={{0,8},{1,9},{2,10},{3,11},{4,12},{5,13},{6,14},{7,15},{8,0},{9,1},... | collective-permute-start | bytes 307208 | tf_op jit(solution)/shard_map/ppermute | solution.py:553
  10.9 12.7 %collective-permute-start.5 = (bf16[16,3200]{1,0:T(8,128)(2,1)S(1)}, bf16[16,3200]{1,0:T(8,128)(2,1)S(1)}, u32[]{:S(2)}, u32[]{:S(2)}) collective-permute-start(bf16[16,3200]{1,0:T(8,128)(2,1)S(1)} %get-tuple-element.68), channel_id=1, source_target_pairs={{0,10},{1,11},{2,8},{3,9},{4,14},{5,15},{6,12},{7,13},{8,2},{9,3},... | collective-permute-start | bytes 307208 | tf_op jit(solution)/shard_map/ppermute | solution.py:553
  12.2 15.2 %collective-permute-start.6 = (bf16[16,3200]{1,0:T(8,128)(2,1)S(1)}, bf16[16,3200]{1,0:T(8,128)(2,1)S(1)}, u32[]{:S(2)}, u32[]{:S(2)}) collective-permute-start(bf16[16,3200]{1,0:T(8,128)(2,1)S(1)} %get-tuple-element.69), channel_id=1, source_target_pairs={{0,12},{1,13},{2,14},{3,15},{4,8},{5,9},{6,10},{7,11},{8,4},{9,5},... | collective-permute-start | bytes 307208 | tf_op jit(solution)/shard_map/ppermute | solution.py:553
  18.7 9.7 %collective-permute-start.7 = (bf16[16,3200]{1,0:T(8,128)(2,1)S(1)}, bf16[16,3200]{1,0:T(8,128)(2,1)S(1)}, u32[]{:S(2)}, u32[]{:S(2)}) collective-permute-start(bf16[16,3200]{1,0:T(8,128)(2,1)S(1)} %get-tuple-element.70), channel_id=1, source_target_pairs={{0,14},{1,15},{2,12},{3,13},{4,10},{5,11},{6,8},{7,9},{8,6},{9,7},... | collective-permute-start | bytes 307208 | tf_op jit(solution)/shard_map/ppermute | solution.py:553
  29.7 6.2 %collective-permute-start.8 = (bf16[16,3200]{1,0:T(8,128)(2,1)S(1)}, bf16[16,3200]{1,0:T(8,128)(2,1)S(1)}, u32[]{:S(2)}, u32[]{:S(2)}) collective-permute-start(bf16[16,3200]{1,0:T(8,128)(2,1)S(1)} %get-tuple-element.75), channel_id=1, source_target_pairs={{0,6},{1,7},{2,4},{3,5},{4,2},{5,3},{6,0},{7,1},{8,14},{9,15},{10,... | collective-permute-start | bytes 307208 | tf_op jit(solution)/shard_map/ppermute | solution.py:553
  32.6 4.8 %collective-permute-start.9 = (bf16[16,3200]{1,0:T(8,128)(2,1)S(1)}, bf16[16,3200]{1,0:T(8,128)(2,1)S(1)}, u32[]{:S(2)}, u32[]{:S(2)}) collective-permute-start(bf16[16,3200]{1,0:T(8,128)(2,1)S(1)} %get-tuple-element.76), channel_id=1, source_target_pairs={{0,4},{1,5},{2,6},{3,7},{4,0},{5,1},{6,2},{7,3},{8,12},{9,13},{10,... | collective-permute-start | bytes 307208 | tf_op jit(solution)/shard_map/ppermute | solution.py:553
  32.7 4.7 %collective-permute-start.10 = (bf16[16,3200]{1,0:T(8,128)(2,1)S(1)}, bf16[16,3200]{1,0:T(8,128)(2,1)S(1)}, u32[]{:S(2)}, u32[]{:S(2)}) collective-permute-start(bf16[16,3200]{1,0:T(8,128)(2,1)S(1)} %get-tuple-element.77), channel_id=1, source_target_pairs={{0,2},{1,3},{2,0},{3,1},{4,6},{5,7},{6,4},{7,5},{8,10},{9,11},{10,... | collective-permute-start | bytes 307208 | tf_op jit(solution)/shard_map/ppermute | solution.py:553
  33.6 4.2 %collective-permute-start.11 = (bf16[16,3200]{1,0:T(8,128)(2,1)S(1)}, bf16[16,3200]{1,0:T(8,128)(2,1)S(1)}, u32[]{:S(2)}, u32[]{:S(2)}) collective-permute-start(bf16[16,3200]{1,0:T(8,128)(2,1)S(1)} %get-tuple-element.74.refs_0_), channel_id=1, source_target_pairs={{0,1},{1,0},{2,3},{3,2},{4,5},{5,4},{6,7},{7,6},{8,9},{9,8},{10,11... | collective-permute-start | bytes 307208 | tf_op jit(solution)/shard_map/ppermute | solution.py:553
  35.9 1.9 %collective-permute-start.12 = (bf16[16,3200]{1,0:T(8,128)(2,1)S(1)}, bf16[16,3200]{1,0:T(8,128)(2,1)S(1)}, u32[]{:S(2)}, u32[]{:S(2)}) collective-permute-start(bf16[16,3200]{1,0:T(8,128)(2,1)S(1)} %collective-permute-done.8.refs_1_), channel_id=1, source_target_pairs={{0,1},{1,0},{2,3},{3,2},{4,5},{5,4},{6,7},{7,6},{8,9},{9,8},{10,11... | collective-permute-start | bytes 307208 | tf_op jit(solution)/shard_map/ppermute | solution.py:553
  37.3 1.3 %collective-permute-start.13 = (bf16[16,3200]{1,0:T(8,128)(2,1)S(1)}, bf16[16,3200]{1,0:T(8,128)(2,1)S(1)}, u32[]{:S(2)}, u32[]{:S(2)}) collective-permute-start(bf16[16,3200]{1,0:T(8,128)(2,1)S(1)} %collective-permute-done.9.refs_2_), channel_id=1, source_target_pairs={{0,1},{1,0},{2,3},{3,2},{4,5},{5,4},{6,7},{7,6},{8,9},{9,8},{10,11... | collective-permute-start | bytes 307208 | tf_op jit(solution)/shard_map/ppermute | solution.py:553
  37.4 1.4 %collective-permute-start.14 = (bf16[16,3200]{1,0:T(8,128)(2,1)S(1)}, bf16[16,3200]{1,0:T(8,128)(2,1)S(1)}, u32[]{:S(2)}, u32[]{:S(2)}) collective-permute-start(bf16[16,3200]{1,0:T(8,128)(2,1)S(1)} %collective-permute-done.10.refs_3_), channel_id=1, source_target_pairs={{0,1},{1,0},{2,3},{3,2},{4,5},{5,4},{6,7},{7,6},{8,9},{9,8},{10,11... | collective-permute-start | bytes 307208 | tf_op jit(solution)/shard_map/ppermute | solution.py:553
  40.7 7.4 %collective-permute-start.15 = (bf16[32,3200]{1,0:T(8,128)(2,1)S(1)}, bf16[32,3200]{1,0:T(8,128)(2,1)S(1)}, u32[]{:S(2)}, u32[]{:S(2)}) collective-permute-start(bf16[32,3200]{1,0:T(8,128)(2,1)S(1)} %get-tuple-element.83), channel_id=1, source_target_pairs={{0,2},{1,3},{2,0},{3,1},{4,6},{5,7},{6,4},{7,5},{8,10},{9,11},{10,... | collective-permute-start | bytes 614408 | tf_op jit(solution)/shard_map/ppermute | solution.py:553
  42.0 8.0 %collective-permute-start.16 = (bf16[32,3200]{1,0:T(8,128)(2,1)S(1)}, bf16[32,3200]{1,0:T(8,128)(2,1)S(1)}, u32[]{:S(2)}, u32[]{:S(2)}) collective-permute-start(bf16[32,3200]{1,0:T(8,128)(2,1)S(1)} %get-tuple-element.85), channel_id=1, source_target_pairs={{0,4},{1,5},{2,6},{3,7},{4,0},{5,1},{6,2},{7,3},{8,12},{9,13},{10,... | collective-permute-start | bytes 614408 | tf_op jit(solution)/shard_map/ppermute | solution.py:553
  43.6 10.1 %collective-permute-start.17 = (bf16[32,3200]{1,0:T(8,128)(2,1)S(1)}, bf16[32,3200]{1,0:T(8,128)(2,1)S(1)}, u32[]{:S(2)}, u32[]{:S(2)}) collective-permute-start(bf16[32,3200]{1,0:T(8,128)(2,1)S(1)} %get-tuple-element.87), channel_id=1, source_target_pairs={{0,6},{1,7},{2,4},{3,5},{4,2},{5,3},{6,0},{7,1},{8,14},{9,15},{10,... | collective-permute-start | bytes 614408 | tf_op jit(solution)/shard_map/ppermute | solution.py:553
  54.9 10.3 %collective-permute-start.22 = (bf16[16,3200]{1,0:T(8,128)(2,1)S(1)}, bf16[16,3200]{1,0:T(8,128)(2,1)S(1)}, u32[]{:S(2)}, u32[]{:S(2)}) collective-permute-start(bf16[16,3200]{1,0:T(8,128)(2,1)S(1)} %get-tuple-element.98), channel_id=1, source_target_pairs={{0,8},{1,9},{2,10},{3,11},{4,12},{5,13},{6,14},{7,15},{8,0},{9,1},... | collective-permute-start | bytes 307208 | tf_op jit(solution)/shard_map/ppermute | solution.py:553
  57.6 9.4 %collective-permute-start.24 = (bf16[16,3200]{1,0:T(8,128)(2,1)S(1)}, bf16[16,3200]{1,0:T(8,128)(2,1)S(1)}, u32[]{:S(2)}, u32[]{:S(2)}) collective-permute-start(bf16[16,3200]{1,0:T(8,128)(2,1)S(1)} %get-tuple-element.100), channel_id=1, source_target_pairs={{0,12},{1,13},{2,14},{3,15},{4,8},{5,9},{6,10},{7,11},{8,4},{9,5},... | collective-permute-start | bytes 307208 | tf_op jit(solution)/shard_map/ppermute | solution.py:553
  61.5 7.9 %collective-permute-start.18 = (bf16[16,3200]{1,0:T(8,128)(2,1)S(1)}, bf16[16,3200]{1,0:T(8,128)(2,1)S(1)}, u32[]{:S(2)}, u32[]{:S(2)}) collective-permute-start(bf16[16,3200]{1,0:T(8,128)(2,1)S(1)} %get-tuple-element.94), channel_id=1, source_target_pairs={{0,6},{1,7},{2,4},{3,5},{4,2},{5,3},{6,0},{7,1},{8,14},{9,15},{10,... | collective-permute-start | bytes 307208 | tf_op jit(solution)/shard_map/ppermute | solution.py:553
  61.8 9.3 %collective-permute-start.19 = (bf16[16,3200]{1,0:T(8,128)(2,1)S(1)}, bf16[16,3200]{1,0:T(8,128)(2,1)S(1)}, u32[]{:S(2)}, u32[]{:S(2)}) collective-permute-start(bf16[16,3200]{1,0:T(8,128)(2,1)S(1)} %get-tuple-element.95), channel_id=1, source_target_pairs={{0,4},{1,5},{2,6},{3,7},{4,0},{5,1},{6,2},{7,3},{8,12},{9,13},{10,... | collective-permute-start | bytes 307208 | tf_op jit(solution)/shard_map/ppermute | solution.py:553
  64.0 7.1 %collective-permute-start.20 = (bf16[16,3200]{1,0:T(8,128)(2,1)S(1)}, bf16[16,3200]{1,0:T(8,128)(2,1)S(1)}, u32[]{:S(2)}, u32[]{:S(2)}) collective-permute-start(bf16[16,3200]{1,0:T(8,128)(2,1)S(1)} %get-tuple-element.96), channel_id=1, source_target_pairs={{0,2},{1,3},{2,0},{3,1},{4,6},{5,7},{6,4},{7,5},{8,10},{9,11},{10,... | collective-permute-start | bytes 307208 | tf_op jit(solution)/shard_map/ppermute | solution.py:553
  65.2 10.1 %collective-permute-start.21 = (bf16[16,3200]{1,0:T(8,128)(2,1)S(1)}, bf16[16,3200]{1,0:T(8,128)(2,1)S(1)}, u32[]{:S(2)}, u32[]{:S(2)}) collective-permute-start(bf16[16,3200]{1,0:T(8,128)(2,1)S(1)} %get-tuple-element.97), channel_id=1, source_target_pairs={{0,10},{1,11},{2,8},{3,9},{4,14},{5,15},{6,12},{7,13},{8,2},{9,3},... | collective-permute-start | bytes 307208 | tf_op jit(solution)/shard_map/ppermute | solution.py:553
  67.0 8.3 %collective-permute-start.23 = (bf16[16,3200]{1,0:T(8,128)(2,1)S(1)}, bf16[16,3200]{1,0:T(8,128)(2,1)S(1)}, u32[]{:S(2)}, u32[]{:S(2)}) collective-permute-start(bf16[16,3200]{1,0:T(8,128)(2,1)S(1)} %get-tuple-element.99), channel_id=1, source_target_pairs={{0,14},{1,15},{2,12},{3,13},{4,10},{5,11},{6,8},{7,9},{8,6},{9,7},... | collective-permute-start | bytes 307208 | tf_op jit(solution)/shard_map/ppermute | solution.py:553
  75.5 1.5 %collective-permute-start.25 = (bf16[64,1600]{1,0:T(8,128)(2,1)S(1)}, bf16[64,1600]{1,0:T(8,128)(2,1)S(1)}, u32[]{:S(2)}, u32[]{:S(2)}) collective-permute-start(bf16[64,1600]{1,0:T(8,128)(2,1)S(1)} %get-tuple-element.102), channel_id=1, source_target_pairs={{0,1},{1,0},{2,3},{3,2},{4,5},{5,4},{6,7},{7,6},{8,9},{9,8},{10,11... | collective-permute-start | bytes 614408 | tf_op jit(solution)/shard_map/ppermute | solution.py:553
